TPU v7x, 128 devices: a whole 4x4x4 slice. The times are simulated.
128 devices in a mesh: ulysses: 4 (over z), blk: 8 (over y, core), tensor: 4 (over x).
Axes of the slice: x: 4, y: 4, z: 4, core: 2. Of those that a mesh axis runs over, the one named last changes fastest.
Arguments:
- tokens: bfloat16 [8192, 5120], P(('ulysses', 'blk'), 'tensor'), may hold values from -20 to 20
- w_qkv: bfloat16 [5120, 3, 4096], P(None, None, ('ulysses', 'tensor')), may hold values from -2 to 2
- qkv_scale: float32 [3, 32], P(None, ('ulysses', 'tensor')), may hold values from 0.6 to 9
- block_mask: int32 [32, 64, 64], P(('ulysses', 'tensor')), may hold values from 0 to 1, as said below
- w_out: bfloat16 [4, 1024, 5120], P(None, 'tensor'), may hold values from -0.125 to 0.125
Outputs:
- mixed: bfloat16 [8192, 5120], P(('ulysses', 'blk'), 'tensor')
Inputs may be any that keep to these rules, and one draw needn't show every extreme that they name: `block_mask`: 0 or 1; the share of ones differs from head to head.
All inputs are finite; a program needn't handle non-finite values.
Results may differ from a plain program's by a relative error of at most 0.015.
Values may be sent and summed in bfloat16 or wider, within the bound.
No kernel may reach another device: no remote copies, remote signals or barrier semaphores. Data moves between devices by JAX's collectives and lax.ppermute only.
A program may use at most 128 MiB of HBM per device.

v0:
```python
import math

import jax
import jax.numpy as jnp
from jax import lax
from jax.sharding import PartitionSpec as P


def local(tokens, w_qkv, qkv_scale, block_mask, w_out):
    group_count = lax.axis_size("ulysses")
    tensor_count = lax.axis_size("tensor")
    cycle_count = lax.axis_size("blk")
    tok_rows, feat_cols = tokens.shape
    width_all, triple, head_cols = w_qkv.shape
    heads_here = qkv_scale.shape[1]
    head_dim = head_cols // heads_here
    blocks_all = block_mask.shape[1]
    group_rows = tok_rows * group_count
    block_rows = cycle_count * group_rows // blocks_all
    start_sum = jnp.zeros((group_count, tok_rows, triple, head_cols), jnp.float32)
    pieces = lax.all_gather(tokens[None], ("ulysses", "tensor"), axis=0, tiled=True)

    def one_shard(which, accum):
        group_id = which // tensor_count
        feature_id = which % tensor_count
        weights = lax.dynamic_slice_in_dim(w_qkv, feature_id * feat_cols, feat_cols, 0)
        token_part = lax.dynamic_index_in_dim(pieces, which, 0, keepdims=False)
        product = jnp.einsum("rd,dcn->rcn", token_part, weights, preferred_element_type=jnp.float32)
        current = lax.dynamic_index_in_dim(accum, group_id, 0, keepdims=False)
        return lax.dynamic_update_index_in_dim(accum, current + product, group_id, 0)

    projected = lax.fori_loop(0, pieces.shape[0], one_shard, start_sum)
    projected = (
        projected.reshape(group_rows, triple, heads_here, head_dim) * qkv_scale[None, :, :, None]
    )
    projected = projected.astype(jnp.bfloat16)
    queries = projected[:, 0]
    keys = projected[:, 1]
    values = projected[:, 2]
    cycle_index = lax.axis_index("blk")
    local_rows = jnp.arange(group_rows, dtype=jnp.int32)
    query_pos = (
        local_rows // tok_rows * cycle_count + cycle_index
    ) * tok_rows + local_rows % tok_rows
    query_block = query_pos // block_rows
    block_ids = jnp.arange(blocks_all, dtype=jnp.int32)
    query_onehot = (query_block[:, None] == block_ids[None, :]).astype(jnp.bfloat16)
    query_live = jnp.einsum(
        "qn,hnm->hqm",
        query_onehot,
        block_mask.astype(jnp.bfloat16),
        preferred_element_type=jnp.float32,
    ).astype(jnp.bfloat16)
    score_scale = 1.0 / math.sqrt(head_dim)
    start_state = (
        jnp.full((heads_here, group_rows), -1e30, jnp.float32),
        jnp.zeros((heads_here, group_rows), jnp.float32),
        jnp.zeros((heads_here, group_rows, head_dim), jnp.float32),
    )
    key_all = lax.all_gather(keys, "blk", axis=0, tiled=True)
    value_all = lax.all_gather(values, "blk", axis=0, tiled=True)

    def one_block(which, state):
        highest, denominator, numerator = state
        key_part = lax.dynamic_slice_in_dim(key_all, which * group_rows, group_rows, 0)
        value_part = lax.dynamic_slice_in_dim(value_all, which * group_rows, group_rows, 0)
        gathered_row = which * group_rows + local_rows
        owner_cycle = gathered_row // group_rows
        inner_row = gathered_row % group_rows
        key_pos = (
            inner_row // tok_rows * cycle_count + owner_cycle
        ) * tok_rows + inner_row % tok_rows
        key_block = key_pos // block_rows
        key_onehot = (key_block[:, None] == block_ids[None, :]).astype(jnp.bfloat16)
        allowed = (
            jnp.einsum("hqn,kn->hqk", query_live, key_onehot, preferred_element_type=jnp.float32)
            > 0.5
        )
        allowed = allowed | (query_block[:, None] == key_block[None, :])[None]
        scores = (
            jnp.einsum("qhd,khd->hqk", queries, key_part, preferred_element_type=jnp.float32)
            * score_scale
        )
        scores = jnp.where(allowed, scores, -jnp.inf)
        new_high = jnp.maximum(highest, jnp.max(scores, axis=-1))
        weights = jnp.exp(scores - new_high[..., None])
        factor = jnp.exp(highest - new_high)
        denominator = denominator * factor + jnp.sum(weights, axis=-1)
        numerator = numerator * factor[..., None] + jnp.einsum(
            "hqk,khd->hqd",
            weights.astype(jnp.bfloat16),
            value_part,
            preferred_element_type=jnp.float32,
        )
        return (new_high, denominator, numerator)

    highest, denominator, numerator = lax.fori_loop(
        0, key_all.shape[0] // group_rows, one_block, start_state
    )
    attended = (numerator / denominator[..., None]).astype(jnp.bfloat16)
    grouped = attended.reshape(heads_here, group_count, tok_rows, head_dim)
    arrived = lax.all_to_all(grouped, "ulysses", split_axis=1, concat_axis=0, tiled=True)
    out_rows = w_out.reshape(group_count * heads_here, head_dim, w_out.shape[2])
    partial_value = jnp.einsum(
        "grd,gdf->rf", arrived[:, 0], out_rows, preferred_element_type=jnp.float32
    )
    summed = lax.psum_scatter(
        partial_value.astype(jnp.bfloat16), "tensor", scatter_dimension=1, tiled=True
    )
    return summed


def solution(mesh):
    return jax.shard_map(
        local,
        mesh=mesh,
        in_specs=(
            P(("ulysses", "blk"), "tensor"),
            P(None, None, ("ulysses", "tensor")),
            P(None, ("ulysses", "tensor")),
            P(("ulysses", "tensor"), None, None),
            P(None, "tensor", None),
        ),
        out_specs=P(("ulysses", "blk"), "tensor"),
        check_vma=False,
    )
```

profile of v0, /device:TPU:0, one launch (start us, length us, event | category | flops | bytes accessed | tf_op | source)
XLA Modules:
  0.0 420.0 jit_solution(13156679793859834342)
XLA Ops:
  8.1 84.5 %all-gather.7.cloned.1.call-done = bf16[4096,1280]{1,0:T(8,128)(2,1)} async-done(((bf16[256,1280]{1,0:T(8,128)(2,1)}), bf16[4096,1280]{1,0:T(8,128)(2,1)}) %all-gather.7.cloned.1.call-update) | async-done | bytes 10485776 | tf_op jit(solution)/shard_map/all_gather | solution.py:21
  92.8 57.4 %while.36 = (s32[]{:T(128)}, f32[4,256,3,256]{3,1,0,2:T(8,128)S(1)}, bf16[16,256,1280]{2,1,0:T(8,128)(2,1)}, bf16[5120,3,256]{2,0,1:T(8,128)(2,1)}, s32[]{:T(128...) while((s32[]{:T(128)}, ...), condition=%wide.region_1.2_spmd, body=%wide.region_0.1_spmd.sunk | while | flops 503513120 | bytes 5768004 | solution.py:32
  159.7 30.5 %all-gather.9.cloned.1.call-done = bf16[8192,1,2,128]{3,2,1,0:T(2,128)(2,1)} async-done(((bf16[1024,1,2,128]{3,2,1,0:T(2,128)(2,1)}), bf16[8192,1,2,128]{3,2,1,0:T(2,128)(2,1)}) %all-gather.9.cloned.1.call-update) | async-done | bytes 4194320 | tf_op jit(solution)/shard_map/all_gather | solution.py:60
  190.3 33.8 %all-gather.11.cloned.1.call-done = bf16[8192,1,2,128]{3,2,1,0:T(2,128)(2,1)} async-done(((bf16[1024,1,2,128]{3,2,1,0:T(2,128)(2,1)}), bf16[8192,1,2,128]{3,2,1,0:T(2,128)(2,1)}) %all-gather.11.cloned.1.call-update) | async-done | bytes 4194320 | tf_op jit(solution)/shard_map/all_gather | solution.py:61
  224.1 134.8 %while.37 = (s32[]{:T(128)}, f32[2,1024]{1,0:T(2,128)S(1)}, f32[2,1024]{1,0:T(2,128)S(1)}, f32[2,1024,128]{2,1,0:T(8,128)S(1)}, bf16[2,1024,64]{1,2,0:T(8,128)(2...) while((s32[]{:T(128)}, f32[2,1024]{1,0:T(2,128)S(1)}, ...), condition=%wide.region_5.6_spmd.clone, body=%wide.region_2.5_spmd.clone.sunk | while | flops 1363053568 | bytes 83775712 | solution.py:97
  228.0 4.8 %fusion.113 = (f32[2,1024]{1,0:T(2,128)S(1)}, f32[2,1024,1024]{1,2,0:T(8,128)}) fusion(bf16[1024,2,128]{2,0,1:T(8,128)(2,1)S(1)} %get-tuple-element.690, bf16[1024,2,128]{2,1,0:T(2,128)(2,1)S(1)} %get-tuple-element.614, pred[1024,1024]{0,1:T(8,128)(4,1)S(1)} %broadcast_compare_fusion.2, f32[1024,2,1024]{2,0,1:T(8,128)S(1)} %fusion.112), kind=kOutput, calls=%fused_computation.126.clone.1 | convolution fusion | flops 547354624 | bytes 18882560 | tf_op jit(solution)/shard_map/while/body/eval_jaxpr/qhd,khd->hqk/dot_general | solution.py:81
  232.8 4.7 %fusion.115 = f32[2,1024]{1,0:T(2,128)S(1)} fusion(f32[2,1024,1024]{1,2,0:T(8,128)} %get-tuple-element.618, f32[2,1024]{1,0:T(2,128)S(1)} %fusion.114), kind=kLoop, calls=%fused_computation.16.clone.1 | loop fusion | flops 4192256 | bytes 8404992 | tf_op jit(solution)/shard_map/while/body/eval_jaxpr/reduce_sum | solution.py:88
  244.8 4.8 %fusion.113 = (f32[2,1024]{1,0:T(2,128)S(1)}, f32[2,1024,1024]{1,2,0:T(8,128)}) fusion(bf16[1024,2,128]{2,0,1:T(8,128)(2,1)S(1)} %get-tuple-element.690, bf16[1024,2,128]{2,1,0:T(2,128)(2,1)S(1)} %get-tuple-element.614, pred[1024,1024]{0,1:T(8,128)(4,1)S(1)} %broadcast_compare_fusion.2, f32[1024,2,1024]{2,0,1:T(8,128)S(1)} %fusion.112), kind=kOutput, calls=%fused_computation.126.clone.1 | convolution fusion | flops 547354624 | bytes 18882560 | tf_op jit(solution)/shard_map/while/body/eval_jaxpr/qhd,khd->hqk/dot_general | solution.py:81
  249.6 4.7 %fusion.115 = f32[2,1024]{1,0:T(2,128)S(1)} fusion(f32[2,1024,1024]{1,2,0:T(8,128)} %get-tuple-element.618, f32[2,1024]{1,0:T(2,128)S(1)} %fusion.114), kind=kLoop, calls=%fused_computation.16.clone.1 | loop fusion | flops 4192256 | bytes 8404992 | tf_op jit(solution)/shard_map/while/body/eval_jaxpr/reduce_sum | solution.py:88
  261.7 4.8 %fusion.113 = (f32[2,1024]{1,0:T(2,128)S(1)}, f32[2,1024,1024]{1,2,0:T(8,128)}) fusion(bf16[1024,2,128]{2,0,1:T(8,128)(2,1)S(1)} %get-tuple-element.690, bf16[1024,2,128]{2,1,0:T(2,128)(2,1)S(1)} %get-tuple-element.614, pred[1024,1024]{0,1:T(8,128)(4,1)S(1)} %broadcast_compare_fusion.2, f32[1024,2,1024]{2,0,1:T(8,128)S(1)} %fusion.112), kind=kOutput, calls=%fused_computation.126.clone.1 | convolution fusion | flops 547354624 | bytes 18882560 | tf_op jit(solution)/shard_map/while/body/eval_jaxpr/qhd,khd->hqk/dot_general | solution.py:81
  266.5 4.7 %fusion.115 = f32[2,1024]{1,0:T(2,128)S(1)} fusion(f32[2,1024,1024]{1,2,0:T(8,128)} %get-tuple-element.618, f32[2,1024]{1,0:T(2,128)S(1)} %fusion.114), kind=kLoop, calls=%fused_computation.16.clone.1 | loop fusion | flops 4192256 | bytes 8404992 | tf_op jit(solution)/shard_map/while/body/eval_jaxpr/reduce_sum | solution.py:88
  278.6 4.8 %fusion.113 = (f32[2,1024]{1,0:T(2,128)S(1)}, f32[2,1024,1024]{1,2,0:T(8,128)}) fusion(bf16[1024,2,128]{2,0,1:T(8,128)(2,1)S(1)} %get-tuple-element.690, bf16[1024,2,128]{2,1,0:T(2,128)(2,1)S(1)} %get-tuple-element.614, pred[1024,1024]{0,1:T(8,128)(4,1)S(1)} %broadcast_compare_fusion.2, f32[1024,2,1024]{2,0,1:T(8,128)S(1)} %fusion.112), kind=kOutput, calls=%fused_computation.126.clone.1 | convolution fusion | flops 547354624 | bytes 18882560 | tf_op jit(solution)/shard_map/while/body/eval_jaxpr/qhd,khd->hqk/dot_general | solution.py:81
  283.3 4.7 %fusion.115 = f32[2,1024]{1,0:T(2,128)S(1)} fusion(f32[2,1024,1024]{1,2,0:T(8,128)} %get-tuple-element.618, f32[2,1024]{1,0:T(2,128)S(1)} %fusion.114), kind=kLoop, calls=%fused_computation.16.clone.1 | loop fusion | flops 4192256 | bytes 8404992 | tf_op jit(solution)/shard_map/while/body/eval_jaxpr/reduce_sum | solution.py:88
  295.4 4.8 %fusion.113 = (f32[2,1024]{1,0:T(2,128)S(1)}, f32[2,1024,1024]{1,2,0:T(8,128)}) fusion(bf16[1024,2,128]{2,0,1:T(8,128)(2,1)S(1)} %get-tuple-element.690, bf16[1024,2,128]{2,1,0:T(2,128)(2,1)S(1)} %get-tuple-element.614, pred[1024,1024]{0,1:T(8,128)(4,1)S(1)} %broadcast_compare_fusion.2, f32[1024,2,1024]{2,0,1:T(8,128)S(1)} %fusion.112), kind=kOutput, calls=%fused_computation.126.clone.1 | convolution fusion | flops 547354624 | bytes 18882560 | tf_op jit(solution)/shard_map/while/body/eval_jaxpr/qhd,khd->hqk/dot_general | solution.py:81
  300.2 4.7 %fusion.115 = f32[2,1024]{1,0:T(2,128)S(1)} fusion(f32[2,1024,1024]{1,2,0:T(8,128)} %get-tuple-element.618, f32[2,1024]{1,0:T(2,128)S(1)} %fusion.114), kind=kLoop, calls=%fused_computation.16.clone.1 | loop fusion | flops 4192256 | bytes 8404992 | tf_op jit(solution)/shard_map/while/body/eval_jaxpr/reduce_sum | solution.py:88
  312.3 4.8 %fusion.113 = (f32[2,1024]{1,0:T(2,128)S(1)}, f32[2,1024,1024]{1,2,0:T(8,128)}) fusion(bf16[1024,2,128]{2,0,1:T(8,128)(2,1)S(1)} %get-tuple-element.690, bf16[1024,2,128]{2,1,0:T(2,128)(2,1)S(1)} %get-tuple-element.614, pred[1024,1024]{0,1:T(8,128)(4,1)S(1)} %broadcast_compare_fusion.2, f32[1024,2,1024]{2,0,1:T(8,128)S(1)} %fusion.112), kind=kOutput, calls=%fused_computation.126.clone.1 | convolution fusion | flops 547354624 | bytes 18882560 | tf_op jit(solution)/shard_map/while/body/eval_jaxpr/qhd,khd->hqk/dot_general | solution.py:81
  317.1 4.7 %fusion.115 = f32[2,1024]{1,0:T(2,128)S(1)} fusion(f32[2,1024,1024]{1,2,0:T(8,128)} %get-tuple-element.618, f32[2,1024]{1,0:T(2,128)S(1)} %fusion.114), kind=kLoop, calls=%fused_computation.16.clone.1 | loop fusion | flops 4192256 | bytes 8404992 | tf_op jit(solution)/shard_map/while/body/eval_jaxpr/reduce_sum | solution.py:88
  329.1 4.8 %fusion.113 = (f32[2,1024]{1,0:T(2,128)S(1)}, f32[2,1024,1024]{1,2,0:T(8,128)}) fusion(bf16[1024,2,128]{2,0,1:T(8,128)(2,1)S(1)} %get-tuple-element.690, bf16[1024,2,128]{2,1,0:T(2,128)(2,1)S(1)} %get-tuple-element.614, pred[1024,1024]{0,1:T(8,128)(4,1)S(1)} %broadcast_compare_fusion.2, f32[1024,2,1024]{2,0,1:T(8,128)S(1)} %fusion.112), kind=kOutput, calls=%fused_computation.126.clone.1 | convolution fusion | flops 547354624 | bytes 18882560 | tf_op jit(solution)/shard_map/while/body/eval_jaxpr/qhd,khd->hqk/dot_general | solution.py:81
  333.9 4.7 %fusion.115 = f32[2,1024]{1,0:T(2,128)S(1)} fusion(f32[2,1024,1024]{1,2,0:T(8,128)} %get-tuple-element.618, f32[2,1024]{1,0:T(2,128)S(1)} %fusion.114), kind=kLoop, calls=%fused_computation.16.clone.1 | loop fusion | flops 4192256 | bytes 8404992 | tf_op jit(solution)/shard_map/while/body/eval_jaxpr/reduce_sum | solution.py:88
  346.0 4.8 %fusion.113 = (f32[2,1024]{1,0:T(2,128)S(1)}, f32[2,1024,1024]{1,2,0:T(8,128)}) fusion(bf16[1024,2,128]{2,0,1:T(8,128)(2,1)S(1)} %get-tuple-element.690, bf16[1024,2,128]{2,1,0:T(2,128)(2,1)S(1)} %get-tuple-element.614, pred[1024,1024]{0,1:T(8,128)(4,1)S(1)} %broadcast_compare_fusion.2, f32[1024,2,1024]{2,0,1:T(8,128)S(1)} %fusion.112), kind=kOutput, calls=%fused_computation.126.clone.1 | convolution fusion | flops 547354624 | bytes 18882560 | tf_op jit(solution)/shard_map/while/body/eval_jaxpr/qhd,khd->hqk/dot_general | solution.py:81
  350.8 4.7 %fusion.115 = f32[2,1024]{1,0:T(2,128)S(1)} fusion(f32[2,1024,1024]{1,2,0:T(8,128)} %get-tuple-element.618, f32[2,1024]{1,0:T(2,128)S(1)} %fusion.114), kind=kLoop, calls=%fused_computation.16.clone.1 | loop fusion | flops 4192256 | bytes 8404992 | tf_op jit(solution)/shard_map/while/body/eval_jaxpr/reduce_sum | solution.py:88
  359.3 14.0 %all_to_all.15 = bf16[2,4,256,128]{3,2,0,1:T(8,128)(2,1)S(1)} all-to-all(bf16[2,4,256,128]{3,2,0,1:T(8,128)(2,1)S(1)} %copy.27), channel_id=1, replica_groups=mesh['ulysses'=4,'blk'=8,'tensor'=4] {'ulysses'}, dimensions={1} | all-to-all | bytes 1048576 | tf_op jit(solution)/shard_map/all_to_all | solution.py:102
  373.3 8.1 %fusion.68 = bf16[256,5120]{1,0:T(8,128)(2,1)} fusion(bf16[8,256,128]{2,1,0:T(8,128)(2,1)S(1)} %bitcast.74, bf16[8,128,5120]{2,1,0:T(8,128)(2,1)} %bitcast.76), kind=kOutput, calls=%fused_computation.94 | convolution fusion | flops 2685665280 | bytes 13631488 | tf_op jit(solution)/shard_map/grd,gdf->rf/dot_general | solution.py:104
  381.5 32.0 %reduce-scatter.2.cloned.1.call-done = bf16[256,1280]{1,0:T(8,128)(2,1)} async-done(((bf16[256,5120]{1,0:T(8,128)(2,1)}), bf16[256,1280]{1,0:T(8,128)(2,1)}) %reduce-scatter.2.cloned.1.call-update) | async-done | bytes 655376 | tf_op jit(solution)/shard_map/reduce_scatter | solution.py:107
  (138 shorter events, 126.9 us)
Async XLA Ops:
  6.5 86.0 %all-gather.7.cloned.1.call-start = ((), (), s32[]{:S(2)}) async-start(), calls=%async_computation.3 | async-start | bytes 11141120 | tf_op jit(solution)/shard_map/all_gather | solution.py:21
  7.3 183.0 %all-gather.9.cloned.1.call-start = ((), (), s32[]{:S(2)}) async-start(), calls=%async_computation.4 | async-start | bytes 4718592 | tf_op jit(solution)/shard_map/all_gather | solution.py:60
  153.2 6.0 %copy-start.1 = (s32[2,64,64]{2,1,0:T(8,128)S(1)}, s32[2,64,64]{2,1,0:T(8,128)}, u32[]{:S(2)}) copy-start(s32[2,64,64]{2,1,0:T(8,128)} %param.12) | copy-start | bytes 98308
  158.4 65.7 %all-gather.11.cloned.1.call-start = ((), (), s32[]{:S(2)}) async-start(), calls=%async_computation.5 | async-start | bytes 4718592 | tf_op jit(solution)/shard_map/all_gather | solution.py:61
  159.1 254.3 %reduce-scatter.2.cloned.1.call-start = ((), (), s32[]{:S(2)}) async-start(), calls=%async_computation.2 | async-start | bytes 3276800 | tf_op jit(solution)/shard_map/reduce_scatter | solution.py:107
  232.8 5.8 %copy-start = (f32[2,1024,1024]{1,2,0:T(8,128)S(1)}, f32[2,1024,1024]{1,2,0:T(8,128)}, u32[]{:S(2)}) copy-start(f32[2,1024,1024]{1,2,0:T(8,128)} %get-tuple-element.618) | copy-start | bytes 25165828 | tf_op jit(solution)/shard_map/while
  249.6 5.8 %copy-start = (f32[2,1024,1024]{1,2,0:T(8,128)S(1)}, f32[2,1024,1024]{1,2,0:T(8,128)}, u32[]{:S(2)}) copy-start(f32[2,1024,1024]{1,2,0:T(8,128)} %get-tuple-element.618) | copy-start | bytes 25165828 | tf_op jit(solution)/shard_map/while
  266.5 5.8 %copy-start = (f32[2,1024,1024]{1,2,0:T(8,128)S(1)}, f32[2,1024,1024]{1,2,0:T(8,128)}, u32[]{:S(2)}) copy-start(f32[2,1024,1024]{1,2,0:T(8,128)} %get-tuple-element.618) | copy-start | bytes 25165828 | tf_op jit(solution)/shard_map/while
  283.3 5.8 %copy-start = (f32[2,1024,1024]{1,2,0:T(8,128)S(1)}, f32[2,1024,1024]{1,2,0:T(8,128)}, u32[]{:S(2)}) copy-start(f32[2,1024,1024]{1,2,0:T(8,128)} %get-tuple-element.618) | copy-start | bytes 25165828 | tf_op jit(solution)/shard_map/while
  300.2 5.8 %copy-start = (f32[2,1024,1024]{1,2,0:T(8,128)S(1)}, f32[2,1024,1024]{1,2,0:T(8,128)}, u32[]{:S(2)}) copy-start(f32[2,1024,1024]{1,2,0:T(8,128)} %get-tuple-element.618) | copy-start | bytes 25165828 | tf_op jit(solution)/shard_map/while
  317.0 5.8 %copy-start = (f32[2,1024,1024]{1,2,0:T(8,128)S(1)}, f32[2,1024,1024]{1,2,0:T(8,128)}, u32[]{:S(2)}) copy-start(f32[2,1024,1024]{1,2,0:T(8,128)} %get-tuple-element.618) | copy-start | bytes 25165828 | tf_op jit(solution)/shard_map/while
  333.9 5.8 %copy-start = (f32[2,1024,1024]{1,2,0:T(8,128)S(1)}, f32[2,1024,1024]{1,2,0:T(8,128)}, u32[]{:S(2)}) copy-start(f32[2,1024,1024]{1,2,0:T(8,128)} %get-tuple-element.618) | copy-start | bytes 25165828 | tf_op jit(solution)/shard_map/while
  350.8 5.8 %copy-start = (f32[2,1024,1024]{1,2,0:T(8,128)S(1)}, f32[2,1024,1024]{1,2,0:T(8,128)}, u32[]{:S(2)}) copy-start(f32[2,1024,1024]{1,2,0:T(8,128)} %get-tuple-element.618) | copy-start | bytes 25165828 | tf_op jit(solution)/shard_map/while
Sparse Core Ops, SparseCore 0:
  9.5 82.9 all-gather.6
  158.5 31.6 all-gather.8
  192.0 32.0 all-gather.10
  381.6 31.8 reduce-scatter.1
where the time goes:
time: 421 us; the launch traced here: 420 us
  waiting for transfers between devices  182 us (43%)
  matrix products  117 us (28%)
  other arithmetic  46.7 us (11%)
  local copies, waits for them, and re-layouts  45.1 us (11%)
  blocking collectives  14 us (3%)
  between operations  13.2 us (3%)
    all_gather x1, waiting for transfers between devices, local(): lax.all_gather(tokens[None], ('ulysses', 'tensor'), axis=0, tiled=True)  84.5 us
    dot_general x16, matrix products, one_shard(): jnp.einsum('rd,dcn->rcn', token_part, weights, preferred_element_type=jnp...  41.7 us
    dot_general x8, matrix products, one_block(): jnp.einsum('qhd,khd->hqk', queries, key_part, preferred_element_type=jnp....  38.2 us
    reduce_sum x8, other arithmetic, one_block(): denominator = denominator * factor + jnp.sum(weights, axis=-1)  37.5 us
    all_gather x1, waiting for transfers between devices, local(): value_all = lax.all_gather(values, 'blk', axis=0, tiled=True)  33.8 us
    reduce_scatter x1, waiting for transfers between devices, local(): lax.psum_scatter(partial_value.astype(jnp.bfloat16), 'tensor', scatter_di...  32 us
    all_gather x1, waiting for transfers between devices, local(): key_all = lax.all_gather(keys, 'blk', axis=0, tiled=True)  30.5 us
    dot_general x8, matrix products, one_block(): jnp.einsum('hqk,khd->hqd', weights.astype(jnp.bfloat16), value_part, pref...  18.7 us
  transfers between devices with their start and end apart: 4, of which 4 were waited for; matrix products, arithmetic and copies ran while one was open for 0% of the time, Pallas kernels for 0%

commit v1 on v0

v1 whole, which is shorter than its diff:
```python
import functools
import math

import jax
import jax.numpy as jnp
from jax import lax
from jax.experimental import pallas as pl
from jax.experimental.pallas import tpu as pltpu
from jax.sharding import PartitionSpec as P

HD = 128
BLOCK = 128
NEG = -1e30
LOG2E = 1.4426950408889634
OFFSETS = (0, -1, 1, 2)
CONTRACT_LAST = (((1,), (1,)), ((), ()))


def ring(n, step):
    return [(i, (i + step) % n) for i in range(n)]


def y_ring(n, step):
    return [(i, (i + 2 * step) % n) for i in range(n)]


def core_swap(n):
    return [(i, i ^ 1) for i in range(n)]


def attn_kernel(bk, q_ref, qm_ref, *refs):
    kv_refs, o_ref = refs[:-1], refs[-1]
    rows = q_ref.shape[0]
    q = jnp.concatenate([q_ref[...], qm_ref[...]], axis=1)
    tiles = [(r, j) for r in range(len(kv_refs)) for j in range(kv_refs[r].shape[0] // bk)]
    lane = lax.broadcasted_iota(jnp.int32, (bk, HD), 1)
    inner = lax.broadcasted_iota(jnp.int32, (bk, HD), 0) // BLOCK
    ones = (lane == 0).astype(jnp.float32).astype(jnp.bfloat16)
    per_tile = bk // BLOCK

    def score(i):
        r, j = tiles[i]
        onehot = (lane == inner + i * per_tile).astype(jnp.float32).astype(jnp.bfloat16)
        k = jnp.concatenate([kv_refs[r][j * bk : (j + 1) * bk, :HD], onehot], axis=1)
        return lax.dot_general(q, k, CONTRACT_LAST, preferred_element_type=jnp.float32)

    high = jnp.full((rows, 1), -3e38, jnp.float32)
    acc = jnp.zeros((rows, 2 * HD), jnp.float32)
    s = score(0)
    for i in range(len(tiles)):
        s_next = score(i + 1) if i + 1 < len(tiles) else None
        new_high = jnp.maximum(high, jnp.max(s, axis=1, keepdims=True))
        p = jnp.exp2(s - new_high).astype(jnp.bfloat16)
        factor = jnp.exp2(high - new_high)
        r, j = tiles[i]
        v = jnp.concatenate([kv_refs[r][j * bk : (j + 1) * bk, HD:], ones], axis=1)
        acc = acc * factor + jnp.dot(p, v, preferred_element_type=jnp.float32)
        high = new_high
        s = s_next
    o_ref[...] = (acc[:, :HD] / acc[:, HD : HD + 1]).astype(jnp.bfloat16)


def attention(q, qm, kvs, bq=512, bk=512):
    rows = q.shape[0]
    keys = sum(kv.shape[0] for kv in kvs)
    return pl.pallas_call(
        functools.partial(attn_kernel, bk),
        grid=(rows // bq,),
        in_specs=[pl.BlockSpec((bq, HD), lambda i: (i, 0)), pl.BlockSpec((bq, HD), lambda i: (i, 0))]
        + [pl.BlockSpec(kv.shape, lambda i: (0, 0)) for kv in kvs],
        out_specs=pl.BlockSpec((bq, HD), lambda i: (i, 0)),
        out_shape=jax.ShapeDtypeStruct((rows, HD), jnp.bfloat16),
        compiler_params=pltpu.CompilerParams(vmem_limit_bytes=48 << 20),
        cost_estimate=pl.CostEstimate(
            flops=8 * rows * keys * HD, bytes_accessed=keys * 512, transcendentals=rows * keys
        ),
    )(q, qm, *kvs)


def local(tokens, w_qkv, qkv_scale, block_mask, w_out):
    nu, nb, nt = lax.axis_size("ulysses"), lax.axis_size("blk"), lax.axis_size("tensor")
    u, b, t = lax.axis_index("ulysses"), lax.axis_index("blk"), lax.axis_index("tensor")
    y, core = b // 2, b % 2
    feat = tokens.shape[1]
    half = tokens.shape[0] // 2
    quarter = half // 2
    pp = lax.ppermute

    def direct(value, axis, n):
        return [value] + [pp(value, axis, ring(n, s)) for s in (1, -1, 2)]

    w_rel = [
        lax.dynamic_slice_in_dim(w_qkv, ((t + o) % nt) * feat, feat, 0) for o in OFFSETS
    ]
    scale = qkv_scale * jnp.array([LOG2E / math.sqrt(HD), 1.0, 1.0], jnp.float32)[:, None]

    a_own = jnp.concatenate(direct(tokens[:half], "tensor", nt), axis=1)
    b_own = jnp.concatenate(direct(tokens[half:], "ulysses", nu), axis=0)

    a_m = pp(a_own, "ulysses", ring(nu, 1))
    b_m = pp(b_own, "tensor", ring(nt, 1))
    a_p = pp(a_own, "ulysses", ring(nu, -1))
    b_p = pp(b_own, "tensor", ring(nt, -1))
    a_opp = jnp.concatenate(
        [
            pp(a_m[:quarter], "ulysses", ring(nu, 1)),
            pp(a_p[quarter:], "ulysses", ring(nu, -1)),
        ],
        axis=0,
    )
    bh = b_own.shape[0] // 2
    b_opp = jnp.concatenate(
        [pp(b_m[:bh], "tensor", ring(nt, 1)), pp(b_p[bh:], "tensor", ring(nt, -1))], axis=0
    )

    def project(value, w):
        return jnp.einsum("rd,dcn->rcn", value, w, preferred_element_type=jnp.float32)

    w_full = jnp.concatenate(w_rel, axis=0)

    def finish(acc):
        rows = acc.shape[0]
        full = acc.reshape(rows, 3, 2, HD) * scale[None, :, :, None]
        full = full.astype(jnp.bfloat16)
        keep = lax.dynamic_index_in_dim(full, core, 2, keepdims=False)
        give = lax.dynamic_index_in_dim(full, 1 - core, 2, keepdims=False)
        got = pp(give.reshape(rows, 3 * HD), "blk", core_swap(nb))
        both = jnp.concatenate([keep.reshape(rows, 3 * HD), got], axis=0)
        kv = lax.all_gather(
            both[:, HD:],
            "blk",
            axis=0,
            tiled=True,
            axis_index_groups=[list(range(0, nb, 2)), list(range(1, nb, 2))],
        )
        return both[:, :HD], kv

    acc_a = jnp.concatenate([project(v, w_full) for v in (a_own, a_m, a_p, a_opp)], axis=0)
    q_a, kv_a = finish(acc_a)
    acc_b = sum(project(v, w) for v, w in zip((b_own, b_m, b_p, b_opp), w_rel))
    q_b, kv_b = finish(acc_b)

    groups = (u + jnp.array(OFFSETS, jnp.int32)) % nu
    cores = jnp.stack([core, 1 - core])

    def block_ids(ys, odd):
        return (
            ((groups[None, None, :] * nb + 2 * ys[:, None, None] + cores[None, :, None]) * 2 + odd)
        ).reshape(-1)

    all_y = jnp.arange(nb // 2, dtype=jnp.int32)
    key_ids = jnp.concatenate([block_ids(all_y, 0), block_ids(all_y, 1)])
    query_ids = jnp.concatenate([block_ids(y[None], 0), block_ids(y[None], 1)])
    blocks = jnp.arange(block_mask.shape[1], dtype=jnp.int32)
    key_hot = (key_ids[:, None] == blocks[None, :]).astype(jnp.float32)
    query_hot = (query_ids[:, None] == blocks[None, :]).astype(jnp.float32)
    mask = lax.dynamic_index_in_dim(block_mask, core, 0, keepdims=False).astype(jnp.float32)
    live = query_hot @ mask @ key_hot.T > 0.5
    live = live | (query_ids[:, None] == key_ids[None, :])
    bias = jnp.where(live, 0.0, NEG).astype(jnp.bfloat16)
    bias = jnp.pad(bias, ((0, 0), (0, HD - bias.shape[1])))
    bias = jnp.repeat(bias, BLOCK, axis=0)

    out = attention(jnp.concatenate([q_a, q_b], axis=0), bias, [kv_a, kv_b])

    out = out.reshape(2, 2, nu, half, HD)
    other = pp(out[:, 1], "blk", core_swap(nb))
    mine = out[:, 0]
    first = jnp.where(core == 0, mine, other)
    second = jnp.where(core == 0, other, mine)
    heads = jnp.concatenate([first, second], axis=-1)
    heads = heads.transpose(1, 0, 2, 3).reshape(nu, 2 * half, 2 * HD)
    arrived = [heads[0]] + [
        pp(heads[i], "ulysses", ring(nu, OFFSETS[i])) for i in range(1, nu)
    ]
    partial_value = sum(
        jnp.dot(
            v,
            lax.dynamic_index_in_dim(w_out, (u - o) % nu, 0, keepdims=False),
            preferred_element_type=jnp.float32,
        )
        for v, o in zip(arrived, OFFSETS)
    )
    return lax.psum_scatter(
        partial_value.astype(jnp.bfloat16), "tensor", scatter_dimension=1, tiled=True
    )


def solution(mesh):
    return jax.shard_map(
        local,
        mesh=mesh,
        in_specs=(
            P(("ulysses", "blk"), "tensor"),
            P(None, None, ("ulysses", "tensor")),
            P(None, ("ulysses", "tensor")),
            P(("ulysses", "tensor"), None, None),
            P(None, "tensor", None),
        ),
        out_specs=P(("ulysses", "blk"), "tensor"),
        check_vma=False,
    )
```

time: 421 us -> 250 us (0.59)
  matrix products: 117 us -> 34.2 us
  waiting for transfers between devices: 182 us -> 119 us
  other arithmetic: 46.7 us -> 7.24 us
  starting transfers between devices: 0.12 us -> 30.4 us
  local copies, waits for them, and re-layouts: 45.1 us -> 23.1 us
  Pallas kernels: 0 us -> 21.5 us
  blocking collectives: 14 us -> 0 us
    all_gather x3 -> x2, waiting for transfers between devices: 149 us -> 60.7 us  [finish(): lax.all_gather(both[:, HD:], 'blk', axis=0, tiled=True, axis_index_groups...]
    dot_general x41 -> x13, matrix products: 117 us -> 34.2 us  [the longest x8 25.3 us: project(): jnp.einsum('rd,dcn->rcn', value, w, preferred_element_type=jnp.float32)]
    reduce_sum x8 -> x0, other arithmetic: 37.5 us -> none  [one_block(): denominator = denominator * factor + jnp.sum(weights, axis=-1)]
    ppermute x0 -> x20, starting transfers between devices: none -> 30.1 us  [the longest x6 11.1 us: direct(): return [value] + [pp(value, axis, ring(n, s)) for s in (1, -1, 2)]]
    dynamic_slice x24 -> x2, local copies, waits for them, and re-layouts: 30.5 us -> 6.12 us  [the longest x1 5.93 us: local(): lax.dynamic_slice_in_dim(w_qkv, (t + o) % nt * feat, feat, 0)]
    ppermute x0 -> x20, waiting for transfers between devices: none -> 24.3 us  [the longest x1 16 us: local(): a_p = pp(a_own, 'ulysses', ring(nu, -1))]
    pallas_call x0 -> x1, Pallas kernels: none -> 21.5 us  [attention(): pl.pallas_call(functools.partial(attn_kernel, bk), grid=(rows // bq,), in...]
    all_to_all x1 -> x0, blocking collectives: 14 us -> none  [local(): lax.all_to_all(grouped, 'ulysses', split_axis=1, concat_axis=0, tiled=True)]
  transfers between devices with their start and end apart: 4 -> 23, of which waited for: 4 -> 10; matrix products, arithmetic and copies ran while one was open for 0% -> 21% of each run, Pallas kernels for 0% -> 0%
where the time goes in v1:
time: 250 us; the launch traced here: 249 us
  waiting for transfers between devices  119 us (48%)
  matrix products  34.2 us (14%)
  starting transfers between devices  30.4 us (12%)
  local copies, waits for them, and re-layouts  23.1 us (9%)
  Pallas kernels  21.5 us (9%)
  between operations  13.6 us (5%)
  other arithmetic  7.24 us (3%)
    all_gather x2, waiting for transfers between devices, finish(): lax.all_gather(both[:, HD:], 'blk', axis=0, tiled=True, axis_index_groups...  60.7 us
    reduce_scatter x1, waiting for transfers between devices, local(): lax.psum_scatter(partial_value.astype(jnp.bfloat16), 'tensor', scatter_di...  33.6 us
    dot_general x8, matrix products, project(): jnp.einsum('rd,dcn->rcn', value, w, preferred_element_type=jnp.float32)  25.3 us
    pallas_call x1, Pallas kernels, attention(): pl.pallas_call(functools.partial(attn_kernel, bk), grid=(rows // bq,), in...  21.5 us
    ppermute x1, waiting for transfers between devices, local(): a_p = pp(a_own, 'ulysses', ring(nu, -1))  16 us
    ppermute x6, starting transfers between devices, direct(): return [value] + [pp(value, axis, ring(n, s)) for s in (1, -1, 2)]  11.1 us
    dot_general x4, matrix products, local(): jnp.dot(v, lax.dynamic_index_in_dim(w_out, (u - o) % nu, 0, keepdims=Fals...  8.61 us
    dynamic_slice x1, local copies, waits for them, and re-layouts, local(): lax.dynamic_slice_in_dim(w_qkv, (t + o) % nt * feat, feat, 0)  5.93 us
  transfers between devices with their start and end apart: 23, of which 10 were waited for; matrix products, arithmetic and copies ran while one was open for 21% of the time, Pallas kernels for 0%

profile of v1, /device:TPU:0, one launch (start us, length us, event | category | flops | bytes accessed | tf_op | source)
XLA Modules:
  0.0 248.7 jit_solution(7267079585690601315)
XLA Ops:
  7.7 3.2 %collective-permute-start.2 = (bf16[128,1280]{1,0:T(8,128)(2,1)S(1)}, bf16[128,1280]{1,0:T(8,128)(2,1)S(1)}, u32[]{:S(2)}, u32[]{:S(2)}) collective-permute-start(bf16[128,1280]{1,0:T(8,128)(2,1)S(1)} %get-tuple-element.19), channel_id=1, source_target_pairs={{0,2},{1,3},{2,0},{3,1},{4,6},{5,7},{6,4},{7,5},{8,10},{9,11},{10,... | collective-permute-start | bytes 983048 | tf_op jit(solution)/shard_map/ppermute | solution.py:90
  12.9 3.9 %collective-permute-start.10 = (bf16[128,1280]{1,0:T(8,128)(2,1)S(1)}, bf16[128,1280]{1,0:T(8,128)(2,1)}, u32[]{:S(2)}, u32[]{:S(2)}) collective-permute-start(bf16[128,1280]{1,0:T(8,128)(2,1)S(1)} %get-tuple-element.20), channel_id=1, source_target_pairs={{0,64},{32,96},{64,0},{96,32},{1,65},{33,97},{65,1},{97,33},{2,66}... | collective-permute-start | bytes 983048 | tf_op jit(solution)/shard_map/ppermute | solution.py:90
  17.5 5.9 %constant_dynamic-slice_fusion.4 = (bf16[1280,3,256]{2,0,1:T(8,128)(2,1)S(1)}, bf16[1280,3,256]{2,0,1:T(8,128)(2,1)}, bf16[1280,3,256]{2,0,1:T(8,128)(2,1)}, bf16[1280,3,256]{2,0,1:T(8,128)(2,1)}) fusion(bf16[5120,3,256]{2,0,1:T(8,128)(2,1)} %param.8, s32[]{:T(128)S(6)} %select_n.110, s32[]{:T(128)S(6)} %select_n.106, s32[]{:T(128)S(6)} %select_n.104, ...), kind=kLoop, calls=%fused_computation.75 | loop fusion | bytes 15728656 | tf_op jit(solution)/shard_map/dynamic_slice | solution.py:93
  28.1 4.0 %collective-permute-start.4 = (bf16[128,5120]{1,0:T(8,128)(2,1)}, bf16[128,5120]{1,0:T(8,128)(2,1)}, u32[]{:S(2)}, u32[]{:S(2)}) collective-permute-start(bf16[128,5120]{1,0:T(8,128)(2,1)} %pad_maximum_fusion.2), channel_id=1, source_target_pairs={{0,96},{32,0},{64,32},{96,64},{1,97},{33,1},{65,33},{97,65},{2,98}... | collective-permute-start | bytes 3932168 | tf_op jit(solution)/shard_map/ppermute | solution.py:102
  33.4 2.3 pad_maximum_fusion.3
  35.6 2.4 collective-permute-start.12
  38.1 4.4 %fusion.23 = f32[512,3,256]{0,2,1:T(8,128)} fusion(bf16[1280,3,256]{2,0,1:T(8,128)(2,1)} %get-tuple-element.11, bf16[128,1280]{1,0:T(8,128)(2,1)} %collective-permute-done.10, bf16[128,1280]{1,0:T(8,128)(2,1)} %collective-permute-done.9, bf16[128,1280]{1,0:T(8,128)(2,1)} %copy-done.5, bf16[128,1280]{1,0:T(8,128)(2,1)S(1)} %get-tuple-element.20), kind=kOutput, calls=%fused_computation.34 | convolution fusion | flops 1011875840 | bytes 4849664 | tf_op jit(solution)/shard_map/rd,dcn->rcn/dot_general | solution.py:117
  44.6 16.0 %collective-permute-done.4 = bf16[128,5120]{1,0:T(8,128)(2,1)} collective-permute-done((bf16[128,5120]{1,0:T(8,128)(2,1)}, bf16[128,5120]{1,0:T(8,128)(2,1)}, u32[]{:S(2)}, u32[]{:S(2)}) %collective-permute-start.4) | collective-permute-done | bytes 1310752 | tf_op jit(solution)/shard_map/ppermute | solution.py:102
  61.8 3.8 %collective-permute-start.6 = (bf16[64,5120]{1,0:T(8,128)(2,1)S(1)}, bf16[64,5120]{1,0:T(8,128)(2,1)S(1)}, u32[]{:S(2)}, u32[]{:S(2)}) collective-permute-start(bf16[64,5120]{1,0:T(8,128)(2,1)S(1)} %slice.69), channel_id=1, source_target_pairs={{0,96},{32,0},{64,32},{96,64},{1,97},{33,1},{65,33},{97,65},{2,98}... | collective-permute-start | bytes 1966088 | tf_op jit(solution)/shard_map/ppermute | solution.py:107
  68.7 3.1 %collective-permute-start.14 = (bf16[256,1280]{1,0:T(8,128)(2,1)}, bf16[256,1280]{1,0:T(8,128)(2,1)}, u32[]{:S(2)}, u32[]{:S(2)}) collective-permute-start(bf16[256,1280]{1,0:T(8,128)(2,1)} %slice.71), channel_id=1, source_target_pairs={{0,3},{1,0},{2,1},{3,2},{4,7},{5,4},{6,5},{7,6},{8,11},{9,8},{10,9... | collective-permute-start | bytes 1966088 | tf_op jit(solution)/shard_map/ppermute | solution.py:113
  73.8 3.1 %fusion.25 = f32[128,3,256]{2,0,1:T(8,128)S(1)} fusion(bf16[128,5120]{1,0:T(8,128)(2,1)} %collective-permute-done.4, bf16[1280,3,256]{2,0,1:T(8,128)(2,1)S(1)} %get-tuple-element.9, bf16[1280,3,256]{2,0,1:T(8,128)(2,1)S(1)} %copy-done.4, bf16[1280,3,256]{2,0,1:T(8,128)(2,1)S(1)} %copy-done.2, bf16[1280,3,256]{2,0,1:T(8,128)(2,1)S(1)} %copy-done.3), kind=kOutput, calls=%fused_computation.36 | convolution fusion | flops 1038090240 | bytes 9568256 | tf_op jit(solution)/shard_map/rd,dcn->rcn/dot_general | solution.py:117
  76.9 3.7 %fusion.19 = f32[512,3,256]{0,2,1:T(8,128)} fusion(bf16[1280,3,256]{2,0,1:T(8,128)(2,1)S(1)} %copy-done.4, bf16[512,1280]{1,0:T(8,128)(2,1)} %collective-permute-done.12), kind=kOutput, calls=%fused_computation.30 | convolution fusion | flops 1006632960 | bytes 4849664 | tf_op jit(solution)/shard_map/rd,dcn->rcn/dot_general | solution.py:117
  80.6 3.7 %fusion.21 = f32[512,3,256]{0,2,1:T(8,128)} fusion(bf16[1280,3,256]{2,0,1:T(8,128)(2,1)S(1)} %copy-done.2, bf16[512,1280]{1,0:T(8,128)(2,1)} %collective-permute-done.11), kind=kOutput, calls=%fused_computation.32 | convolution fusion | flops 1006632960 | bytes 4849664 | tf_op jit(solution)/shard_map/rd,dcn->rcn/dot_general | solution.py:117
  84.3 3.1 %fusion.27 = f32[128,3,256]{2,0,1:T(8,128)S(1)} fusion(bf16[128,5120]{1,0:T(8,128)(2,1)} %collective-permute-done.3, bf16[1280,3,256]{2,0,1:T(8,128)(2,1)S(1)} %get-tuple-element.9, bf16[1280,3,256]{2,0,1:T(8,128)(2,1)S(1)} %copy-done.4, bf16[1280,3,256]{2,0,1:T(8,128)(2,1)S(1)} %copy-done.2, bf16[1280,3,256]{2,0,1:T(8,128)(2,1)S(1)} %copy-done.3), kind=kOutput, calls=%fused_computation.38 | convolution fusion | flops 1038090240 | bytes 9568256 | tf_op jit(solution)/shard_map/rd,dcn->rcn/dot_general | solution.py:117
  90.6 2.5 %copy.15 = f32[512,3,2,128]{0,3,1,2:T(8,128)S(1)} copy(f32[512,3,2,128]{3,2,0,1:T(2,128)} %reshape.124) | data formatting | bytes 3145728 | tf_op jit(solution)/shard_map/reshape | solution.py:123
  93.2 4.0 %add_add_fusion = f32[512,3,256]{0,2,1:T(8,128)S(1)} fusion(f32[512,3,256]{0,2,1:T(8,128)} %fusion.19, f32[512,3,256]{0,2,1:T(8,128)} %fusion.23, f32[512,3,256]{0,2,1:T(8,128)} %fusion.21, bf16[1280,3,256]{2,0,1:T(8,128)(2,1)S(1)} %get-tuple-element.9, bf16[256,1280]{1,0:T(8,128)(2,1)} %collective-permute-done.14, ...), kind=kOutput, calls=%fused_computation.18 | convolution fusion | flops 1010434048 | bytes 9568256 | tf_op jit(solution)/shard_map/rd,dcn->rcn/dot_general | solution.py:117
  105.1 28.2 %all-gather.3.cloned.1.call-done.refs_0_ = bf16[4096,256]{1,0:T(8,128)(2,1)} async-done(((bf16[1024,256]{1,0:T(8,128)(2,1)}), bf16[4096,256]{1,0:T(8,128)(2,1)}) %all-gather.3.cloned.1.call-update) | async-done | bytes 2097168 | tf_op jit(solution)/shard_map/all_gather | solution.py:129
  133.2 32.6 %all-gather.5.cloned.1.call-done.refs_1_ = bf16[4096,256]{1,0:T(8,128)(2,1)} async-done(((bf16[1024,256]{1,0:T(8,128)(2,1)}), bf16[4096,256]{1,0:T(8,128)(2,1)}) %all-gather.5.cloned.1.call-update) | async-done | bytes 2097168 | tf_op jit(solution)/shard_map/all_gather | solution.py:129
  169.1 21.5 %shard_map.73 = bf16[2048,128]{1,0:T(8,128)(2,1)S(1)} custom-call(bf16[2048,128]{1,0:T(8,128)(2,1)S(1)} %fusion.46.q_ref, bf16[2048,128]{1,0:T(8,128)(2,1)S(1)} %bitcast.79, bf16[4096,256]{1,0:T(8,128)(2,1)S(1)} %copy-done, bf16[4096,256]{1,0:T(8,128)(2,1)S(1)} %copy-done.1), custom_call_target="tpu_custom_call" | custom-call | flops 17179869184 | bytes 4194304 | tf_op jit(solution)/shard_map/pallas_call | solution.py:66
  192.4 3.2 %collective-permute-start.19 = (bf16[256,256]{1,0:T(8,128)(2,1)S(1)}, bf16[256,256]{1,0:T(8,128)(2,1)S(1)}, u32[]{:S(2)}, u32[]{:S(2)}) collective-permute-start(bf16[256,256]{1,0:T(8,128)(2,1)S(1)} %bitcast.91), channel_id=1, source_target_pairs={{0,64},{32,96},{64,0},{96,32},{1,65},{33,97},{65,1},{97,33},{2,66}... | collective-permute-start | bytes 393224 | tf_op jit(solution)/shard_map/ppermute | solution.py:174
  197.7 2.7 %fusion.6 = f32[256,5120]{1,0:T(8,128)S(1)} fusion(bf16[256,256]{1,0:T(8,128)(2,1)S(1)} %bitcast.89, bf16[4,256,5120]{2,1,0:T(8,128)(2,1)} %param.11, s32[]{:T(128)S(6)} %select_n.119), kind=kOutput, calls=%fused_computation.9 | convolution fusion | flops 671088640 | bytes 7995396 | tf_op jit(solution)/shard_map/dot_general | solution.py:177
  202.6 2.6 %convolution_add_fusion.1 = f32[256,5120]{1,0:T(8,128)S(1)} fusion(f32[256,5120]{1,0:T(8,128)S(1)} %fusion.6, bf16[256,256]{1,0:T(8,128)(2,1)S(1)} %collective-permute-done.17, bf16[4,256,5120]{2,1,0:T(8,128)(2,1)} %param.11, s32[]{:T(128)S(6)} %select_n.121), kind=kOutput, calls=%fused_computation.2 | convolution fusion | flops 672399360 | bytes 13238276 | tf_op jit(solution)/shard_map/dot_general | solution.py:177
  206.2 2.4 fusion.1
  208.6 33.6 %reduce-scatter.2.cloned.1.call-done = bf16[256,1280]{1,0:T(8,128)(2,1)} async-done(((bf16[256,5120]{1,0:T(8,128)(2,1)}), bf16[256,1280]{1,0:T(8,128)(2,1)}) %reduce-scatter.2.cloned.1.call-update) | async-done | bytes 655376 | tf_op jit(solution)/shard_map/reduce_scatter | solution.py:184
  (106 shorter events, 39.3 us)
Async XLA Ops:
  6.5 126.7 %all-gather.3.cloned.1.call-start = ((), (), s32[]{:S(2)}) async-start(), calls=%async_computation.1 | async-start | bytes 2621440 | tf_op jit(solution)/shard_map/all_gather | solution.py:129
  7.7 15.7 %collective-permute-start.2 = (bf16[128,1280]{1,0:T(8,128)(2,1)S(1)}, bf16[128,1280]{1,0:T(8,128)(2,1)S(1)}, u32[]{:S(2)}, u32[]{:S(2)}) collective-permute-start(bf16[128,1280]{1,0:T(8,128)(2,1)S(1)} %get-tuple-element.19), channel_id=1, source_target_pairs={{0,2},{1,3},{2,0},{3,1},{4,6},{5,7},{6,4},{7,5},{8,10},{9,11},{10,... | collective-permute-start | bytes 983048 | tf_op jit(solution)/shard_map/ppermute | solution.py:90
  10.8 15.1 %collective-permute-start.1 = (bf16[128,1280]{1,0:T(8,128)(2,1)S(1)}, bf16[128,1280]{1,0:T(8,128)(2,1)S(1)}, u32[]{:S(2)}, u32[]{:S(2)}) collective-permute-start(bf16[128,1280]{1,0:T(8,128)(2,1)S(1)} %get-tuple-element.19), channel_id=1, source_target_pairs={{0,3},{1,0},{2,1},{3,2},{4,7},{5,4},{6,5},{7,6},{8,11},{9,8},{10,9... | collective-permute-start | bytes 983048 | tf_op jit(solution)/shard_map/ppermute | solution.py:90
  12.0 13.9 %collective-permute-start = (bf16[128,1280]{1,0:T(8,128)(2,1)S(1)}, bf16[128,1280]{1,0:T(8,128)(2,1)}, u32[]{:S(2)}, u32[]{:S(2)}) collective-permute-start(bf16[128,1280]{1,0:T(8,128)(2,1)S(1)} %get-tuple-element.19), channel_id=1, source_target_pairs={{0,1},{1,2},{2,3},{3,0},{4,5},{5,6},{6,7},{7,4},{8,9},{9,10},{10,1... | collective-permute-start | bytes 983048 | tf_op jit(solution)/shard_map/ppermute | solution.py:90
  12.9 19.3 %collective-permute-start.10 = (bf16[128,1280]{1,0:T(8,128)(2,1)S(1)}, bf16[128,1280]{1,0:T(8,128)(2,1)}, u32[]{:S(2)}, u32[]{:S(2)}) collective-permute-start(bf16[128,1280]{1,0:T(8,128)(2,1)S(1)} %get-tuple-element.20), channel_id=1, source_target_pairs={{0,64},{32,96},{64,0},{96,32},{1,65},{33,97},{65,1},{97,33},{2,66}... | collective-permute-start | bytes 983048 | tf_op jit(solution)/shard_map/ppermute | solution.py:90
  16.7 15.4 %collective-permute-start.9 = (bf16[128,1280]{1,0:T(8,128)(2,1)S(1)}, bf16[128,1280]{1,0:T(8,128)(2,1)}, u32[]{:S(2)}, u32[]{:S(2)}) collective-permute-start(bf16[128,1280]{1,0:T(8,128)(2,1)S(1)} %get-tuple-element.20), channel_id=1, source_target_pairs={{0,96},{32,0},{64,32},{96,64},{1,97},{33,1},{65,33},{97,65},{2,98}... | collective-permute-start | bytes 983048 | tf_op jit(solution)/shard_map/ppermute | solution.py:90
  23.4 9.3 %collective-permute-start.8 = (bf16[128,1280]{1,0:T(8,128)(2,1)S(1)}, bf16[128,1280]{1,0:T(8,128)(2,1)S(1)}, u32[]{:S(2)}, u32[]{:S(2)}) collective-permute-start(bf16[128,1280]{1,0:T(8,128)(2,1)S(1)} %get-tuple-element.20), channel_id=1, source_target_pairs={{0,32},{32,64},{64,96},{96,0},{1,33},{33,65},{65,97},{97,1},{2,34}... | collective-permute-start | bytes 983048 | tf_op jit(solution)/shard_map/ppermute | solution.py:90
  28.1 9.9 %copy-start.7 = (f32[3]{0:T(128)S(1)}, f32[3]{0:T(128)}, u32[]{:S(2)}) copy-start(f32[3]{0:T(128)} %constant.140.clone) | copy-start | bytes 40
  28.1 32.5 %collective-permute-start.4 = (bf16[128,5120]{1,0:T(8,128)(2,1)}, bf16[128,5120]{1,0:T(8,128)(2,1)}, u32[]{:S(2)}, u32[]{:S(2)}) collective-permute-start(bf16[128,5120]{1,0:T(8,128)(2,1)} %pad_maximum_fusion.2), channel_id=1, source_target_pairs={{0,96},{32,0},{64,32},{96,64},{1,97},{33,1},{65,33},{97,65},{2,98}... | collective-permute-start | bytes 3932168 | tf_op jit(solution)/shard_map/ppermute | solution.py:102
  32.1 33.4 %collective-permute-start.3 = (bf16[128,5120]{1,0:T(8,128)(2,1)}, bf16[128,5120]{1,0:T(8,128)(2,1)}, u32[]{:S(2)}, u32[]{:S(2)}) collective-permute-start(bf16[128,5120]{1,0:T(8,128)(2,1)} %pad_maximum_fusion.2), channel_id=1, source_target_pairs={{0,32},{32,64},{64,96},{96,0},{1,33},{33,65},{65,97},{97,1},{2,34}... | collective-permute-start | bytes 3932168 | tf_op jit(solution)/shard_map/ppermute | solution.py:100
  35.6 31.1 %collective-permute-start.12 = (bf16[512,1280]{1,0:T(8,128)(2,1)}, bf16[512,1280]{1,0:T(8,128)(2,1)}, u32[]{:S(2)}, u32[]{:S(2)}) collective-permute-start(bf16[512,1280]{1,0:T(8,128)(2,1)} %pad_maximum_fusion.3), channel_id=1, source_target_pairs={{0,3},{1,0},{2,1},{3,2},{4,7},{5,4},{6,5},{7,6},{8,11},{9,8},{10,9... | collective-permute-start | bytes 3932168 | tf_op jit(solution)/shard_map/ppermute | solution.py:103
  38.0 33.8 %collective-permute-start.11 = (bf16[512,1280]{1,0:T(8,128)(2,1)}, bf16[512,1280]{1,0:T(8,128)(2,1)}, u32[]{:S(2)}, u32[]{:S(2)}) collective-permute-start(bf16[512,1280]{1,0:T(8,128)(2,1)} %pad_maximum_fusion.3), channel_id=1, source_target_pairs={{0,1},{1,2},{2,3},{3,0},{4,5},{5,6},{6,7},{7,4},{8,9},{9,10},{10,1... | collective-permute-start | bytes 3932168 | tf_op jit(solution)/shard_map/ppermute | solution.py:101
  61.8 25.6 %collective-permute-start.6 = (bf16[64,5120]{1,0:T(8,128)(2,1)S(1)}, bf16[64,5120]{1,0:T(8,128)(2,1)S(1)}, u32[]{:S(2)}, u32[]{:S(2)}) collective-permute-start(bf16[64,5120]{1,0:T(8,128)(2,1)S(1)} %slice.69), channel_id=1, source_target_pairs={{0,96},{32,0},{64,32},{96,64},{1,97},{33,1},{65,33},{97,65},{2,98}... | collective-permute-start | bytes 1966088 | tf_op jit(solution)/shard_map/ppermute | solution.py:107
  66.7 20.7 %collective-permute-start.5 = (bf16[64,5120]{1,0:T(8,128)(2,1)S(1)}, bf16[64,5120]{1,0:T(8,128)(2,1)S(1)}, u32[]{:S(2)}, u32[]{:S(2)}) collective-permute-start(bf16[64,5120]{1,0:T(8,128)(2,1)S(1)} %slice.68), channel_id=1, source_target_pairs={{0,32},{32,64},{64,96},{96,0},{1,33},{33,65},{65,97},{97,1},{2,34}... | collective-permute-start | bytes 1966088 | tf_op jit(solution)/shard_map/ppermute | solution.py:106
  68.7 24.4 %collective-permute-start.14 = (bf16[256,1280]{1,0:T(8,128)(2,1)}, bf16[256,1280]{1,0:T(8,128)(2,1)}, u32[]{:S(2)}, u32[]{:S(2)}) collective-permute-start(bf16[256,1280]{1,0:T(8,128)(2,1)} %slice.71), channel_id=1, source_target_pairs={{0,3},{1,0},{2,1},{3,2},{4,7},{5,4},{6,5},{7,6},{8,11},{9,8},{10,9... | collective-permute-start | bytes 1966088 | tf_op jit(solution)/shard_map/ppermute | solution.py:113
  73.8 19.4 %collective-permute-start.13 = (bf16[256,1280]{1,0:T(8,128)(2,1)}, bf16[256,1280]{1,0:T(8,128)(2,1)}, u32[]{:S(2)}, u32[]{:S(2)}) collective-permute-start(bf16[256,1280]{1,0:T(8,128)(2,1)} %slice.70), channel_id=1, source_target_pairs={{0,1},{1,2},{2,3},{3,0},{4,5},{5,6},{6,7},{7,4},{8,9},{9,10},{10,1... | collective-permute-start | bytes 1966088 | tf_op jit(solution)/shard_map/ppermute | solution.py:113
  98.1 1.8 collective-permute-start.7
  100.7 65.1 %all-gather.5.cloned.1.call-start = ((), (), s32[]{:S(2)}) async-start(), calls=%async_computation.2 | async-start | bytes 2621440 | tf_op jit(solution)/shard_map/all_gather | solution.py:129
  101.0 1.8 collective-permute-start.15
  103.7 138.5 %reduce-scatter.2.cloned.1.call-start = ((), (), s32[]{:S(2)}) async-start(), calls=%async_computation.3 | async-start | bytes 3276800 | tf_op jit(solution)/shard_map/reduce_scatter | solution.py:184
  190.6 1.6 collective-permute-start.16
  192.4 12.8 %collective-permute-start.19 = (bf16[256,256]{1,0:T(8,128)(2,1)S(1)}, bf16[256,256]{1,0:T(8,128)(2,1)S(1)}, u32[]{:S(2)}, u32[]{:S(2)}) collective-permute-start(bf16[256,256]{1,0:T(8,128)(2,1)S(1)} %bitcast.91), channel_id=1, source_target_pairs={{0,64},{32,96},{64,0},{96,32},{1,65},{33,97},{65,1},{97,33},{2,66}... | collective-permute-start | bytes 393224 | tf_op jit(solution)/shard_map/ppermute | solution.py:174
  195.6 7.0 %collective-permute-start.17 = (bf16[256,256]{1,0:T(8,128)(2,1)S(1)}, bf16[256,256]{1,0:T(8,128)(2,1)S(1)}, u32[]{:S(2)}, u32[]{:S(2)}) collective-permute-start(bf16[256,256]{1,0:T(8,128)(2,1)S(1)} %bitcast.92), channel_id=1, source_target_pairs={{0,96},{32,0},{64,32},{96,64},{1,97},{33,1},{65,33},{97,65},{2,98}... | collective-permute-start | bytes 393224 | tf_op jit(solution)/shard_map/ppermute | solution.py:174
  196.7 9.4 %collective-permute-start.18 = (bf16[256,256]{1,0:T(8,128)(2,1)S(1)}, bf16[256,256]{1,0:T(8,128)(2,1)S(1)}, u32[]{:S(2)}, u32[]{:S(2)}) collective-permute-start(bf16[256,256]{1,0:T(8,128)(2,1)S(1)} %bitcast.90), channel_id=1, source_target_pairs={{0,32},{32,64},{64,96},{96,0},{1,33},{33,65},{65,97},{97,1},{2,34}... | collective-permute-start | bytes 393224 | tf_op jit(solution)/shard_map/ppermute | solution.py:174
  (12 other events, 54.3 us)
Sparse Core Ops, SparseCore 0:
  100.9 32.3 all-gather.2
  134.9 30.8 all-gather.4
  208.7 33.4 reduce-scatter.1

commit v2 on v1

v2 whole, which is shorter than its diff:
```python
import functools
import math

import jax
import jax.numpy as jnp
from jax import lax
from jax.experimental import pallas as pl
from jax.experimental.pallas import tpu as pltpu
from jax.sharding import PartitionSpec as P

HD = 128
BLOCK = 128
NEG = -1e30
LOG2E = 1.4426950408889634
OFFSETS = (0, -1, 1, 2)
CONTRACT_LAST = (((1,), (1,)), ((), ()))


def ring(n, step):
    return [(i, (i + step) % n) for i in range(n)]


def y_ring(n, step):
    return [(i, (i + 2 * step) % n) for i in range(n)]


def core_swap(n):
    return [(i, i ^ 1) for i in range(n)]


def project_tile(x, w_ref, acc_ref, rows):
    for c in range(3):
        acc_ref[rows, c * 256 : (c + 1) * 256] += jnp.dot(
            x, w_ref[c], preferred_element_type=jnp.float32
        )


def emit_heads(acc, scale_ref, core, q_ref, kv_ref, give_ref):
    scaled = (acc * scale_ref[...]).astype(jnp.bfloat16)
    heads = [[scaled[:, c * 256 + h * HD : c * 256 + (h + 1) * HD] for c in range(3)] for h in (0, 1)]
    is_first = core == 0

    @pl.when(is_first)
    def _():
        q_ref[...] = heads[0][0]
        kv_ref[...] = jnp.concatenate(heads[0][1:], axis=1)
        give_ref[...] = jnp.concatenate(heads[1], axis=1)

    @pl.when(jnp.logical_not(is_first))
    def _():
        q_ref[...] = heads[1][0]
        kv_ref[...] = jnp.concatenate(heads[1][1:], axis=1)
        give_ref[...] = jnp.concatenate(heads[0], axis=1)


def heads_shape(rows):
    return [jax.ShapeDtypeStruct((rows, n * HD), jnp.bfloat16) for n in (1, 2, 3)]


def heads_specs(rows):
    return [pl.BlockSpec((rows, n * HD), lambda r, s: (0, 0)) for n in (1, 2, 3)]


def rows_kernel(sizes, where_ref, w_ref, scale_ref, *refs):
    xs, outs, acc_ref = refs[: len(sizes)], refs[len(sizes) : -1], refs[-1]
    r = pl.program_id(0)

    @pl.when(r == 0)
    def _():
        acc_ref[...] = jnp.zeros_like(acc_ref)

    start = 0
    for x_ref, n in zip(xs, sizes):
        project_tile(x_ref[...], w_ref, acc_ref, slice(start, start + n))
        start += n

    @pl.when(r == pl.num_programs(0) - 1)
    def _():
        emit_heads(acc_ref[...], scale_ref, where_ref[4], *outs)


def project_rows(where, w, scale, xs):
    sizes = [x.shape[0] for x in xs]
    rows, feat = sum(sizes), xs[0].shape[1] // 4
    return pl.pallas_call(
        functools.partial(rows_kernel, sizes),
        grid_spec=pltpu.PrefetchScalarGridSpec(
            num_scalar_prefetch=1,
            grid=(4,),
            in_specs=[
                pl.BlockSpec((3, feat, 256), lambda r, s: (0, s[r], 0)),
                pl.BlockSpec((1, 768), lambda r, s: (0, 0)),
            ]
            + [pl.BlockSpec((n, feat), lambda r, s: (0, r)) for n in sizes],
            out_specs=heads_specs(rows),
            scratch_shapes=[pltpu.VMEM((rows, 768), jnp.float32)],
        ),
        out_shape=heads_shape(rows),
        compiler_params=pltpu.CompilerParams(vmem_limit_bytes=40 << 20),
        cost_estimate=pl.CostEstimate(
            flops=2 * rows * 4 * feat * 768, bytes_accessed=w.size * 2, transcendentals=0
        ),
    )(where, w, scale, *xs)


def part_kernel(where_ref, w_ref, *refs):
    xs, acc_ref = refs[:-1], refs[-1]
    r = pl.program_id(0)

    @pl.when(r == 0)
    def _():
        acc_ref[...] = jnp.zeros_like(acc_ref)

    for i, x_ref in enumerate(xs):

        @pl.when(r == i)
        def _():
            project_tile(x_ref[...], w_ref, acc_ref, slice(None))


def project_part(where, w, xs):
    rows, feat = xs[0].shape
    return pl.pallas_call(
        part_kernel,
        grid_spec=pltpu.PrefetchScalarGridSpec(
            num_scalar_prefetch=1,
            grid=(len(xs),),
            in_specs=[pl.BlockSpec((3, feat, 256), lambda r, s: (0, s[r], 0))]
            + [pl.BlockSpec((rows, feat), lambda r, s: (0, 0)) for _ in xs],
            out_specs=pl.BlockSpec((rows, 768), lambda r, s: (0, 0)),
        ),
        out_shape=jax.ShapeDtypeStruct((rows, 768), jnp.float32),
        compiler_params=pltpu.CompilerParams(vmem_limit_bytes=40 << 20),
        cost_estimate=pl.CostEstimate(
            flops=2 * rows * len(xs) * feat * 768, bytes_accessed=6 << 20, transcendentals=0
        ),
    )(where, w, *xs)


def last_kernel(na, nb, where_ref, w_ref, scale_ref, a0, a1, b0, b1, part_ref, *refs):
    outs, acc_ref = refs[:-1], refs[-1]
    r = pl.program_id(0)

    @pl.when(r == 0)
    def _():
        acc_ref[:na] = jnp.zeros((na, 768), jnp.float32)
        acc_ref[na:] = part_ref[...]

    project_tile(a0[...], w_ref, acc_ref, slice(0, na // 2))
    project_tile(a1[...], w_ref, acc_ref, slice(na // 2, na))

    @pl.when(r == pl.num_programs(0) - 1)
    def _():
        project_tile(b0[...], w_ref, acc_ref, slice(na, na + nb // 2))
        project_tile(b1[...], w_ref, acc_ref, slice(na + nb // 2, na + nb))
        emit_heads(acc_ref[...], scale_ref, where_ref[4], *outs)


def project_last(where, w, scale, a0, a1, b0, b1, part):
    na, nb, feat = 2 * a0.shape[0], 2 * b0.shape[0], b0.shape[1]
    rows = na + nb
    fixed = lambda x: pl.BlockSpec(x.shape, lambda r, s: (0, 0))
    return pl.pallas_call(
        functools.partial(last_kernel, na, nb),
        grid_spec=pltpu.PrefetchScalarGridSpec(
            num_scalar_prefetch=1,
            grid=(4,),
            in_specs=[
                pl.BlockSpec((3, feat, 256), lambda r, s: (0, s[r], 0)),
                pl.BlockSpec((1, 768), lambda r, s: (0, 0)),
                pl.BlockSpec((na // 2, feat), lambda r, s: (0, r)),
                pl.BlockSpec((na // 2, feat), lambda r, s: (0, r)),
                fixed(b0),
                fixed(b1),
                fixed(part),
            ],
            out_specs=heads_specs(rows),
            scratch_shapes=[pltpu.VMEM((rows, 768), jnp.float32)],
        ),
        out_shape=heads_shape(rows),
        compiler_params=pltpu.CompilerParams(vmem_limit_bytes=40 << 20),
        cost_estimate=pl.CostEstimate(
            flops=2 * rows * 2 * feat * 768, bytes_accessed=w.size * 2, transcendentals=0
        ),
    )(where, w, scale, a0, a1, b0, b1, part)


def attn_kernel(bk, first_block, begin, end, q_ref, qm_ref, *refs):
    kv_refs, o_ref = refs[:-1], refs[-1]
    if not begin:
        state_ref, kv_refs = kv_refs[0], kv_refs[1:]
    rows = q_ref.shape[0]
    q = jnp.concatenate([q_ref[...], qm_ref[...]], axis=1)
    tiles = [(r, j) for r in range(len(kv_refs)) for j in range(kv_refs[r].shape[0] // bk)]
    lane = lax.broadcasted_iota(jnp.int32, (bk, HD), 1)
    inner = lax.broadcasted_iota(jnp.int32, (bk, HD), 0) // BLOCK
    ones = (lane == 0).astype(jnp.float32).astype(jnp.bfloat16)
    per_tile = bk // BLOCK

    def score(i):
        r, j = tiles[i]
        onehot = (lane == inner + (first_block + i * per_tile)).astype(jnp.float32).astype(jnp.bfloat16)
        k = jnp.concatenate([kv_refs[r][j * bk : (j + 1) * bk, :HD], onehot], axis=1)
        return lax.dot_general(q, k, CONTRACT_LAST, preferred_element_type=jnp.float32)

    if begin:
        high = jnp.full((rows, 1), -3e38, jnp.float32)
        acc = jnp.zeros((rows, 2 * HD), jnp.float32)
    else:
        acc = state_ref[...]
        high = acc[:, 2 * HD - 1 :]
    s = score(0)
    for i in range(len(tiles)):
        s_next = score(i + 1) if i + 1 < len(tiles) else None
        new_high = jnp.maximum(high, jnp.max(s, axis=1, keepdims=True))
        p = jnp.exp2(s - new_high).astype(jnp.bfloat16)
        factor = jnp.exp2(high - new_high)
        r, j = tiles[i]
        v = jnp.concatenate([kv_refs[r][j * bk : (j + 1) * bk, HD:], ones], axis=1)
        acc = acc * factor + jnp.dot(p, v, preferred_element_type=jnp.float32)
        high = new_high
        s = s_next
    if end:
        o_ref[...] = (acc[:, :HD] / acc[:, HD : HD + 1]).astype(jnp.bfloat16)
    else:
        o_ref[...] = jnp.where(lax.broadcasted_iota(jnp.int32, acc.shape, 1) == 2 * HD - 1, high, acc)


def attention(q, qm, kvs, first_block, state, end, bk, bq=512):
    rows = q.shape[0]
    keys = sum(kv.shape[0] for kv in kvs)
    begin = state is None
    row_block = lambda n: pl.BlockSpec((bq, n), lambda i: (i, 0))
    return pl.pallas_call(
        functools.partial(attn_kernel, bk, first_block, begin, end),
        grid=(rows // bq,),
        in_specs=[row_block(HD), row_block(HD)]
        + ([] if begin else [row_block(2 * HD)])
        + [pl.BlockSpec(kv.shape, lambda i: (0, 0)) for kv in kvs],
        out_specs=row_block(HD if end else 2 * HD),
        out_shape=jax.ShapeDtypeStruct((rows, HD), jnp.bfloat16)
        if end
        else jax.ShapeDtypeStruct((rows, 2 * HD), jnp.float32),
        compiler_params=pltpu.CompilerParams(vmem_limit_bytes=40 << 20),
        cost_estimate=pl.CostEstimate(
            flops=8 * rows * keys * HD, bytes_accessed=keys * 512, transcendentals=rows * keys
        ),
    )(*([q, qm] if begin else [q, qm, state]), *kvs)


def local(tokens, w_qkv, qkv_scale, block_mask, w_out):
    nu, nb, nt = lax.axis_size("ulysses"), lax.axis_size("blk"), lax.axis_size("tensor")
    u, b, t = lax.axis_index("ulysses"), lax.axis_index("blk"), lax.axis_index("tensor")
    y, core = b // 2, b % 2
    half = tokens.shape[0] // 2
    quarter = half // 2
    pp = lax.ppermute
    offsets = jnp.array(OFFSETS, jnp.int32)

    def direct(value, axis, n):
        return [value] + [pp(value, axis, ring(n, s)) for s in (1, -1, 2)]

    where = jnp.concatenate([(t + offsets) % nt, core[None]])
    w = jnp.transpose(w_qkv, (1, 0, 2))
    scale = qkv_scale * jnp.array([LOG2E / math.sqrt(HD), 1.0, 1.0], jnp.float32)[:, None]
    scale = jnp.repeat(scale.reshape(1, 6), HD, axis=1)

    ny = nb // 2
    groups = (u + offsets) % nu
    cores = jnp.stack([core, 1 - core])

    def block_id(yy, slot, group, odd):
        return (groups[group] * nb + 2 * (yy % ny) + cores[slot]) * 2 + odd

    early = [(g, 0) for g in range(3)]
    late = [(3, 0)] + [(g, 1) for g in range(4)]
    keys = [(y, s) + g for s in (0, 1) for g in late]
    keys += [(yy, s) + g for yy in range(ny) for s in (0, 1) for g in early]
    keys += [(y + o, s) + g for o in (-1, 1) for s in (0, 1) for g in late]
    keys += [(y + 2, s) + g for s in (0, 1) for g in late]
    key_ids = jnp.stack([block_id(*k) for k in keys])
    query_ids = jnp.stack(
        [block_id(y, s, g, odd) for s in (0, 1) for g in range(4) for odd in (0, 1)]
    )
    blocks = jnp.arange(block_mask.shape[1], dtype=jnp.int32)
    key_hot = (key_ids[:, None] == blocks[None, :]).astype(jnp.float32)
    query_hot = (query_ids[:, None] == blocks[None, :]).astype(jnp.float32)
    mask = lax.dynamic_index_in_dim(block_mask, core, 0, keepdims=False).astype(jnp.float32)
    live = query_hot @ mask @ key_hot.T > 0.5
    live = live | (query_ids[:, None] == key_ids[None, :])
    bias = jnp.where(live, 0.0, NEG).astype(jnp.bfloat16)
    bias = jnp.pad(bias, ((0, 0), (0, HD - bias.shape[1])))
    bias = jnp.repeat(bias, BLOCK, axis=0)

    a_own = jnp.concatenate(direct(tokens[:half], "tensor", nt), axis=1)
    b_own = jnp.concatenate(direct(tokens[half:], "ulysses", nu), axis=0)
    a_m = pp(a_own, "ulysses", ring(nu, 1))
    b_m = pp(b_own, "tensor", ring(nt, 1))
    a_p = pp(a_own, "ulysses", ring(nu, -1))
    b_p = pp(b_own, "tensor", ring(nt, -1))
    bh = b_own.shape[0] // 2
    a0 = pp(a_m[:quarter], "ulysses", ring(nu, 1))
    a1 = pp(a_p[quarter:], "ulysses", ring(nu, -1))
    b0 = pp(b_m[:bh], "tensor", ring(nt, 1))
    b1 = pp(b_p[bh:], "tensor", ring(nt, -1))

    q1, kv1, give1 = project_rows(where, w, scale, [a_own, a_m, a_p])
    got1 = pp(give1, "blk", core_swap(nb))
    kv1_all = lax.all_gather(
        jnp.concatenate([kv1, got1[:, HD:]], axis=0),
        "blk",
        axis=0,
        tiled=True,
        axis_index_groups=[list(range(0, nb, 2)), list(range(1, nb, 2))],
    )
    part = project_part(where, w, [b_own, b_m, b_p])
    q2, kv2, give2 = project_last(where, w, scale, a0, a1, b0, b1, part)
    got2 = pp(give2, "blk", core_swap(nb))
    kv2_own = jnp.concatenate([kv2, got2[:, HD:]], axis=0)
    kv2_m = pp(kv2_own, "blk", y_ring(nb, 1))
    kv2_p = pp(kv2_own, "blk", y_ring(nb, -1))
    kh = kv2_own.shape[0] // 2
    kv2_0 = pp(kv2_m[:kh], "blk", y_ring(nb, 1))
    kv2_1 = pp(kv2_p[kh:], "blk", y_ring(nb, -1))

    def in_order(early_q, late_q):
        e = [early_q[i * half : (i + 1) * half] for i in range(3)]
        l = [late_q[i * half : (i + 1) * half] for i in range(5)]
        e.append(l[0])
        return [x for g in range(4) for x in (e[g], l[1 + g])]

    q = jnp.concatenate(in_order(q1, q2) + in_order(got1[:, :HD], got2[:, :HD]), axis=0)

    state = attention(q, bias, [kv2_own], 0, None, False, 640)
    state = attention(q, bias, [kv1_all], 10, state, False, 768)
    state = attention(q, bias, [kv2_m, kv2_p], 34, state, False, 640)
    out = attention(q, bias, [kv2_0, kv2_1], 54, state, True, 640)

    out = out.reshape(2, nu, 2 * half, HD)
    other = pp(out[1], "blk", core_swap(nb))
    mine = out[0]
    first = jnp.where(core == 0, mine, other)
    second = jnp.where(core == 0, other, mine)
    heads = jnp.concatenate([first, second], axis=-1)
    arrived = [heads[0]] + [
        pp(heads[i], "ulysses", ring(nu, OFFSETS[i])) for i in range(1, nu)
    ]
    partial_value = sum(
        jnp.dot(
            v,
            lax.dynamic_index_in_dim(w_out, (u - o) % nu, 0, keepdims=False),
            preferred_element_type=jnp.float32,
        )
        for v, o in zip(arrived, OFFSETS)
    )
    return lax.psum_scatter(
        partial_value.astype(jnp.bfloat16), "tensor", scatter_dimension=1, tiled=True
    )


def solution(mesh):
    return jax.shard_map(
        local,
        mesh=mesh,
        in_specs=(
            P(("ulysses", "blk"), "tensor"),
            P(None, None, ("ulysses", "tensor")),
            P(None, ("ulysses", "tensor")),
            P(("ulysses", "tensor"), None, None),
            P(None, "tensor", None),
        ),
        out_specs=P(("ulysses", "blk"), "tensor"),
        check_vma=False,
    )
```

time: 250 us -> 228 us (0.912)
  waiting for transfers between devices: 119 us -> 86.1 us
  Pallas kernels: 21.5 us -> 52.9 us
  matrix products: 34.2 us -> 8.92 us
  other arithmetic: 7.24 us -> 1.21 us
  starting transfers between devices: 30.4 us -> 34.9 us
  between operations: 13.6 us -> 16.5 us
  local copies, waits for them, and re-layouts: 23.1 us -> 25.7 us
    all_gather x2 -> x1, waiting for transfers between devices: 60.7 us -> 0.01 us  [local(): lax.all_gather(jnp.concatenate([kv1, got1[:, HD:]], axis=0), 'blk', axis=...]
    pallas_call x1 -> x7, Pallas kernels: 21.5 us -> 52.9 us  [the longest x4 33.2 us: attention(): pl.pallas_call(functools.partial(attn_kernel, bk, first_block, begin, end...]
    dot_general x8 -> x0, matrix products: 25.3 us -> none  [project(): jnp.einsum('rd,dcn->rcn', value, w, preferred_element_type=jnp.float32)]
    ppermute x7 -> x11, waiting for transfers between devices: 4.32 us -> 19.5 us  [the longest x1 17.3 us: local(): kv2_p = pp(kv2_own, 'blk', y_ring(nb, -1))]
    unnamed x26 -> x49, local copies, waits for them, and re-layouts: 3.94 us -> 14.6 us
    ppermute x6, waiting for transfers between devices: 1.73 us -> 9.73 us  [direct(): return [value] + [pp(value, axis, ring(n, s)) for s in (1, -1, 2)]]
    dynamic_slice x2 -> x0, local copies, waits for them, and re-layouts: 6.12 us -> none  [the longest x1 5.93 us: local(): lax.dynamic_slice_in_dim(w_qkv, (t + o) % nt * feat, feat, 0)]
    reshape x6 -> x1, local copies, waits for them, and re-layouts: 5.28 us -> 0.08 us  [local(): scale = jnp.repeat(scale.reshape(1, 6), HD, axis=1)]
  transfers between devices with their start and end apart: 23 -> 26, of which waited for: 10 -> 9; matrix products, arithmetic and copies ran while one was open for 21% -> 9% of each run, Pallas kernels for 0% -> 20%
where the time goes in v2:
time: 228 us; the launch traced here: 226 us
  waiting for transfers between devices  86.1 us (38%)
  Pallas kernels  52.9 us (23%)
  starting transfers between devices  34.9 us (15%)
  local copies, waits for them, and re-layouts  25.7 us (11%)
  between operations  16.5 us (7%)
  matrix products  8.92 us (4%)
    reduce_scatter x1, waiting for transfers between devices, local(): lax.psum_scatter(partial_value.astype(jnp.bfloat16), 'tensor', scatter_di...  36.1 us
    pallas_call x4, Pallas kernels, attention(): pl.pallas_call(functools.partial(attn_kernel, bk, first_block, begin, end...  33.2 us
    ppermute x1, waiting for transfers between devices, local(): a_p = pp(a_own, 'ulysses', ring(nu, -1))  19.6 us
    ppermute x1, waiting for transfers between devices, local(): kv2_p = pp(kv2_own, 'blk', y_ring(nb, -1))  17.3 us
    unnamed x49, local copies, waits for them, and re-layouts  14.6 us
    ppermute x6, starting transfers between devices, direct(): return [value] + [pp(value, axis, ring(n, s)) for s in (1, -1, 2)]  11.9 us
    ppermute x6, waiting for transfers between devices, direct(): return [value] + [pp(value, axis, ring(n, s)) for s in (1, -1, 2)]  9.73 us
    dot_general x4, matrix products, local(): jnp.dot(v, lax.dynamic_index_in_dim(w_out, (u - o) % nu, 0, keepdims=Fals...  8.63 us
  transfers between devices with their start and end apart: 26, of which 9 were waited for; matrix products, arithmetic and copies ran while one was open for 9% of the time, Pallas kernels for 20%

profile of v2, /device:TPU:0, one launch (start us, length us, event | category | flops | bytes accessed | tf_op | source)
XLA Modules:
  0.0 226.1 jit_solution(9505355193397486955)
XLA Ops:
  7.7 3.2 %collective-permute-start.2 = (bf16[128,1280]{1,0:T(8,128)(2,1)S(1)}, bf16[128,1280]{1,0:T(8,128)(2,1)S(1)}, u32[]{:S(2)}, u32[]{:S(2)}) collective-permute-start(bf16[128,1280]{1,0:T(8,128)(2,1)S(1)} %get-tuple-element.18), channel_id=1, source_target_pairs={{0,2},{1,3},{2,0},{3,1},{4,6},{5,7},{6,4},{7,5},{8,10},{9,11},{10,... | collective-permute-start | bytes 983048 | tf_op jit(solution)/shard_map/ppermute | solution.py:261
  12.9 4.0 %collective-permute-start.9 = (bf16[128,1280]{1,0:T(8,128)(2,1)S(1)}, bf16[128,1280]{1,0:T(8,128)(2,1)S(1)}, u32[]{:S(2)}, u32[]{:S(2)}) collective-permute-start(bf16[128,1280]{1,0:T(8,128)(2,1)S(1)} %get-tuple-element.17), channel_id=1, source_target_pairs={{0,64},{32,96},{64,0},{96,32},{1,65},{33,97},{65,1},{97,33},{2,66}... | collective-permute-start | bytes 983048 | tf_op jit(solution)/shard_map/ppermute | solution.py:261
  21.9 4.0 %collective-permute-done.1 = bf16[128,1280]{1,0:T(8,128)(2,1)S(1)} collective-permute-done((bf16[128,1280]{1,0:T(8,128)(2,1)S(1)}, bf16[128,1280]{1,0:T(8,128)(2,1)S(1)}, u32[]{:S(2)}, u32[]{:S(2)}) %collective-permute-start.1) | collective-permute-done | bytes 327712 | tf_op jit(solution)/shard_map/ppermute | solution.py:261
  26.1 4.1 %collective-permute-start.4 = (bf16[128,5120]{1,0:T(8,128)(2,1)S(1)}, bf16[128,5120]{1,0:T(8,128)(2,1)}, u32[]{:S(2)}, u32[]{:S(2)}) collective-permute-start(bf16[128,5120]{1,0:T(8,128)(2,1)S(1)} %pad_maximum_fusion.refs_0_), channel_id=1, source_target_pairs={{0,96},{32,0},{64,32},{96,64},{1,97},{33,1},{65,33},{97,65},{2,98}... | collective-permute-start | bytes 3932168 | tf_op jit(solution)/shard_map/ppermute | solution.py:299
  30.2 3.3 %collective-permute-done.8 = bf16[128,1280]{1,0:T(8,128)(2,1)S(1)} collective-permute-done((bf16[128,1280]{1,0:T(8,128)(2,1)S(1)}, bf16[128,1280]{1,0:T(8,128)(2,1)S(1)}, u32[]{:S(2)}, u32[]{:S(2)}) %collective-permute-start.8) | collective-permute-done | bytes 327712 | tf_op jit(solution)/shard_map/ppermute | solution.py:261
  33.6 2.4 %collective-permute-start.12 = (bf16[512,1280]{1,0:T(8,128)(2,1)S(1)}, bf16[512,1280]{1,0:T(8,128)(2,1)}, u32[]{:S(2)}, u32[]{:S(2)}) collective-permute-start(bf16[512,1280]{1,0:T(8,128)(2,1)S(1)} %pad_maximum_fusion.1.refs_0_), channel_id=1, source_target_pairs={{0,3},{1,0},{2,1},{3,2},{4,7},{5,4},{6,5},{7,6},{8,11},{9,8},{10,9... | collective-permute-start | bytes 3932168 | tf_op jit(solution)/shard_map/ppermute | solution.py:300
  40.1 19.6 %collective-permute-done.4.refs_2_ = bf16[128,5120]{1,0:T(8,128)(2,1)} collective-permute-done((bf16[128,5120]{1,0:T(8,128)(2,1)S(1)}, bf16[128,5120]{1,0:T(8,128)(2,1)}, u32[]{:S(2)}, u32[]{:S(2)}) %collective-permute-start.4) | collective-permute-done | bytes 1310752 | tf_op jit(solution)/shard_map/ppermute | solution.py:299
  61.7 2.6 %collective-permute-start.6 = (bf16[64,5120]{1,0:T(8,128)(2,1)}, bf16[64,5120]{1,0:T(8,128)(2,1)S(1)}, u32[]{:S(2)}, u32[]{:S(2)}) collective-permute-start(bf16[64,5120]{1,0:T(8,128)(2,1)} %slice.233), channel_id=1, source_target_pairs={{0,96},{32,0},{64,32},{96,64},{1,97},{33,1},{65,33},{97,65},{2,98}... | collective-permute-start | bytes 1966088 | tf_op jit(solution)/shard_map/ppermute | solution.py:303
  68.3 2.5 %collective-permute-start.13 = (bf16[256,1280]{1,0:T(8,128)(2,1)}, bf16[256,1280]{1,0:T(8,128)(2,1)}, u32[]{:S(2)}, u32[]{:S(2)}) collective-permute-start(bf16[256,1280]{1,0:T(8,128)(2,1)} %slice.235), channel_id=1, source_target_pairs={{0,3},{1,0},{2,1},{3,2},{4,7},{5,4},{6,5},{7,6},{8,11},{9,8},{10,9... | collective-permute-start | bytes 1966088 | tf_op jit(solution)/shard_map/ppermute | solution.py:305
  72.8 3.2 %copy-done = bf16[5120,3,256]{2,0,1:T(8,128)(2,1)S(1)} copy-done((bf16[5120,3,256]{2,0,1:T(8,128)(2,1)S(1)}, bf16[5120,3,256]{2,0,1:T(8,128)(2,1)}, u32[]{:S(2)}) %copy-start) | copy-done | bytes 7864344
  76.0 6.3 %shard_map.73 = (bf16[384,128]{1,0:T(8,128)(2,1)S(1)}, bf16[384,256]{1,0:T(8,128)(2,1)S(1)}, bf16[384,384]{1,0:T(8,128)(2,1)S(1)}) custom-call(s32[5]{0:T(128)S(1)} %pad_add_fusion.where_ref, bf16[3,5120,256]{2,1,0:T(8,128)(2,1)S(1)} %bitcast.113, f32[1,768]{1,0:T(1,128)S(1)} %bitcast.120, bf16[128,5120]{1,0:T(8,128)(2,1)S(1)} %pad_maximum_fusion.refs_0_, ...), custom_call_target="tpu_custom_call" | custom-call | flops 3019898880 | bytes 7864320 | tf_op jit(solution)/shard_map/pallas_call | solution.py:85
  83.0 6.2 %shard_map.74.part_ref = f32[512,768]{1,0:T(8,128)S(1)} custom-call(s32[5]{0:T(128)S(1)} %pad_add_fusion.where_ref, bf16[3,5120,256]{2,1,0:T(8,128)(2,1)S(1)} %bitcast.114, bf16[512,1280]{1,0:T(8,128)(2,1)S(1)} %pad_maximum_fusion.1.refs_0_, bf16[512,1280]{1,0:T(8,128)(2,1)} %collective-permute-done.10.refs_1_, bf16[512,1280]{1,0:T(8,128)(2,1)} %collective-permute-done.12.refs_2_), custom_call_target="tpu_custom_call" | custom-call | flops 3019898880 | bytes 6291456 | tf_op jit(solution)/shard_map/pallas_call | solution.py:123
  91.0 3.2 %copy-done.1 = bf16[5120,3,256]{2,0,1:T(8,128)(2,1)S(1)} copy-done((bf16[5120,3,256]{2,0,1:T(8,128)(2,1)S(1)}, bf16[5120,3,256]{2,0,1:T(8,128)(2,1)}, u32[]{:S(2)}) %copy-start.1) | copy-done | bytes 7864344
  94.3 7.2 %shard_map.75 = (bf16[640,128]{1,0:T(8,128)(2,1)S(1)}, bf16[640,256]{1,0:T(8,128)(2,1)S(1)}, bf16[640,384]{1,0:T(8,128)(2,1)S(1)}) custom-call(s32[5]{0:T(128)S(1)} %pad_add_fusion.where_ref, bf16[3,5120,256]{2,1,0:T(8,128)(2,1)S(1)} %bitcast.115, f32[1,768]{1,0:T(1,128)S(1)} %bitcast.121, bf16[64,5120]{1,0:T(8,128)(2,1)} %collective-permute-done.5.a0, ...), custom_call_target="tpu_custom_call" | custom-call | flops 2516582400 | bytes 7864320 | tf_op jit(solution)/shard_map/pallas_call | solution.py:163
  103.7 3.1 %collective-permute-start.17 = (bf16[1280,256]{1,0:T(8,128)(2,1)S(1)}, bf16[1280,256]{1,0:T(8,128)(2,1)S(1)}, u32[]{:S(2)}, u32[]{:S(2)}) collective-permute-start(bf16[1280,256]{1,0:T(8,128)(2,1)S(1)} %pad_maximum_fusion.2.refs_0_), channel_id=1, source_target_pairs={{0,24},{4,28},{8,0},{12,4},{16,8},{20,12},{24,16},{28,20},{1,25},{... | collective-permute-start | bytes 1966088 | tf_op jit(solution)/shard_map/ppermute | solution.py:321
  108.5 4.9 %shard_map.76.refs_0_ = f32[2048,256]{1,0:T(8,128)S(1)} custom-call(bf16[2048,128]{1,0:T(8,128)(2,1)S(1)} %constant_dynamic-update-slice_fusion.q_ref, bf16[2048,128]{1,0:T(8,128)(2,1)S(1)} %bitcast.116, bf16[1280,256]{1,0:T(8,128)(2,1)S(1)} %pad_maximum_fusion.2.refs_0_), custom_call_target="tpu_custom_call" | custom-call | flops 2684354560 | bytes 655360 | tf_op jit(solution)/shard_map/pallas_call | solution.py:234
  114.7 17.3 %collective-permute-done.17.refs_2_ = bf16[1280,256]{1,0:T(8,128)(2,1)S(1)} collective-permute-done((bf16[1280,256]{1,0:T(8,128)(2,1)S(1)}, bf16[1280,256]{1,0:T(8,128)(2,1)S(1)}, u32[]{:S(2)}, u32[]{:S(2)}) %collective-permute-start.17) | collective-permute-done | bytes 655392 | tf_op jit(solution)/shard_map/ppermute | solution.py:321
  137.8 10.0 %shard_map.77.refs_0_ = f32[2048,256]{1,0:T(8,128)S(1)} custom-call(bf16[2048,128]{1,0:T(8,128)(2,1)S(1)} %constant_dynamic-update-slice_fusion.q_ref, bf16[2048,128]{1,0:T(8,128)(2,1)S(1)} %bitcast.117, f32[2048,256]{1,0:T(8,128)S(1)} %copy-done.7, bf16[3072,256]{1,0:T(8,128)(2,1)S(1)} %copy-done.5), custom_call_target="tpu_custom_call" | custom-call | flops 6442450944 | bytes 1572864 | tf_op jit(solution)/shard_map/pallas_call | solution.py:234
  147.9 9.8 %shard_map.78.refs_0_ = f32[2048,256]{1,0:T(8,128)S(1)} custom-call(bf16[2048,128]{1,0:T(8,128)(2,1)S(1)} %constant_dynamic-update-slice_fusion.q_ref, bf16[2048,128]{1,0:T(8,128)(2,1)S(1)} %bitcast.118, f32[2048,256]{1,0:T(8,128)S(1)} %shard_map.77.refs_0_, bf16[1280,256]{1,0:T(8,128)(2,1)S(1)} %collective-permute-done.16.refs_1_, ...), custom_call_target="tpu_custom_call" | custom-call | flops 5368709120 | bytes 1310720 | tf_op jit(solution)/shard_map/pallas_call | solution.py:234
  157.7 8.5 %shard_map.79 = bf16[2048,128]{1,0:T(8,128)(2,1)S(1)} custom-call(bf16[2048,128]{1,0:T(8,128)(2,1)S(1)} %constant_dynamic-update-slice_fusion.q_ref, bf16[2048,128]{1,0:T(8,128)(2,1)S(1)} %bitcast.119, f32[2048,256]{1,0:T(8,128)S(1)} %shard_map.78.refs_0_, bf16[640,256]{1,0:T(8,128)(2,1)S(1)} %collective-permute-done.18.refs_1_, ...), custom_call_target="tpu_custom_call" | custom-call | flops 2684354560 | bytes 655360 | tf_op jit(solution)/shard_map/pallas_call | solution.py:234
  173.2 2.8 %fusion.6 = f32[256,5120]{1,0:T(8,128)S(1)} fusion(bf16[4,256,5120]{2,1,0:T(8,128)(2,1)} %param.11, s32[]{:T(128)S(6)} %select_n.204, bf16[4,256,128]{2,1,0:T(8,128)(2,1)S(1)} %get-tuple-element.22, bf16[4,256,128]{2,1,0:T(8,128)(2,1)S(1)} %get-tuple-element.23), kind=kOutput, calls=%fused_computation.8 | convolution fusion | flops 671350784 | bytes 8388612 | tf_op jit(solution)/shard_map/dot_general | solution.py:349
  177.2 2.6 %convolution_add_fusion.1 = f32[256,5120]{1,0:T(8,128)S(1)} fusion(f32[256,5120]{1,0:T(8,128)S(1)} %fusion.6, bf16[256,256]{1,0:T(8,128)(2,1)S(1)} %collective-permute-done.21, bf16[4,256,5120]{2,1,0:T(8,128)(2,1)} %param.11, s32[]{:T(128)S(6)} %select_n.206), kind=kOutput, calls=%fused_computation.1 | convolution fusion | flops 672399360 | bytes 13238276 | tf_op jit(solution)/shard_map/dot_general | solution.py:349
  180.8 2.4 %fusion.1 = bf16[256,5120]{1,0:T(8,128)(2,1)} fusion(f32[256,5120]{1,0:T(8,128)S(1)} %fusion.2, f32[256,5120]{1,0:T(8,128)S(1)} %convolution_add_fusion.1, bf16[256,256]{1,0:T(8,128)(2,1)S(1)} %collective-permute-done.22, bf16[4,256,5120]{2,1,0:T(8,128)(2,1)S(1)} %bitcast.123, s32[]{:T(128)S(6)} %select_n.208), kind=kOutput, calls=%fused_computation.3 | convolution fusion | flops 675020800 | bytes 15859716 | tf_op jit(solution)/shard_map/dot_general | solution.py:349
  183.2 36.1 %reduce-scatter.2.cloned.1.call-done = bf16[256,1280]{1,0:T(8,128)(2,1)} async-done(((bf16[256,5120]{1,0:T(8,128)(2,1)}), bf16[256,1280]{1,0:T(8,128)(2,1)}) %reduce-scatter.2.cloned.1.call-update) | async-done | bytes 655376 | tf_op jit(solution)/shard_map/reduce_scatter | solution.py:356
  (119 shorter events, 40.4 us)
Async XLA Ops:
  6.5 128.3 %all-gather.2.cloned.1.call-start = ((), (), s32[]{:S(2)}) async-start(), calls=%async_computation.1 | async-start | bytes 1966080 | tf_op jit(solution)/shard_map/all_gather | solution.py:309
  7.7 12.2 %collective-permute-start.2 = (bf16[128,1280]{1,0:T(8,128)(2,1)S(1)}, bf16[128,1280]{1,0:T(8,128)(2,1)S(1)}, u32[]{:S(2)}, u32[]{:S(2)}) collective-permute-start(bf16[128,1280]{1,0:T(8,128)(2,1)S(1)} %get-tuple-element.18), channel_id=1, source_target_pairs={{0,2},{1,3},{2,0},{3,1},{4,6},{5,7},{6,4},{7,5},{8,10},{9,11},{10,... | collective-permute-start | bytes 983048 | tf_op jit(solution)/shard_map/ppermute | solution.py:261
  10.8 15.1 %collective-permute-start.1 = (bf16[128,1280]{1,0:T(8,128)(2,1)S(1)}, bf16[128,1280]{1,0:T(8,128)(2,1)S(1)}, u32[]{:S(2)}, u32[]{:S(2)}) collective-permute-start(bf16[128,1280]{1,0:T(8,128)(2,1)S(1)} %get-tuple-element.18), channel_id=1, source_target_pairs={{0,3},{1,0},{2,1},{3,2},{4,7},{5,4},{6,5},{7,6},{8,11},{9,8},{10,9... | collective-permute-start | bytes 983048 | tf_op jit(solution)/shard_map/ppermute | solution.py:261
  12.0 13.9 %collective-permute-start = (bf16[128,1280]{1,0:T(8,128)(2,1)S(1)}, bf16[128,1280]{1,0:T(8,128)(2,1)S(1)}, u32[]{:S(2)}, u32[]{:S(2)}) collective-permute-start(bf16[128,1280]{1,0:T(8,128)(2,1)S(1)} %get-tuple-element.18), channel_id=1, source_target_pairs={{0,1},{1,2},{2,3},{3,0},{4,5},{5,6},{6,7},{7,4},{8,9},{9,10},{10,1... | collective-permute-start | bytes 983048 | tf_op jit(solution)/shard_map/ppermute | solution.py:261
  12.9 17.3 %collective-permute-start.9 = (bf16[128,1280]{1,0:T(8,128)(2,1)S(1)}, bf16[128,1280]{1,0:T(8,128)(2,1)S(1)}, u32[]{:S(2)}, u32[]{:S(2)}) collective-permute-start(bf16[128,1280]{1,0:T(8,128)(2,1)S(1)} %get-tuple-element.17), channel_id=1, source_target_pairs={{0,64},{32,96},{64,0},{96,32},{1,65},{33,97},{65,1},{97,33},{2,66}... | collective-permute-start | bytes 983048 | tf_op jit(solution)/shard_map/ppermute | solution.py:261
  16.8 16.7 %collective-permute-start.8 = (bf16[128,1280]{1,0:T(8,128)(2,1)S(1)}, bf16[128,1280]{1,0:T(8,128)(2,1)S(1)}, u32[]{:S(2)}, u32[]{:S(2)}) collective-permute-start(bf16[128,1280]{1,0:T(8,128)(2,1)S(1)} %get-tuple-element.17), channel_id=1, source_target_pairs={{0,96},{32,0},{64,32},{96,64},{1,97},{33,1},{65,33},{97,65},{2,98}... | collective-permute-start | bytes 983048 | tf_op jit(solution)/shard_map/ppermute | solution.py:261
  19.9 13.6 %collective-permute-start.7 = (bf16[128,1280]{1,0:T(8,128)(2,1)S(1)}, bf16[128,1280]{1,0:T(8,128)(2,1)S(1)}, u32[]{:S(2)}, u32[]{:S(2)}) collective-permute-start(bf16[128,1280]{1,0:T(8,128)(2,1)S(1)} %get-tuple-element.17), channel_id=1, source_target_pairs={{0,32},{32,64},{64,96},{96,0},{1,33},{33,65},{65,97},{97,1},{2,34}... | collective-permute-start | bytes 983048 | tf_op jit(solution)/shard_map/ppermute | solution.py:261
  26.1 33.6 %collective-permute-start.4 = (bf16[128,5120]{1,0:T(8,128)(2,1)S(1)}, bf16[128,5120]{1,0:T(8,128)(2,1)}, u32[]{:S(2)}, u32[]{:S(2)}) collective-permute-start(bf16[128,5120]{1,0:T(8,128)(2,1)S(1)} %pad_maximum_fusion.refs_0_), channel_id=1, source_target_pairs={{0,96},{32,0},{64,32},{96,64},{1,97},{33,1},{65,33},{97,65},{2,98}... | collective-permute-start | bytes 3932168 | tf_op jit(solution)/shard_map/ppermute | solution.py:299
  30.2 34.1 %collective-permute-start.3 = (bf16[128,5120]{1,0:T(8,128)(2,1)S(1)}, bf16[128,5120]{1,0:T(8,128)(2,1)}, u32[]{:S(2)}, u32[]{:S(2)}) collective-permute-start(bf16[128,5120]{1,0:T(8,128)(2,1)S(1)} %pad_maximum_fusion.refs_0_), channel_id=1, source_target_pairs={{0,32},{32,64},{64,96},{96,0},{1,33},{33,65},{65,97},{97,1},{2,34}... | collective-permute-start | bytes 3932168 | tf_op jit(solution)/shard_map/ppermute | solution.py:297
  33.6 32.7 %collective-permute-start.12 = (bf16[512,1280]{1,0:T(8,128)(2,1)S(1)}, bf16[512,1280]{1,0:T(8,128)(2,1)}, u32[]{:S(2)}, u32[]{:S(2)}) collective-permute-start(bf16[512,1280]{1,0:T(8,128)(2,1)S(1)} %pad_maximum_fusion.1.refs_0_), channel_id=1, source_target_pairs={{0,3},{1,0},{2,1},{3,2},{4,7},{5,4},{6,5},{7,6},{8,11},{9,8},{10,9... | collective-permute-start | bytes 3932168 | tf_op jit(solution)/shard_map/ppermute | solution.py:300
  36.0 34.8 %collective-permute-start.10 = (bf16[512,1280]{1,0:T(8,128)(2,1)S(1)}, bf16[512,1280]{1,0:T(8,128)(2,1)}, u32[]{:S(2)}, u32[]{:S(2)}) collective-permute-start(bf16[512,1280]{1,0:T(8,128)(2,1)S(1)} %pad_maximum_fusion.1.refs_0_), channel_id=1, source_target_pairs={{0,1},{1,2},{2,3},{3,0},{4,5},{5,6},{6,7},{7,4},{8,9},{9,10},{10,1... | collective-permute-start | bytes 3932168 | tf_op jit(solution)/shard_map/ppermute | solution.py:298
  61.7 29.3 %collective-permute-start.6 = (bf16[64,5120]{1,0:T(8,128)(2,1)}, bf16[64,5120]{1,0:T(8,128)(2,1)S(1)}, u32[]{:S(2)}, u32[]{:S(2)}) collective-permute-start(bf16[64,5120]{1,0:T(8,128)(2,1)} %slice.233), channel_id=1, source_target_pairs={{0,96},{32,0},{64,32},{96,64},{1,97},{33,1},{65,33},{97,65},{2,98}... | collective-permute-start | bytes 1966088 | tf_op jit(solution)/shard_map/ppermute | solution.py:303
  66.2 24.7 %collective-permute-start.5 = (bf16[64,5120]{1,0:T(8,128)(2,1)}, bf16[64,5120]{1,0:T(8,128)(2,1)}, u32[]{:S(2)}, u32[]{:S(2)}) collective-permute-start(bf16[64,5120]{1,0:T(8,128)(2,1)} %slice.232), channel_id=1, source_target_pairs={{0,32},{32,64},{64,96},{96,0},{1,33},{33,65},{65,97},{97,1},{2,34}... | collective-permute-start | bytes 1966088 | tf_op jit(solution)/shard_map/ppermute | solution.py:302
  68.3 22.7 %collective-permute-start.13 = (bf16[256,1280]{1,0:T(8,128)(2,1)}, bf16[256,1280]{1,0:T(8,128)(2,1)}, u32[]{:S(2)}, u32[]{:S(2)}) collective-permute-start(bf16[256,1280]{1,0:T(8,128)(2,1)} %slice.235), channel_id=1, source_target_pairs={{0,3},{1,0},{2,1},{3,2},{4,7},{5,4},{6,5},{7,6},{8,11},{9,8},{10,9... | collective-permute-start | bytes 1966088 | tf_op jit(solution)/shard_map/ppermute | solution.py:305
  72.8 18.2 %collective-permute-start.11 = (bf16[256,1280]{1,0:T(8,128)(2,1)}, bf16[256,1280]{1,0:T(8,128)(2,1)}, u32[]{:S(2)}, u32[]{:S(2)}) collective-permute-start(bf16[256,1280]{1,0:T(8,128)(2,1)} %slice.234), channel_id=1, source_target_pairs={{0,1},{1,2},{2,3},{3,0},{4,5},{5,6},{6,7},{7,4},{8,9},{9,10},{10,1... | collective-permute-start | bytes 1966088 | tf_op jit(solution)/shard_map/ppermute | solution.py:304
  82.3 6.9 %collective-permute-start.14 = (bf16[384,384]{1,0:T(8,128)(2,1)S(1)}, bf16[384,384]{1,0:T(8,128)(2,1)S(1)}, u32[]{:S(2)}, u32[]{:S(2)}) collective-permute-start(bf16[384,384]{1,0:T(8,128)(2,1)S(1)} %get-tuple-element.13), channel_id=1, source_target_pairs={{0,4},{4,0},{8,12},{12,8},{16,20},{20,16},{24,28},{28,24},{1,5},{5... | collective-permute-start | bytes 884744 | tf_op jit(solution)/shard_map/ppermute | solution.py:308
  90.7 128.5 %reduce-scatter.2.cloned.1.call-start = ((), (), s32[]{:S(2)}) async-start(), calls=%async_computation.2 | async-start | bytes 3276800 | tf_op jit(solution)/shard_map/reduce_scatter | solution.py:356
  103.7 28.3 %collective-permute-start.17 = (bf16[1280,256]{1,0:T(8,128)(2,1)S(1)}, bf16[1280,256]{1,0:T(8,128)(2,1)S(1)}, u32[]{:S(2)}, u32[]{:S(2)}) collective-permute-start(bf16[1280,256]{1,0:T(8,128)(2,1)S(1)} %pad_maximum_fusion.2.refs_0_), channel_id=1, source_target_pairs={{0,24},{4,28},{8,0},{12,4},{16,8},{20,12},{24,16},{28,20},{1,25},{... | collective-permute-start | bytes 1966088 | tf_op jit(solution)/shard_map/ppermute | solution.py:321
  106.8 26.8 %collective-permute-start.16 = (bf16[1280,256]{1,0:T(8,128)(2,1)S(1)}, bf16[1280,256]{1,0:T(8,128)(2,1)S(1)}, u32[]{:S(2)}, u32[]{:S(2)}) collective-permute-start(bf16[1280,256]{1,0:T(8,128)(2,1)S(1)} %pad_maximum_fusion.2.refs_0_), channel_id=1, source_target_pairs={{0,8},{4,12},{8,16},{12,20},{16,24},{20,28},{24,0},{28,4},{1,9},{5... | collective-permute-start | bytes 1966088 | tf_op jit(solution)/shard_map/ppermute | solution.py:320
  132.0 25.7 %collective-permute-start.19 = (bf16[640,256]{1,0:T(8,128)(2,1)S(1)}, bf16[640,256]{1,0:T(8,128)(2,1)S(1)}, u32[]{:S(2)}, u32[]{:S(2)}) collective-permute-start(bf16[640,256]{1,0:T(8,128)(2,1)S(1)} %slice.247), channel_id=1, source_target_pairs={{0,24},{4,28},{8,0},{12,4},{16,8},{20,12},{24,16},{28,20},{1,25},{... | collective-permute-start | bytes 983048 | tf_op jit(solution)/shard_map/ppermute | solution.py:324
  134.3 23.4 %collective-permute-start.18 = (bf16[640,256]{1,0:T(8,128)(2,1)}, bf16[640,256]{1,0:T(8,128)(2,1)S(1)}, u32[]{:S(2)}, u32[]{:S(2)}) collective-permute-start(bf16[640,256]{1,0:T(8,128)(2,1)} %slice.246), channel_id=1, source_target_pairs={{0,8},{4,12},{8,16},{12,20},{16,24},{20,28},{24,0},{28,4},{1,9},{5... | collective-permute-start | bytes 983048 | tf_op jit(solution)/shard_map/ppermute | solution.py:323
  168.2 12.5 %collective-permute-start.22 = (bf16[256,256]{1,0:T(8,128)(2,1)S(1)}, bf16[256,256]{1,0:T(8,128)(2,1)S(1)}, u32[]{:S(2)}, u32[]{:S(2)}) collective-permute-start(bf16[256,256]{1,0:T(8,128)(2,1)S(1)} %get-tuple-element.19), channel_id=1, source_target_pairs={{0,32},{32,64},{64,96},{96,0},{1,33},{33,65},{65,97},{97,1},{2,34}... | collective-permute-start | bytes 393224 | tf_op jit(solution)/shard_map/ppermute | solution.py:346
  169.6 7.6 %collective-permute-start.21 = (bf16[256,256]{1,0:T(8,128)(2,1)S(1)}, bf16[256,256]{1,0:T(8,128)(2,1)S(1)}, u32[]{:S(2)}, u32[]{:S(2)}) collective-permute-start(bf16[256,256]{1,0:T(8,128)(2,1)S(1)} %get-tuple-element.20), channel_id=1, source_target_pairs={{0,96},{32,0},{64,32},{96,64},{1,97},{33,1},{65,33},{97,65},{2,98}... | collective-permute-start | bytes 393224 | tf_op jit(solution)/shard_map/ppermute | solution.py:346
  171.6 8.3 %collective-permute-start.23 = (bf16[256,256]{1,0:T(8,128)(2,1)S(1)}, bf16[256,256]{1,0:T(8,128)(2,1)S(1)}, u32[]{:S(2)}, u32[]{:S(2)}) collective-permute-start(bf16[256,256]{1,0:T(8,128)(2,1)S(1)} %get-tuple-element.21), channel_id=1, source_target_pairs={{0,64},{32,96},{64,0},{96,32},{1,65},{33,97},{65,1},{97,33},{2,66}... | collective-permute-start | bytes 393224 | tf_op jit(solution)/shard_map/ppermute | solution.py:346
  (18 other events, 164.2 us)
Sparse Core Ops, SparseCore 0:
  90.9 38.7 all-gather.1
  183.3 35.8 reduce-scatter.1

commit v3 on v2

--- a/solution.py
+++ b/solution.py
@@ -28,13 +28,6 @@
     return [(i, i ^ 1) for i in range(n)]
 
 
-def project_tile(x, w_ref, acc_ref, rows):
-    for c in range(3):
-        acc_ref[rows, c * 256 : (c + 1) * 256] += jnp.dot(
-            x, w_ref[c], preferred_element_type=jnp.float32
-        )
-
-
 def emit_heads(acc, scale_ref, core, q_ref, kv_ref, give_ref):
     scaled = (acc * scale_ref[...]).astype(jnp.bfloat16)
     heads = [[scaled[:, c * 256 + h * HD : c * 256 + (h + 1) * HD] for c in range(3)] for h in (0, 1)]
@@ -57,132 +50,141 @@
     return [jax.ShapeDtypeStruct((rows, n * HD), jnp.bfloat16) for n in (1, 2, 3)]
 
 
-def heads_specs(rows):
-    return [pl.BlockSpec((rows, n * HD), lambda r, s: (0, 0)) for n in (1, 2, 3)]
-
-
-def rows_kernel(sizes, where_ref, w_ref, scale_ref, *refs):
-    xs, outs, acc_ref = refs[: len(sizes)], refs[len(sizes) : -1], refs[-1]
-    r = pl.program_id(0)
-
-    @pl.when(r == 0)
-    def _():
-        acc_ref[...] = jnp.zeros_like(acc_ref)
-
-    start = 0
-    for x_ref, n in zip(xs, sizes):
-        project_tile(x_ref[...], w_ref, acc_ref, slice(start, start + n))
-        start += n
-
-    @pl.when(r == pl.num_programs(0) - 1)
-    def _():
-        emit_heads(acc_ref[...], scale_ref, where_ref[4], *outs)
-
-
-def project_rows(where, w, scale, xs):
-    sizes = [x.shape[0] for x in xs]
-    rows, feat = sum(sizes), xs[0].shape[1] // 4
+def start_weights(where_ref, w_hbm, w_buf, sems):
+    feat = w_buf.shape[2]
+    copies = []
+    for i in range(4):
+        rows = pl.ds(pl.multiple_of(where_ref[i] * feat, feat), feat)
+        copies.append(pltpu.make_async_copy(w_hbm.at[:, rows, :], w_buf.at[i], sems.at[i]))
+        copies[-1].start()
+    return copies
+
+
+def early_kernel(where_ref, w_hbm, scale_ref, *refs):
+    a_refs, b_refs = refs[:3], refs[3:6]
+    q_ref, kv_ref, give_ref, part_ref, acc_ref, w_buf, sems = refs[6:]
+    copies = start_weights(where_ref, w_hbm, w_buf, sems)
+    na = a_refs[0].shape[0] // 4
+    for i in range(4):
+        copies[i].wait()
+        rows = pl.ds(pl.multiple_of(where_ref[i] * na, na), na)
+        x = [a_ref[rows, :] for a_ref in a_refs]
+        if i < 3:
+            x.append(b_refs[i][...])
+        x = jnp.concatenate(x, axis=0)
+        n = x.shape[0]
+        for c in range(3):
+            cols = slice(c * 256, (c + 1) * 256)
+            d = jnp.dot(x, w_buf[i, c], preferred_element_type=jnp.float32)
+            acc_ref[:n, cols] = d if i == 0 else acc_ref[:n, cols] + d
+    emit_heads(acc_ref[: 3 * na], scale_ref, where_ref[4], q_ref, kv_ref, give_ref)
+    part_ref[...] = acc_ref[3 * na :]
+
+
+def last_kernel(where_ref, w_hbm, scale_ref, a0, a1, b0, b1, part_ref, q_ref, kv_ref, give_ref, acc_ref, xa_ref, w_buf, sems):
+    copies = start_weights(where_ref, w_hbm, w_buf, sems)
+    ha = a0.shape[0]
+    na = ha // 2
+    xa_ref[:ha] = a0[...]
+    xa_ref[ha:] = a1[...]
+    for i in range(4):
+        copies[i].wait()
+        x = xa_ref[pl.ds(pl.multiple_of(where_ref[i] * na, na), na), :]
+        for c in range(3):
+            cols = slice(c * 256, (c + 1) * 256)
+            if i < 3:
+                d = jnp.dot(x, w_buf[i, c], preferred_element_type=jnp.float32)
+                acc_ref[:na, cols] = d if i == 0 else acc_ref[:na, cols] + d
+            else:
+                x_all = jnp.concatenate([x, b0[...], b1[...]], axis=0)
+                d = jnp.dot(x_all, w_buf[i, c], preferred_element_type=jnp.float32)
+                acc_ref[:na, cols] = acc_ref[:na, cols] + d[:na]
+                acc_ref[na:, cols] = part_ref[:, cols] + d[na:]
+    emit_heads(acc_ref[...], scale_ref, where_ref[4], q_ref, kv_ref, give_ref)
+
+
+VM = pl.BlockSpec(memory_space=pltpu.VMEM)
+FIXED = [pl.BlockSpec(memory_space=pltpu.SMEM), pl.BlockSpec(memory_space=pltpu.HBM), VM]
+
+
+def weight_scratch(w):
+    return [
+        pltpu.VMEM((4, 3, w.shape[1] // 4, w.shape[2]), jnp.bfloat16),
+        pltpu.SemaphoreType.DMA((4,)),
+    ]
+
+
+def project_early(where, w, scale, a_parts, b_parts):
+    na, nb = a_parts[0].shape[0] // 4, b_parts[0].shape[0]
     return pl.pallas_call(
-        functools.partial(rows_kernel, sizes),
+        early_kernel,
+        in_specs=FIXED + [VM] * 6,
+        out_specs=[VM] * 4,
+        out_shape=heads_shape(3 * na) + [jax.ShapeDtypeStruct((nb, 768), jnp.float32)],
+        scratch_shapes=[pltpu.VMEM((3 * na + nb, 768), jnp.float32)] + weight_scratch(w),
+        compiler_params=pltpu.CompilerParams(vmem_limit_bytes=52 << 20),
+        cost_estimate=pl.CostEstimate(
+            flops=2 * 768 * (3 * na * w.shape[1] + nb * w.shape[1] * 3 // 4), bytes_accessed=w.size * 2, transcendentals=0
+        ),
+    )(where, w, scale, *a_parts, *b_parts)
+
+
+def project_last(where, w, scale, a0, a1, b0, b1, part):
+    na, nb, feat = a0.shape[0] // 2, part.shape[0], a0.shape[1]
+    return pl.pallas_call(
+        last_kernel,
+        in_specs=FIXED + [VM] * 5,
+        out_specs=[VM] * 3,
+        out_shape=heads_shape(na + nb),
+        scratch_shapes=[pltpu.VMEM((na + nb, 768), jnp.float32), pltpu.VMEM((4 * na, feat), jnp.bfloat16)]
+        + weight_scratch(w),
+        compiler_params=pltpu.CompilerParams(vmem_limit_bytes=56 << 20),
+        cost_estimate=pl.CostEstimate(
+            flops=2 * 768 * (na * w.shape[1] + nb * feat), bytes_accessed=w.size * 2, transcendentals=0
+        ),
+    )(where, w, scale, a0, a1, b0, b1, part)
+
+
+def out_kernel(where_ref, *refs):
+    xs, w_ref, o_ref = refs[:4], refs[4], refs[5]
+    k = pl.program_id(1)
+    for i, x_ref in enumerate(xs):
+
+        @pl.when(k == i)
+        def _():
+            d = jnp.dot(x_ref[...], w_ref[0], preferred_element_type=jnp.float32)
+            if i == 0:
+                o_ref[...] = d
+            else:
+                o_ref[...] += d
+
+
+def out_project(where, xs, w_out, places):
+    rows, cols = xs[0].shape[0], w_out.shape[2] // 4
+    n = len(places)
+    first = places[0]
+    step = places[1] - first if n > 1 else 0
+    return pl.pallas_call(
+        out_kernel,
         grid_spec=pltpu.PrefetchScalarGridSpec(
             num_scalar_prefetch=1,
-            grid=(4,),
-            in_specs=[
-                pl.BlockSpec((3, feat, 256), lambda r, s: (0, s[r], 0)),
-                pl.BlockSpec((1, 768), lambda r, s: (0, 0)),
-            ]
-            + [pl.BlockSpec((n, feat), lambda r, s: (0, r)) for n in sizes],
-            out_specs=heads_specs(rows),
-            scratch_shapes=[pltpu.VMEM((rows, 768), jnp.float32)],
-        ),
-        out_shape=heads_shape(rows),
-        compiler_params=pltpu.CompilerParams(vmem_limit_bytes=40 << 20),
+            grid=(n, 4),
+            in_specs=[pl.BlockSpec(x.shape, lambda r, k, s: (0, 0)) for x in xs]
+            + [
+                pl.BlockSpec(
+                    (1, w_out.shape[1], cols), lambda r, k, s: (s[5 + k], 0, s[first + step * r])
+                )
+            ],
+            out_specs=pl.BlockSpec((rows, cols), lambda r, k, s: (r, 0)),
+        ),
+        out_shape=jax.ShapeDtypeStruct((n * rows, cols), jnp.float32),
+        compiler_params=pltpu.CompilerParams(vmem_limit_bytes=56 << 20),
         cost_estimate=pl.CostEstimate(
-            flops=2 * rows * 4 * feat * 768, bytes_accessed=w.size * 2, transcendentals=0
-        ),
-    )(where, w, scale, *xs)
-
-
-def part_kernel(where_ref, w_ref, *refs):
-    xs, acc_ref = refs[:-1], refs[-1]
-    r = pl.program_id(0)
-
-    @pl.when(r == 0)
-    def _():
-        acc_ref[...] = jnp.zeros_like(acc_ref)
-
-    for i, x_ref in enumerate(xs):
-
-        @pl.when(r == i)
-        def _():
-            project_tile(x_ref[...], w_ref, acc_ref, slice(None))
-
-
-def project_part(where, w, xs):
-    rows, feat = xs[0].shape
-    return pl.pallas_call(
-        part_kernel,
-        grid_spec=pltpu.PrefetchScalarGridSpec(
-            num_scalar_prefetch=1,
-            grid=(len(xs),),
-            in_specs=[pl.BlockSpec((3, feat, 256), lambda r, s: (0, s[r], 0))]
-            + [pl.BlockSpec((rows, feat), lambda r, s: (0, 0)) for _ in xs],
-            out_specs=pl.BlockSpec((rows, 768), lambda r, s: (0, 0)),
-        ),
-        out_shape=jax.ShapeDtypeStruct((rows, 768), jnp.float32),
-        compiler_params=pltpu.CompilerParams(vmem_limit_bytes=40 << 20),
-        cost_estimate=pl.CostEstimate(
-            flops=2 * rows * len(xs) * feat * 768, bytes_accessed=6 << 20, transcendentals=0
-        ),
-    )(where, w, *xs)
-
-
-def last_kernel(na, nb, where_ref, w_ref, scale_ref, a0, a1, b0, b1, part_ref, *refs):
-    outs, acc_ref = refs[:-1], refs[-1]
-    r = pl.program_id(0)
-
-    @pl.when(r == 0)
-    def _():
-        acc_ref[:na] = jnp.zeros((na, 768), jnp.float32)
-        acc_ref[na:] = part_ref[...]
-
-    project_tile(a0[...], w_ref, acc_ref, slice(0, na // 2))
-    project_tile(a1[...], w_ref, acc_ref, slice(na // 2, na))
-
-    @pl.when(r == pl.num_programs(0) - 1)
-    def _():
-        project_tile(b0[...], w_ref, acc_ref, slice(na, na + nb // 2))
-        project_tile(b1[...], w_ref, acc_ref, slice(na + nb // 2, na + nb))
-        emit_heads(acc_ref[...], scale_ref, where_ref[4], *outs)
-
-
-def project_last(where, w, scale, a0, a1, b0, b1, part):
-    na, nb, feat = 2 * a0.shape[0], 2 * b0.shape[0], b0.shape[1]
-    rows = na + nb
-    fixed = lambda x: pl.BlockSpec(x.shape, lambda r, s: (0, 0))
-    return pl.pallas_call(
-        functools.partial(last_kernel, na, nb),
-        grid_spec=pltpu.PrefetchScalarGridSpec(
-            num_scalar_prefetch=1,
-            grid=(4,),
-            in_specs=[
-                pl.BlockSpec((3, feat, 256), lambda r, s: (0, s[r], 0)),
-                pl.BlockSpec((1, 768), lambda r, s: (0, 0)),
-                pl.BlockSpec((na // 2, feat), lambda r, s: (0, r)),
-                pl.BlockSpec((na // 2, feat), lambda r, s: (0, r)),
-                fixed(b0),
-                fixed(b1),
-                fixed(part),
-            ],
-            out_specs=heads_specs(rows),
-            scratch_shapes=[pltpu.VMEM((rows, 768), jnp.float32)],
-        ),
-        out_shape=heads_shape(rows),
-        compiler_params=pltpu.CompilerParams(vmem_limit_bytes=40 << 20),
-        cost_estimate=pl.CostEstimate(
-            flops=2 * rows * 2 * feat * 768, bytes_accessed=w.size * 2, transcendentals=0
-        ),
-    )(where, w, scale, a0, a1, b0, b1, part)
+            flops=2 * n * rows * 4 * w_out.shape[1] * cols,
+            bytes_accessed=n * 8 * w_out.shape[1] * cols,
+            transcendentals=0,
+        ),
+    )(where, *xs, w_out)
 
 
 def attn_kernel(bk, first_block, begin, end, q_ref, qm_ref, *refs):
@@ -241,7 +243,7 @@
         out_shape=jax.ShapeDtypeStruct((rows, HD), jnp.bfloat16)
         if end
         else jax.ShapeDtypeStruct((rows, 2 * HD), jnp.float32),
-        compiler_params=pltpu.CompilerParams(vmem_limit_bytes=40 << 20),
+        compiler_params=pltpu.CompilerParams(vmem_limit_bytes=24 << 20),
         cost_estimate=pl.CostEstimate(
             flops=8 * rows * keys * HD, bytes_accessed=keys * 512, transcendentals=rows * keys
         ),
@@ -260,7 +262,7 @@
     def direct(value, axis, n):
         return [value] + [pp(value, axis, ring(n, s)) for s in (1, -1, 2)]
 
-    where = jnp.concatenate([(t + offsets) % nt, core[None]])
+    where = jnp.concatenate([(t + offsets) % nt, core[None], (u - offsets) % nu])
     w = jnp.transpose(w_qkv, (1, 0, 2))
     scale = qkv_scale * jnp.array([LOG2E / math.sqrt(HD), 1.0, 1.0], jnp.float32)[:, None]
     scale = jnp.repeat(scale.reshape(1, 6), HD, axis=1)
@@ -292,19 +294,19 @@
     bias = jnp.pad(bias, ((0, 0), (0, HD - bias.shape[1])))
     bias = jnp.repeat(bias, BLOCK, axis=0)
 
-    a_own = jnp.concatenate(direct(tokens[:half], "tensor", nt), axis=1)
+    a_own = lax.all_gather(tokens[:half], "tensor", axis=0, tiled=True)
     b_own = jnp.concatenate(direct(tokens[half:], "ulysses", nu), axis=0)
     a_m = pp(a_own, "ulysses", ring(nu, 1))
     b_m = pp(b_own, "tensor", ring(nt, 1))
     a_p = pp(a_own, "ulysses", ring(nu, -1))
     b_p = pp(b_own, "tensor", ring(nt, -1))
-    bh = b_own.shape[0] // 2
-    a0 = pp(a_m[:quarter], "ulysses", ring(nu, 1))
-    a1 = pp(a_p[quarter:], "ulysses", ring(nu, -1))
+    ah, bh = a_own.shape[0] // 2, b_own.shape[0] // 2
+    a0 = pp(a_m[:ah], "ulysses", ring(nu, 1))
+    a1 = pp(a_p[ah:], "ulysses", ring(nu, -1))
     b0 = pp(b_m[:bh], "tensor", ring(nt, 1))
     b1 = pp(b_p[bh:], "tensor", ring(nt, -1))
 
-    q1, kv1, give1 = project_rows(where, w, scale, [a_own, a_m, a_p])
+    q1, kv1, give1, part = project_early(where, w, scale, [a_own, a_m, a_p], [b_own, b_m, b_p])
     got1 = pp(give1, "blk", core_swap(nb))
     kv1_all = lax.all_gather(
         jnp.concatenate([kv1, got1[:, HD:]], axis=0),
@@ -313,7 +315,6 @@
         tiled=True,
         axis_index_groups=[list(range(0, nb, 2)), list(range(1, nb, 2))],
     )
-    part = project_part(where, w, [b_own, b_m, b_p])
     q2, kv2, give2 = project_last(where, w, scale, a0, a1, b0, b1, part)
     got2 = pp(give2, "blk", core_swap(nb))
     kv2_own = jnp.concatenate([kv2, got2[:, HD:]], axis=0)
@@ -345,17 +346,20 @@
     arrived = [heads[0]] + [
         pp(heads[i], "ulysses", ring(nu, OFFSETS[i])) for i in range(1, nu)
     ]
-    partial_value = sum(
-        jnp.dot(
-            v,
-            lax.dynamic_index_in_dim(w_out, (u - o) % nu, 0, keepdims=False),
-            preferred_element_type=jnp.float32,
-        )
-        for v, o in zip(arrived, OFFSETS)
-    )
-    return lax.psum_scatter(
-        partial_value.astype(jnp.bfloat16), "tensor", scatter_dimension=1, tiled=True
-    )
+    bf = jnp.bfloat16
+    far = out_project(where, arrived, w_out, (3,)).astype(bf)
+    rows = far.shape[0]
+    hr = rows // 2
+    far_m = pp(far[:hr], "tensor", ring(nt, 1))
+    far_p = pp(far[hr:], "tensor", ring(nt, -1))
+    near = out_project(where, arrived, w_out, (1, 2))
+    to_m, to_p = near[:rows], near[rows:]
+    to_p = jnp.concatenate([to_p[:hr] + far_m.astype(jnp.float32), to_p[hr:]], axis=0).astype(bf)
+    to_m = jnp.concatenate([to_m[:hr], to_m[hr:] + far_p.astype(jnp.float32)], axis=0).astype(bf)
+    from_m = pp(to_p, "tensor", ring(nt, 1))
+    from_p = pp(to_m, "tensor", ring(nt, -1))
+    own = out_project(where, arrived, w_out, (0,))
+    return (own + from_m.astype(jnp.float32) + from_p.astype(jnp.float32)).astype(bf)
 
 
 def solution(mesh):

time: 228 us -> 234 us (1.026)
  Pallas kernels: 52.9 us -> 76.2 us
  waiting for transfers between devices: 86.1 us -> 74.7 us
  matrix products: 8.92 us -> 0.3 us
  local copies, waits for them, and re-layouts: 25.7 us -> 18.8 us
  other arithmetic: 1.21 us -> 7.76 us
  starting transfers between devices: 34.9 us -> 38.7 us
    reduce_scatter x1 -> x0, waiting for transfers between devices: 36.1 us -> none  [local(): lax.psum_scatter(partial_value.astype(jnp.bfloat16), 'tensor', scatter_di...]
    pallas_call x3 -> x5, Pallas kernels: 19.6 us -> 43 us  [the longest x3 19.3 us: out_project(): pl.pallas_call(out_kernel, grid_spec=pltpu.PrefetchScalarGridSpec(num_sca...]
    ppermute x1, waiting for transfers between devices: 19.6 us -> 0.01 us  [local(): a_p = pp(a_own, 'ulysses', ring(nu, -1))]
    ppermute x1, waiting for transfers between devices: 17.3 us -> 0.01 us  [local(): kv2_p = pp(kv2_own, 'blk', y_ring(nb, -1))]
    ppermute x1, waiting for transfers between devices: 0.01 us -> 17.1 us  [local(): kv2_m = pp(kv2_own, 'blk', y_ring(nb, 1))]
    ppermute x1, waiting for transfers between devices: 0.01 us -> 14.8 us  [local(): b_p = pp(b_own, 'tensor', ring(nt, -1))]
    dot_general x4 -> x0, matrix products: 8.63 us -> none  [local(): jnp.dot(v, lax.dynamic_index_in_dim(w_out, (u - o) % nu, 0, keepdims=Fals...]
    all_gather x0 -> x1, waiting for transfers between devices: none -> 8.11 us  [local(): a_own = lax.all_gather(tokens[:half], 'tensor', axis=0, tiled=True)]
  transfers between devices with their start and end apart: 26 -> 27, of which waited for: 9 -> 12; matrix products, arithmetic and copies ran while one was open for 9% -> 6% of each run, Pallas kernels for 20% -> 27%
where the time goes in v3:
time: 234 us; the launch traced here: 233 us
  Pallas kernels  76.2 us (33%)
  waiting for transfers between devices  74.7 us (32%)
  starting transfers between devices  38.7 us (17%)
  local copies, waits for them, and re-layouts  18.8 us (8%)
  between operations  16.6 us (7%)
  other arithmetic  7.76 us (3%)
    pallas_call x4, Pallas kernels, attention(): pl.pallas_call(functools.partial(attn_kernel, bk, first_block, begin, end...  33.2 us
    pallas_call x3, Pallas kernels, out_project(): pl.pallas_call(out_kernel, grid_spec=pltpu.PrefetchScalarGridSpec(num_sca...  19.3 us
    ppermute x1, waiting for transfers between devices, local(): kv2_m = pp(kv2_own, 'blk', y_ring(nb, 1))  17.1 us
    pallas_call x1, Pallas kernels, project_early(): pl.pallas_call(early_kernel, in_specs=FIXED + [VM] * 6, out_specs=[VM] *...  15.4 us
    ppermute x1, waiting for transfers between devices, local(): b_p = pp(b_own, 'tensor', ring(nt, -1))  14.8 us
    ppermute x3, waiting for transfers between devices, direct(): return [value] + [pp(value, axis, ring(n, s)) for s in (1, -1, 2)]  14 us
    unnamed x51, local copies, waits for them, and re-layouts  9.52 us
    pallas_call x1, Pallas kernels, project_last(): pl.pallas_call(last_kernel, in_specs=FIXED + [VM] * 5, out_specs=[VM] * 3...  8.31 us
  transfers between devices with their start and end apart: 27, of which 12 were waited for; matrix products, arithmetic and copies ran while one was open for 6% of the time, Pallas kernels for 27%

profile of v3, /device:TPU:0, one launch (start us, length us, event | category | flops | bytes accessed | tf_op | source)
XLA Modules:
  0.0 233.1 jit_solution(18158407977442335478)
XLA Ops:
  14.6 5.8 %collective-permute-done.2 = bf16[128,1280]{1,0:T(8,128)(2,1)S(1)} collective-permute-done((bf16[128,1280]{1,0:T(8,128)(2,1)S(1)}, bf16[128,1280]{1,0:T(8,128)(2,1)S(1)}, u32[]{:S(2)}, u32[]{:S(2)}) %collective-permute-start.2) | collective-permute-done | bytes 327712 | tf_op jit(solution)/shard_map/ppermute | solution.py:263
  20.4 6.4 %collective-permute-done.3 = bf16[128,1280]{1,0:T(8,128)(2,1)S(1)} collective-permute-done((bf16[128,1280]{1,0:T(8,128)(2,1)S(1)}, bf16[128,1280]{1,0:T(8,128)(2,1)S(1)}, u32[]{:S(2)}, u32[]{:S(2)}) %collective-permute-start.3) | collective-permute-done | bytes 327712 | tf_op jit(solution)/shard_map/ppermute | solution.py:263
  28.7 2.8 %collective-permute-start.6 = (bf16[512,1280]{1,0:T(8,128)(2,1)S(1)}, bf16[512,1280]{1,0:T(8,128)(2,1)}, u32[]{:S(2)}, u32[]{:S(2)}) collective-permute-start(bf16[512,1280]{1,0:T(8,128)(2,1)S(1)} %pad_maximum_fusion.refs_3_), channel_id=1, source_target_pairs={{0,3},{1,0},{2,1},{3,2},{4,7},{5,4},{6,5},{7,6},{8,11},{9,8},{10,9... | collective-permute-start | bytes 3932168 | tf_op jit(solution)/shard_map/ppermute | solution.py:302
  31.5 8.1 %all-gather.3.cloned.1.call-done.refs_0_ = bf16[512,1280]{1,0:T(8,128)(2,1)} async-done(((bf16[128,1280]{1,0:T(8,128)(2,1)}), bf16[512,1280]{1,0:T(8,128)(2,1)}) %all-gather.3.cloned.1.call-update) | async-done | bytes 1310736 | tf_op jit(solution)/shard_map/all_gather | solution.py:297
  41.7 2.4 %collective-permute-start.1 = (bf16[512,1280]{1,0:T(8,128)(2,1)}, bf16[512,1280]{1,0:T(8,128)(2,1)}, u32[]{:S(2)}, u32[]{:S(2)}) collective-permute-start(bf16[512,1280]{1,0:T(8,128)(2,1)} %all-gather.3.cloned.1.call-done.refs_0_), channel_id=1, source_target_pairs={{0,96},{32,0},{64,32},{96,64},{1,97},{33,1},{65,33},{97,65},{2,98}... | collective-permute-start | bytes 3932168 | tf_op jit(solution)/shard_map/ppermute | solution.py:301
  48.2 14.8 %collective-permute-done.6.refs_5_ = bf16[512,1280]{1,0:T(8,128)(2,1)} collective-permute-done((bf16[512,1280]{1,0:T(8,128)(2,1)S(1)}, bf16[512,1280]{1,0:T(8,128)(2,1)}, u32[]{:S(2)}, u32[]{:S(2)}) %collective-permute-start.6) | collective-permute-done | bytes 1310752 | tf_op jit(solution)/shard_map/ppermute | solution.py:302
  64.1 2.9 %collective-permute-start.10 = (bf16[256,1280]{1,0:T(8,128)(2,1)S(1)}, bf16[256,1280]{1,0:T(8,128)(2,1)}, u32[]{:S(2)}, u32[]{:S(2)}) collective-permute-start(bf16[256,1280]{1,0:T(8,128)(2,1)S(1)} %slice.267), channel_id=1, source_target_pairs={{0,3},{1,0},{2,1},{3,2},{4,7},{5,4},{6,5},{7,6},{8,11},{9,8},{10,9... | collective-permute-start | bytes 1966088 | tf_op jit(solution)/shard_map/ppermute | solution.py:307
  69.0 3.1 %collective-permute-done.refs_1_ = bf16[512,1280]{1,0:T(8,128)(2,1)} collective-permute-done((bf16[512,1280]{1,0:T(8,128)(2,1)}, bf16[512,1280]{1,0:T(8,128)(2,1)}, u32[]{:S(2)}, u32[]{:S(2)}) %collective-permute-start) | collective-permute-done | bytes 1310752 | tf_op jit(solution)/shard_map/ppermute | solution.py:299
  74.8 2.9 %collective-permute-start.8 = (bf16[256,1280]{1,0:T(8,128)(2,1)S(1)}, bf16[256,1280]{1,0:T(8,128)(2,1)}, u32[]{:S(2)}, u32[]{:S(2)}) collective-permute-start(bf16[256,1280]{1,0:T(8,128)(2,1)S(1)} %slice.265), channel_id=1, source_target_pairs={{0,96},{32,0},{64,32},{96,64},{1,97},{33,1},{65,33},{97,65},{2,98}... | collective-permute-start | bytes 1966088 | tf_op jit(solution)/shard_map/ppermute | solution.py:305
  77.8 15.4 %shard_map.73 = (bf16[384,128]{1,0:T(8,128)(2,1)S(1)}, bf16[384,256]{1,0:T(8,128)(2,1)S(1)}, bf16[384,384]{1,0:T(8,128)(2,1)S(1)}, f32[512,768]{1,0:T(8,128)}) custom-call(s32[9]{0:T(128)S(1)} %pad_add_fusion.where_ref, bf16[3,5120,256]{2,1,0:T(8,128)(2,1)} %bitcast.103, f32[1,768]{1,0:T(1,128)S(1)} %bitcast.101, bf16[512,1280]{1,0:T(8,128)(2,1)S(1)} %copy-done.3, ...), custom_call_target="tpu_custom_call" | custom-call | flops 6039797760 | bytes 7864320 | tf_op jit(solution)/shard_map/pallas_call | solution.py:119
  95.9 8.3 %shard_map.74 = (bf16[640,128]{1,0:T(8,128)(2,1)}, bf16[640,256]{1,0:T(8,128)(2,1)}, bf16[640,384]{1,0:T(8,128)(2,1)}) custom-call(s32[9]{0:T(128)} %copy-done, bf16[3,5120,256]{2,1,0:T(8,128)(2,1)} %bitcast.104, f32[1,768]{1,0:T(1,128)} %bitcast.102, bf16[256,1280]{1,0:T(8,128)(2,1)} %collective-permute-done.7.a0, ...), custom_call_target="tpu_custom_call" | custom-call | flops 2013265920 | bytes 7864320 | tf_op jit(solution)/shard_map/pallas_call | solution.py:134
  111.9 4.9 %shard_map.75.refs_0_ = f32[2048,256]{1,0:T(8,128)S(1)} custom-call(bf16[2048,128]{1,0:T(8,128)(2,1)S(1)} %constant_dynamic-update-slice_fusion.q_ref, bf16[2048,128]{1,0:T(8,128)(2,1)S(1)} %bitcast.97, bf16[1280,256]{1,0:T(8,128)(2,1)S(1)} %pad_maximum_fusion.1.refs_0_), custom_call_target="tpu_custom_call" | custom-call | flops 2684354560 | bytes 655360 | tf_op jit(solution)/shard_map/pallas_call | solution.py:236
  118.1 17.1 %collective-permute-done.13.refs_1_ = bf16[1280,256]{1,0:T(8,128)(2,1)S(1)} collective-permute-done((bf16[1280,256]{1,0:T(8,128)(2,1)S(1)}, bf16[1280,256]{1,0:T(8,128)(2,1)S(1)}, u32[]{:S(2)}, u32[]{:S(2)}) %collective-permute-start.13) | collective-permute-done | bytes 655392 | tf_op jit(solution)/shard_map/ppermute | solution.py:321
  136.1 3.2 %collective-permute-start.16 = (bf16[640,256]{1,0:T(8,128)(2,1)}, bf16[640,256]{1,0:T(8,128)(2,1)S(1)}, u32[]{:S(2)}, u32[]{:S(2)}) collective-permute-start(bf16[640,256]{1,0:T(8,128)(2,1)} %slice.279), channel_id=1, source_target_pairs={{0,24},{4,28},{8,0},{12,4},{16,8},{20,12},{24,16},{28,20},{1,25},{... | collective-permute-start | bytes 983048 | tf_op jit(solution)/shard_map/ppermute | solution.py:325
  142.3 10.0 %shard_map.76.refs_0_ = f32[2048,256]{1,0:T(8,128)S(1)} custom-call(bf16[2048,128]{1,0:T(8,128)(2,1)S(1)} %constant_dynamic-update-slice_fusion.q_ref, bf16[2048,128]{1,0:T(8,128)(2,1)S(1)} %bitcast.98, f32[2048,256]{1,0:T(8,128)S(1)} %copy-done.5, bf16[3072,256]{1,0:T(8,128)(2,1)S(1)} %copy-done.2), custom_call_target="tpu_custom_call" | custom-call | flops 6442450944 | bytes 1572864 | tf_op jit(solution)/shard_map/pallas_call | solution.py:236
  152.3 9.8 %shard_map.77.refs_0_ = f32[2048,256]{1,0:T(8,128)S(1)} custom-call(bf16[2048,128]{1,0:T(8,128)(2,1)S(1)} %constant_dynamic-update-slice_fusion.q_ref, bf16[2048,128]{1,0:T(8,128)(2,1)S(1)} %bitcast.99, f32[2048,256]{1,0:T(8,128)S(1)} %shard_map.76.refs_0_, bf16[1280,256]{1,0:T(8,128)(2,1)S(1)} %collective-permute-done.13.refs_1_, ...), custom_call_target="tpu_custom_call" | custom-call | flops 5368709120 | bytes 1310720 | tf_op jit(solution)/shard_map/pallas_call | solution.py:236
  162.1 8.5 %shard_map.78 = bf16[2048,128]{1,0:T(8,128)(2,1)S(1)} custom-call(bf16[2048,128]{1,0:T(8,128)(2,1)S(1)} %constant_dynamic-update-slice_fusion.q_ref, bf16[2048,128]{1,0:T(8,128)(2,1)S(1)} %bitcast.100, f32[2048,256]{1,0:T(8,128)S(1)} %shard_map.77.refs_0_, bf16[640,256]{1,0:T(8,128)(2,1)S(1)} %collective-permute-done.15.refs_1_, ...), custom_call_target="tpu_custom_call" | custom-call | flops 2684354560 | bytes 655360 | tf_op jit(solution)/shard_map/pallas_call | solution.py:236
  173.1 2.9 %collective-permute-start.18 = (bf16[256,256]{1,0:T(8,128)(2,1)S(1)}, bf16[256,256]{1,0:T(8,128)(2,1)S(1)}, u32[]{:S(2)}, u32[]{:S(2)}) collective-permute-start(bf16[256,256]{1,0:T(8,128)(2,1)S(1)} %get-tuple-element.29), channel_id=1, source_target_pairs={{0,96},{32,0},{64,32},{96,64},{1,97},{33,1},{65,33},{97,65},{2,98}... | collective-permute-start | bytes 393224 | tf_op jit(solution)/shard_map/ppermute | solution.py:347
  179.1 6.2 %collective-permute-done.19.refs_2_ = bf16[256,256]{1,0:T(8,128)(2,1)S(1)} collective-permute-done((bf16[256,256]{1,0:T(8,128)(2,1)S(1)}, bf16[256,256]{1,0:T(8,128)(2,1)S(1)}, u32[]{:S(2)}, u32[]{:S(2)}) %collective-permute-start.19) | collective-permute-done | bytes 131104 | tf_op jit(solution)/shard_map/ppermute | solution.py:347
  186.0 5.3 %shard_map.81 = f32[256,1280]{1,0:T(8,128)} custom-call(s32[9]{0:T(128)} %copy-done, bf16[256,256]{1,0:T(8,128)(2,1)} %get-tuple-element.28.refs_0_, bf16[256,256]{1,0:T(8,128)(2,1)} %copy-done.8, bf16[256,256]{1,0:T(8,128)(2,1)} %copy-done.9, bf16[256,256]{1,0:T(8,128)(2,1)} %copy-done.10, bf16[4,256,5120]{2,1,0:T(8,128)(2,1)} %refs_4_.5), custom_call_target="tpu_custom_call" | custom-call | flops 671088640 | bytes 2621440 | tf_op jit(solution)/shard_map/pallas_call | solution.py:167
  196.0 8.8 %shard_map.80 = f32[512,1280]{1,0:T(8,128)} custom-call(s32[9]{0:T(128)} %copy-done, bf16[256,256]{1,0:T(8,128)(2,1)} %get-tuple-element.28.refs_0_, bf16[256,256]{1,0:T(8,128)(2,1)} %copy-done.8, bf16[256,256]{1,0:T(8,128)(2,1)} %copy-done.9, bf16[256,256]{1,0:T(8,128)(2,1)} %copy-done.10, bf16[4,256,5120]{2,1,0:T(8,128)(2,1)} %refs_4_.5), custom_call_target="tpu_custom_call" | custom-call | flops 1342177280 | bytes 5242880 | tf_op jit(solution)/shard_map/pallas_call | solution.py:167
  207.9 3.0 %collective-permute-start.24 = (bf16[256,1280]{1,0:T(8,128)(2,1)S(1)}, bf16[256,1280]{1,0:T(8,128)(2,1)S(1)}, u32[]{:S(2)}, u32[]{:S(2)}) collective-permute-start(bf16[256,1280]{1,0:T(8,128)(2,1)S(1)} %pad_maximum_fusion.3), channel_id=1, source_target_pairs={{0,3},{1,0},{2,1},{3,2},{4,7},{5,4},{6,5},{7,6},{8,11},{9,8},{10,9... | collective-permute-start | bytes 1966088 | tf_op jit(solution)/shard_map/ppermute | solution.py:360
  211.0 5.2 %shard_map.79 = f32[256,1280]{1,0:T(8,128)} custom-call(s32[9]{0:T(128)} %copy-done, bf16[256,256]{1,0:T(8,128)(2,1)} %get-tuple-element.28.refs_0_, bf16[256,256]{1,0:T(8,128)(2,1)} %copy-done.8, bf16[256,256]{1,0:T(8,128)(2,1)} %copy-done.9, bf16[256,256]{1,0:T(8,128)(2,1)} %copy-done.10, bf16[4,256,5120]{2,1,0:T(8,128)(2,1)} %refs_4_.5), custom_call_target="tpu_custom_call" | custom-call | flops 671088640 | bytes 2621440 | tf_op jit(solution)/shard_map/pallas_call | solution.py:167
  216.2 7.7 %collective-permute-done.22 = bf16[256,1280]{1,0:T(8,128)(2,1)S(1)} collective-permute-done((bf16[256,1280]{1,0:T(8,128)(2,1)S(1)}, bf16[256,1280]{1,0:T(8,128)(2,1)S(1)}, u32[]{:S(2)}, u32[]{:S(2)}) %collective-permute-start.22) | collective-permute-done | bytes 655392 | tf_op jit(solution)/shard_map/ppermute | solution.py:359
  (128 shorter events, 50.8 us)
Async XLA Ops:
  6.5 33.1 %all-gather.3.cloned.1.call-start = ((), (), s32[]{:S(2)}) async-start(), calls=%async_computation | async-start | bytes 1638400 | tf_op jit(solution)/shard_map/all_gather | solution.py:297
  8.4 130.9 %all-gather.5.cloned.1.call-start = ((), (), s32[]{:S(2)}) async-start(), calls=%async_computation.1 | async-start | bytes 1966080 | tf_op jit(solution)/shard_map/all_gather | solution.py:311
  8.5 11.9 %collective-permute-start.2 = (bf16[128,1280]{1,0:T(8,128)(2,1)S(1)}, bf16[128,1280]{1,0:T(8,128)(2,1)S(1)}, u32[]{:S(2)}, u32[]{:S(2)}) collective-permute-start(bf16[128,1280]{1,0:T(8,128)(2,1)S(1)} %get-tuple-element.25), channel_id=1, source_target_pairs={{0,32},{32,64},{64,96},{96,0},{1,33},{33,65},{65,97},{97,1},{2,34}... | collective-permute-start | bytes 983048 | tf_op jit(solution)/shard_map/ppermute | solution.py:263
  10.6 16.2 %collective-permute-start.3 = (bf16[128,1280]{1,0:T(8,128)(2,1)S(1)}, bf16[128,1280]{1,0:T(8,128)(2,1)S(1)}, u32[]{:S(2)}, u32[]{:S(2)}) collective-permute-start(bf16[128,1280]{1,0:T(8,128)(2,1)S(1)} %get-tuple-element.25), channel_id=1, source_target_pairs={{0,96},{32,0},{64,32},{96,64},{1,97},{33,1},{65,33},{97,65},{2,98}... | collective-permute-start | bytes 983048 | tf_op jit(solution)/shard_map/ppermute | solution.py:263
  12.8 15.8 %collective-permute-start.4 = (bf16[128,1280]{1,0:T(8,128)(2,1)S(1)}, bf16[128,1280]{1,0:T(8,128)(2,1)S(1)}, u32[]{:S(2)}, u32[]{:S(2)}) collective-permute-start(bf16[128,1280]{1,0:T(8,128)(2,1)S(1)} %get-tuple-element.25), channel_id=1, source_target_pairs={{0,64},{32,96},{64,0},{96,32},{1,65},{33,97},{65,1},{97,33},{2,66}... | collective-permute-start | bytes 983048 | tf_op jit(solution)/shard_map/ppermute | solution.py:263
  28.7 34.3 %collective-permute-start.6 = (bf16[512,1280]{1,0:T(8,128)(2,1)S(1)}, bf16[512,1280]{1,0:T(8,128)(2,1)}, u32[]{:S(2)}, u32[]{:S(2)}) collective-permute-start(bf16[512,1280]{1,0:T(8,128)(2,1)S(1)} %pad_maximum_fusion.refs_3_), channel_id=1, source_target_pairs={{0,3},{1,0},{2,1},{3,2},{4,7},{5,4},{6,5},{7,6},{8,11},{9,8},{10,9... | collective-permute-start | bytes 3932168 | tf_op jit(solution)/shard_map/ppermute | solution.py:302
  31.5 35.5 %collective-permute-start.5 = (bf16[512,1280]{1,0:T(8,128)(2,1)S(1)}, bf16[512,1280]{1,0:T(8,128)(2,1)}, u32[]{:S(2)}, u32[]{:S(2)}) collective-permute-start(bf16[512,1280]{1,0:T(8,128)(2,1)S(1)} %pad_maximum_fusion.refs_3_), channel_id=1, source_target_pairs={{0,1},{1,2},{2,3},{3,0},{4,5},{5,6},{6,7},{7,4},{8,9},{9,10},{10,1... | collective-permute-start | bytes 3932168 | tf_op jit(solution)/shard_map/ppermute | solution.py:300
  39.6 32.5 %collective-permute-start = (bf16[512,1280]{1,0:T(8,128)(2,1)}, bf16[512,1280]{1,0:T(8,128)(2,1)}, u32[]{:S(2)}, u32[]{:S(2)}) collective-permute-start(bf16[512,1280]{1,0:T(8,128)(2,1)} %all-gather.3.cloned.1.call-done.refs_0_), channel_id=1, source_target_pairs={{0,32},{32,64},{64,96},{96,0},{1,33},{33,65},{65,97},{97,1},{2,34}... | collective-permute-start | bytes 3932168 | tf_op jit(solution)/shard_map/ppermute | solution.py:299
  41.7 32.0 %collective-permute-start.1 = (bf16[512,1280]{1,0:T(8,128)(2,1)}, bf16[512,1280]{1,0:T(8,128)(2,1)}, u32[]{:S(2)}, u32[]{:S(2)}) collective-permute-start(bf16[512,1280]{1,0:T(8,128)(2,1)} %all-gather.3.cloned.1.call-done.refs_0_), channel_id=1, source_target_pairs={{0,96},{32,0},{64,32},{96,64},{1,97},{33,1},{65,33},{97,65},{2,98}... | collective-permute-start | bytes 3932168 | tf_op jit(solution)/shard_map/ppermute | solution.py:301
  64.1 31.8 %collective-permute-start.10 = (bf16[256,1280]{1,0:T(8,128)(2,1)S(1)}, bf16[256,1280]{1,0:T(8,128)(2,1)}, u32[]{:S(2)}, u32[]{:S(2)}) collective-permute-start(bf16[256,1280]{1,0:T(8,128)(2,1)S(1)} %slice.267), channel_id=1, source_target_pairs={{0,3},{1,0},{2,1},{3,2},{4,7},{5,4},{6,5},{7,6},{8,11},{9,8},{10,9... | collective-permute-start | bytes 1966088 | tf_op jit(solution)/shard_map/ppermute | solution.py:307
  69.0 26.9 %collective-permute-start.9 = (bf16[256,1280]{1,0:T(8,128)(2,1)}, bf16[256,1280]{1,0:T(8,128)(2,1)}, u32[]{:S(2)}, u32[]{:S(2)}) collective-permute-start(bf16[256,1280]{1,0:T(8,128)(2,1)} %slice.266), channel_id=1, source_target_pairs={{0,1},{1,2},{2,3},{3,0},{4,5},{5,6},{6,7},{7,4},{8,9},{9,10},{10,1... | collective-permute-start | bytes 1966088 | tf_op jit(solution)/shard_map/ppermute | solution.py:306
  73.2 22.7 %collective-permute-start.7 = (bf16[256,1280]{1,0:T(8,128)(2,1)S(1)}, bf16[256,1280]{1,0:T(8,128)(2,1)}, u32[]{:S(2)}, u32[]{:S(2)}) collective-permute-start(bf16[256,1280]{1,0:T(8,128)(2,1)S(1)} %slice.264), channel_id=1, source_target_pairs={{0,32},{32,64},{64,96},{96,0},{1,33},{33,65},{65,97},{97,1},{2,34}... | collective-permute-start | bytes 1966088 | tf_op jit(solution)/shard_map/ppermute | solution.py:304
  74.8 21.1 %collective-permute-start.8 = (bf16[256,1280]{1,0:T(8,128)(2,1)S(1)}, bf16[256,1280]{1,0:T(8,128)(2,1)}, u32[]{:S(2)}, u32[]{:S(2)}) collective-permute-start(bf16[256,1280]{1,0:T(8,128)(2,1)S(1)} %slice.265), channel_id=1, source_target_pairs={{0,96},{32,0},{64,32},{96,64},{1,97},{33,1},{65,33},{97,65},{2,98}... | collective-permute-start | bytes 1966088 | tf_op jit(solution)/shard_map/ppermute | solution.py:305
  108.4 26.8 %collective-permute-start.13 = (bf16[1280,256]{1,0:T(8,128)(2,1)S(1)}, bf16[1280,256]{1,0:T(8,128)(2,1)S(1)}, u32[]{:S(2)}, u32[]{:S(2)}) collective-permute-start(bf16[1280,256]{1,0:T(8,128)(2,1)S(1)} %pad_maximum_fusion.1.refs_0_), channel_id=1, source_target_pairs={{0,8},{4,12},{8,16},{12,20},{16,24},{20,28},{24,0},{28,4},{1,9},{5... | collective-permute-start | bytes 1966088 | tf_op jit(solution)/shard_map/ppermute | solution.py:321
  110.0 25.3 %collective-permute-start.14 = (bf16[1280,256]{1,0:T(8,128)(2,1)S(1)}, bf16[1280,256]{1,0:T(8,128)(2,1)S(1)}, u32[]{:S(2)}, u32[]{:S(2)}) collective-permute-start(bf16[1280,256]{1,0:T(8,128)(2,1)S(1)} %pad_maximum_fusion.1.refs_0_), channel_id=1, source_target_pairs={{0,24},{4,28},{8,0},{12,4},{16,8},{20,12},{24,16},{28,20},{1,25},{... | collective-permute-start | bytes 1966088 | tf_op jit(solution)/shard_map/ppermute | solution.py:322
  135.2 26.9 %collective-permute-start.15 = (bf16[640,256]{1,0:T(8,128)(2,1)S(1)}, bf16[640,256]{1,0:T(8,128)(2,1)S(1)}, u32[]{:S(2)}, u32[]{:S(2)}) collective-permute-start(bf16[640,256]{1,0:T(8,128)(2,1)S(1)} %slice.278), channel_id=1, source_target_pairs={{0,8},{4,12},{8,16},{12,20},{16,24},{20,28},{24,0},{28,4},{1,9},{5... | collective-permute-start | bytes 983048 | tf_op jit(solution)/shard_map/ppermute | solution.py:324
  136.1 26.1 %collective-permute-start.16 = (bf16[640,256]{1,0:T(8,128)(2,1)}, bf16[640,256]{1,0:T(8,128)(2,1)S(1)}, u32[]{:S(2)}, u32[]{:S(2)}) collective-permute-start(bf16[640,256]{1,0:T(8,128)(2,1)} %slice.279), channel_id=1, source_target_pairs={{0,24},{4,28},{8,0},{12,4},{16,8},{20,12},{24,16},{28,20},{1,25},{... | collective-permute-start | bytes 983048 | tf_op jit(solution)/shard_map/ppermute | solution.py:325
  173.1 6.0 %collective-permute-start.18 = (bf16[256,256]{1,0:T(8,128)(2,1)S(1)}, bf16[256,256]{1,0:T(8,128)(2,1)S(1)}, u32[]{:S(2)}, u32[]{:S(2)}) collective-permute-start(bf16[256,256]{1,0:T(8,128)(2,1)S(1)} %get-tuple-element.29), channel_id=1, source_target_pairs={{0,96},{32,0},{64,32},{96,64},{1,97},{33,1},{65,33},{97,65},{2,98}... | collective-permute-start | bytes 393224 | tf_op jit(solution)/shard_map/ppermute | solution.py:347
  176.1 9.3 %collective-permute-start.19 = (bf16[256,256]{1,0:T(8,128)(2,1)S(1)}, bf16[256,256]{1,0:T(8,128)(2,1)S(1)}, u32[]{:S(2)}, u32[]{:S(2)}) collective-permute-start(bf16[256,256]{1,0:T(8,128)(2,1)S(1)} %get-tuple-element.30), channel_id=1, source_target_pairs={{0,32},{32,64},{64,96},{96,0},{1,33},{33,65},{65,97},{97,1},{2,34}... | collective-permute-start | bytes 393224 | tf_op jit(solution)/shard_map/ppermute | solution.py:347
  176.1 9.3 %collective-permute-start.20 = (bf16[256,256]{1,0:T(8,128)(2,1)S(1)}, bf16[256,256]{1,0:T(8,128)(2,1)S(1)}, u32[]{:S(2)}, u32[]{:S(2)}) collective-permute-start(bf16[256,256]{1,0:T(8,128)(2,1)S(1)} %get-tuple-element.27), channel_id=1, source_target_pairs={{0,64},{32,96},{64,0},{96,32},{1,65},{33,97},{65,1},{97,33},{2,66}... | collective-permute-start | bytes 393224 | tf_op jit(solution)/shard_map/ppermute | solution.py:347
  192.7 14.1 %collective-permute-start.21 = (bf16[128,1280]{1,0:T(8,128)(2,1)S(1)}, bf16[128,1280]{1,0:T(8,128)(2,1)S(1)}, u32[]{:S(2)}, u32[]{:S(2)}) collective-permute-start(bf16[128,1280]{1,0:T(8,128)(2,1)S(1)} %get-tuple-element.23), channel_id=1, source_target_pairs={{0,1},{1,2},{2,3},{3,0},{4,5},{5,6},{6,7},{7,4},{8,9},{9,10},{10,1... | collective-permute-start | bytes 983048 | tf_op jit(solution)/shard_map/ppermute | solution.py:353
  194.3 12.6 %collective-permute-start.23 = (bf16[128,1280]{1,0:T(8,128)(2,1)S(1)}, bf16[128,1280]{1,0:T(8,128)(2,1)S(1)}, u32[]{:S(2)}, u32[]{:S(2)}) collective-permute-start(bf16[128,1280]{1,0:T(8,128)(2,1)S(1)} %get-tuple-element.24), channel_id=1, source_target_pairs={{0,3},{1,0},{2,1},{3,2},{4,7},{5,4},{6,5},{7,6},{8,11},{9,8},{10,9... | collective-permute-start | bytes 983048 | tf_op jit(solution)/shard_map/ppermute | solution.py:354
  207.5 16.4 %collective-permute-start.22 = (bf16[256,1280]{1,0:T(8,128)(2,1)S(1)}, bf16[256,1280]{1,0:T(8,128)(2,1)S(1)}, u32[]{:S(2)}, u32[]{:S(2)}) collective-permute-start(bf16[256,1280]{1,0:T(8,128)(2,1)S(1)} %pad_maximum_fusion.2), channel_id=1, source_target_pairs={{0,1},{1,2},{2,3},{3,0},{4,5},{5,6},{6,7},{7,4},{8,9},{9,10},{10,1... | collective-permute-start | bytes 1966088 | tf_op jit(solution)/shard_map/ppermute | solution.py:359
  207.9 16.0 %collective-permute-start.24 = (bf16[256,1280]{1,0:T(8,128)(2,1)S(1)}, bf16[256,1280]{1,0:T(8,128)(2,1)S(1)}, u32[]{:S(2)}, u32[]{:S(2)}) collective-permute-start(bf16[256,1280]{1,0:T(8,128)(2,1)S(1)} %pad_maximum_fusion.3), channel_id=1, source_target_pairs={{0,3},{1,0},{2,1},{3,2},{4,7},{5,4},{6,5},{7,6},{8,11},{9,8},{10,9... | collective-permute-start | bytes 1966088 | tf_op jit(solution)/shard_map/ppermute | solution.py:360
  (20 other events, 303.8 us)
Sparse Core Ops, SparseCore 0:
  9.0 30.5 all-gather.2
  96.0 34.0 all-gather.4

commit v4 on v3

--- a/solution.py
+++ b/solution.py
@@ -50,113 +50,89 @@
     return [jax.ShapeDtypeStruct((rows, n * HD), jnp.bfloat16) for n in (1, 2, 3)]
 
 
-def start_weights(where_ref, w_hbm, w_buf, sems):
+def stage_kernel(n_a, b_slices, n_done, has_part, emit_all, where_ref, w_hbm, scale_ref, *refs):
+    a_refs, refs = refs[:n_a], refs[n_a:]
+    b_refs, refs = refs[: len(b_slices)], refs[len(b_slices) :]
+    done_refs, refs = refs[:n_done], refs[n_done:]
+    part_refs, refs = refs[:has_part], refs[has_part:]
+    outs, (acc_ref, w_buf, sems) = refs[:-3], refs[-3:]
     feat = w_buf.shape[2]
     copies = []
     for i in range(4):
         rows = pl.ds(pl.multiple_of(where_ref[i] * feat, feat), feat)
         copies.append(pltpu.make_async_copy(w_hbm.at[:, rows, :], w_buf.at[i], sems.at[i]))
         copies[-1].start()
-    return copies
-
-
-def early_kernel(where_ref, w_hbm, scale_ref, *refs):
-    a_refs, b_refs = refs[:3], refs[3:6]
-    q_ref, kv_ref, give_ref, part_ref, acc_ref, w_buf, sems = refs[6:]
-    copies = start_weights(where_ref, w_hbm, w_buf, sems)
-    na = a_refs[0].shape[0] // 4
+    na = sum(r.shape[0] for r in a_refs)
+    fresh = not has_part
     for i in range(4):
         copies[i].wait()
-        rows = pl.ds(pl.multiple_of(where_ref[i] * na, na), na)
-        x = [a_ref[rows, :] for a_ref in a_refs]
-        if i < 3:
-            x.append(b_refs[i][...])
-        x = jnp.concatenate(x, axis=0)
-        n = x.shape[0]
+        x = [r[:, i * feat : (i + 1) * feat] for r in a_refs]
+        x += [r[...] for r, s in zip(b_refs, b_slices) if s == i]
+        with_b = len(x) > n_a
+        x = jnp.concatenate(x, axis=0) if len(x) > 1 else x[0]
         for c in range(3):
             cols = slice(c * 256, (c + 1) * 256)
             d = jnp.dot(x, w_buf[i, c], preferred_element_type=jnp.float32)
-            acc_ref[:n, cols] = d if i == 0 else acc_ref[:n, cols] + d
-    emit_heads(acc_ref[: 3 * na], scale_ref, where_ref[4], q_ref, kv_ref, give_ref)
-    part_ref[...] = acc_ref[3 * na :]
-
-
-def last_kernel(where_ref, w_hbm, scale_ref, a0, a1, b0, b1, part_ref, q_ref, kv_ref, give_ref, acc_ref, xa_ref, w_buf, sems):
-    copies = start_weights(where_ref, w_hbm, w_buf, sems)
-    ha = a0.shape[0]
-    na = ha // 2
-    xa_ref[:ha] = a0[...]
-    xa_ref[ha:] = a1[...]
-    for i in range(4):
-        copies[i].wait()
-        x = xa_ref[pl.ds(pl.multiple_of(where_ref[i] * na, na), na), :]
-        for c in range(3):
-            cols = slice(c * 256, (c + 1) * 256)
-            if i < 3:
-                d = jnp.dot(x, w_buf[i, c], preferred_element_type=jnp.float32)
-                acc_ref[:na, cols] = d if i == 0 else acc_ref[:na, cols] + d
-            else:
-                x_all = jnp.concatenate([x, b0[...], b1[...]], axis=0)
-                d = jnp.dot(x_all, w_buf[i, c], preferred_element_type=jnp.float32)
-                acc_ref[:na, cols] = acc_ref[:na, cols] + d[:na]
-                acc_ref[na:, cols] = part_ref[:, cols] + d[na:]
-    emit_heads(acc_ref[...], scale_ref, where_ref[4], q_ref, kv_ref, give_ref)
+            acc_ref[:na, cols] = d[:na] if i == 0 else acc_ref[:na, cols] + d[:na]
+            if with_b:
+                first = i == min(b_slices)
+                before = None if first and fresh else part_refs[0][:, cols] if first else acc_ref[na:, cols]
+                acc_ref[na:, cols] = d[na:] if before is None else before + d[na:]
+    if not emit_all and not n_done:
+        outs[0][...] = acc_ref[:na]
+        outs[1][...] = acc_ref[na:]
+        return
+    rows = acc_ref[...] if emit_all else acc_ref[:na]
+    if n_done:
+        rows = jnp.concatenate([done_refs[0][...], rows], axis=0)
+    emit_heads(rows, scale_ref, where_ref[4], *outs[:3])
+    if not emit_all:
+        outs[3][...] = acc_ref[na:]
 
 
 VM = pl.BlockSpec(memory_space=pltpu.VMEM)
 FIXED = [pl.BlockSpec(memory_space=pltpu.SMEM), pl.BlockSpec(memory_space=pltpu.HBM), VM]
 
 
-def weight_scratch(w):
-    return [
-        pltpu.VMEM((4, 3, w.shape[1] // 4, w.shape[2]), jnp.bfloat16),
-        pltpu.SemaphoreType.DMA((4,)),
-    ]
-
-
-def project_early(where, w, scale, a_parts, b_parts):
-    na, nb = a_parts[0].shape[0] // 4, b_parts[0].shape[0]
+def project_stage(where, w, scale, a_parts, b_parts, b_slices, done, part, emit_all, limit):
+    feat = w.shape[1] // 4
+    na = sum(x.shape[0] for x in a_parts)
+    nb = 512 if part is None else part.shape[0]
+    f32 = lambda n: jax.ShapeDtypeStruct((n, 768), jnp.float32)
+    if emit_all:
+        shapes = heads_shape(na + nb)
+    elif done is not None:
+        shapes = heads_shape(done.shape[0] + na) + [f32(nb)]
+    else:
+        shapes = [f32(na), f32(nb)]
+    extra = [x for x in (done, part) if x is not None]
     return pl.pallas_call(
-        early_kernel,
-        in_specs=FIXED + [VM] * 6,
-        out_specs=[VM] * 4,
-        out_shape=heads_shape(3 * na) + [jax.ShapeDtypeStruct((nb, 768), jnp.float32)],
-        scratch_shapes=[pltpu.VMEM((3 * na + nb, 768), jnp.float32)] + weight_scratch(w),
-        compiler_params=pltpu.CompilerParams(vmem_limit_bytes=52 << 20),
+        functools.partial(
+            stage_kernel, len(a_parts), b_slices, int(done is not None), int(part is not None), emit_all
+        ),
+        in_specs=FIXED + [VM] * (len(a_parts) + len(b_parts) + len(extra)),
+        out_specs=[VM] * len(shapes),
+        out_shape=shapes,
+        scratch_shapes=[
+            pltpu.VMEM((na + nb, 768), jnp.float32),
+            pltpu.VMEM((4, 3, feat, w.shape[2]), jnp.bfloat16),
+            pltpu.SemaphoreType.DMA((4,)),
+        ],
+        compiler_params=pltpu.CompilerParams(vmem_limit_bytes=limit << 20),
         cost_estimate=pl.CostEstimate(
-            flops=2 * 768 * (3 * na * w.shape[1] + nb * w.shape[1] * 3 // 4), bytes_accessed=w.size * 2, transcendentals=0
-        ),
-    )(where, w, scale, *a_parts, *b_parts)
-
-
-def project_last(where, w, scale, a0, a1, b0, b1, part):
-    na, nb, feat = a0.shape[0] // 2, part.shape[0], a0.shape[1]
-    return pl.pallas_call(
-        last_kernel,
-        in_specs=FIXED + [VM] * 5,
-        out_specs=[VM] * 3,
-        out_shape=heads_shape(na + nb),
-        scratch_shapes=[pltpu.VMEM((na + nb, 768), jnp.float32), pltpu.VMEM((4 * na, feat), jnp.bfloat16)]
-        + weight_scratch(w),
-        compiler_params=pltpu.CompilerParams(vmem_limit_bytes=56 << 20),
-        cost_estimate=pl.CostEstimate(
-            flops=2 * 768 * (na * w.shape[1] + nb * feat), bytes_accessed=w.size * 2, transcendentals=0
-        ),
-    )(where, w, scale, a0, a1, b0, b1, part)
+            flops=2 * 768 * feat * (4 * na + sum(x.shape[0] for x in b_parts)),
+            bytes_accessed=w.size * 2,
+            transcendentals=0,
+        ),
+    )(where, w, scale, *a_parts, *b_parts, *extra)
 
 
 def out_kernel(where_ref, *refs):
     xs, w_ref, o_ref = refs[:4], refs[4], refs[5]
-    k = pl.program_id(1)
-    for i, x_ref in enumerate(xs):
-
-        @pl.when(k == i)
-        def _():
-            d = jnp.dot(x_ref[...], w_ref[0], preferred_element_type=jnp.float32)
-            if i == 0:
-                o_ref[...] = d
-            else:
-                o_ref[...] += d
+    o_ref[...] = sum(
+        jnp.dot(x_ref[...], w_ref[where_ref[5 + i]], preferred_element_type=jnp.float32)
+        for i, x_ref in enumerate(xs)
+    )
 
 
 def out_project(where, xs, w_out, places):
@@ -168,14 +144,10 @@
         out_kernel,
         grid_spec=pltpu.PrefetchScalarGridSpec(
             num_scalar_prefetch=1,
-            grid=(n, 4),
-            in_specs=[pl.BlockSpec(x.shape, lambda r, k, s: (0, 0)) for x in xs]
-            + [
-                pl.BlockSpec(
-                    (1, w_out.shape[1], cols), lambda r, k, s: (s[5 + k], 0, s[first + step * r])
-                )
-            ],
-            out_specs=pl.BlockSpec((rows, cols), lambda r, k, s: (r, 0)),
+            grid=(n,),
+            in_specs=[pl.BlockSpec(x.shape, lambda r, s: (0, 0)) for x in xs]
+            + [pl.BlockSpec((4, w_out.shape[1], cols), lambda r, s: (0, 0, s[first + step * r]))],
+            out_specs=pl.BlockSpec((rows, cols), lambda r, s: (r, 0)),
         ),
         out_shape=jax.ShapeDtypeStruct((n * rows, cols), jnp.float32),
         compiler_params=pltpu.CompilerParams(vmem_limit_bytes=56 << 20),
@@ -276,13 +248,17 @@
 
     early = [(g, 0) for g in range(3)]
     late = [(3, 0)] + [(g, 1) for g in range(4)]
-    keys = [(y, s) + g for s in (0, 1) for g in late]
-    keys += [(yy, s) + g for yy in range(ny) for s in (0, 1) for g in early]
-    keys += [(y + o, s) + g for o in (-1, 1) for s in (0, 1) for g in late]
-    keys += [(y + 2, s) + g for s in (0, 1) for g in late]
+    def ring_order(part):
+        own = [(y, s) + g for s in (0, 1) for g in part]
+        near = [(y + o, s) + g for o in (-1, 1) for s in (0, 1) for g in part]
+        far = [(y + 2, s) + g for s in (0, 1) for g in part]
+        return own, near, far
+
+    early_ids, late_ids = ring_order(early), ring_order(late)
+    keys = sum(early_ids, []) + sum(late_ids, [])
     key_ids = jnp.stack([block_id(*k) for k in keys])
     query_ids = jnp.stack(
-        [block_id(y, s, g, odd) for s in (0, 1) for g in range(4) for odd in (0, 1)]
+        [block_id(y, s, g, odd) for s in (0, 1) for odd in (0, 1) for g in range(4)]
     )
     blocks = jnp.arange(block_mask.shape[1], dtype=jnp.int32)
     key_hot = (key_ids[:, None] == blocks[None, :]).astype(jnp.float32)
@@ -294,7 +270,7 @@
     bias = jnp.pad(bias, ((0, 0), (0, HD - bias.shape[1])))
     bias = jnp.repeat(bias, BLOCK, axis=0)
 
-    a_own = lax.all_gather(tokens[:half], "tensor", axis=0, tiled=True)
+    a_own = jnp.concatenate(direct(tokens[:half], "tensor", nt), axis=1)
     b_own = jnp.concatenate(direct(tokens[half:], "ulysses", nu), axis=0)
     a_m = pp(a_own, "ulysses", ring(nu, 1))
     b_m = pp(b_own, "tensor", ring(nt, 1))
@@ -306,43 +282,42 @@
     b0 = pp(b_m[:bh], "tensor", ring(nt, 1))
     b1 = pp(b_p[bh:], "tensor", ring(nt, -1))
 
-    q1, kv1, give1, part = project_early(where, w, scale, [a_own, a_m, a_p], [b_own, b_m, b_p])
-    got1 = pp(give1, "blk", core_swap(nb))
-    kv1_all = lax.all_gather(
-        jnp.concatenate([kv1, got1[:, HD:]], axis=0),
-        "blk",
-        axis=0,
-        tiled=True,
-        axis_index_groups=[list(range(0, nb, 2)), list(range(1, nb, 2))],
+    def swap(kv, give):
+        got = pp(give, "blk", core_swap(nb))
+        return got[:, :HD], jnp.concatenate([kv, got[:, HD:]], axis=0)
+
+    def near_y(kv):
+        return [pp(kv, "blk", y_ring(nb, s)) for s in (1, -1)]
+
+    def far_y(kv_m, kv_p):
+        h = kv_m.shape[0] // 2
+        return [pp(kv_m[:h], "blk", y_ring(nb, 1)), pp(kv_p[h:], "blk", y_ring(nb, -1))]
+
+    done, part = project_stage(where, w, scale, [a_own], [b_own], (0,), None, None, False, 48)
+    q1, kv1, give1, part = project_stage(
+        where, w, scale, [a_m, a_p], [b_m, b_p], (1, 2), done, part, False, 46
     )
-    q2, kv2, give2 = project_last(where, w, scale, a0, a1, b0, b1, part)
-    got2 = pp(give2, "blk", core_swap(nb))
-    kv2_own = jnp.concatenate([kv2, got2[:, HD:]], axis=0)
-    kv2_m = pp(kv2_own, "blk", y_ring(nb, 1))
-    kv2_p = pp(kv2_own, "blk", y_ring(nb, -1))
-    kh = kv2_own.shape[0] // 2
-    kv2_0 = pp(kv2_m[:kh], "blk", y_ring(nb, 1))
-    kv2_1 = pp(kv2_p[kh:], "blk", y_ring(nb, -1))
-
-    def in_order(early_q, late_q):
-        e = [early_q[i * half : (i + 1) * half] for i in range(3)]
-        l = [late_q[i * half : (i + 1) * half] for i in range(5)]
-        e.append(l[0])
-        return [x for g in range(4) for x in (e[g], l[1 + g])]
-
-    q = jnp.concatenate(in_order(q1, q2) + in_order(got1[:, :HD], got2[:, :HD]), axis=0)
-
-    state = attention(q, bias, [kv2_own], 0, None, False, 640)
-    state = attention(q, bias, [kv1_all], 10, state, False, 768)
-    state = attention(q, bias, [kv2_m, kv2_p], 34, state, False, 640)
-    out = attention(q, bias, [kv2_0, kv2_1], 54, state, True, 640)
-
-    out = out.reshape(2, nu, 2 * half, HD)
+    q1x, kv1 = swap(kv1, give1)
+    kv1_near = near_y(kv1)
+    kv1_far = far_y(*kv1_near)
+    q2, kv2, give2 = project_stage(where, w, scale, [a0, a1], [b0, b1], (3, 3), None, part, True, 56)
+    q2x, kv2 = swap(kv2, give2)
+    kv2_near = near_y(kv2)
+    kv2_far = far_y(*kv2_near)
+
+    q = jnp.concatenate([q1, q2, q1x, q2x], axis=0)
+    state = attention(q, bias, [kv1] + kv1_near, 0, None, False, 768)
+    state = attention(q, bias, kv1_far, 18, state, False, 384)
+    state = attention(q, bias, [kv2] + kv2_near, 24, state, False, 640)
+    out = attention(q, bias, kv2_far, 54, state, True, 640)
+
+    out = out.reshape(2, 2, nu, half, HD)
     other = pp(out[1], "blk", core_swap(nb))
     mine = out[0]
     first = jnp.where(core == 0, mine, other)
     second = jnp.where(core == 0, other, mine)
     heads = jnp.concatenate([first, second], axis=-1)
+    heads = [heads[:, g].reshape(2 * half, 2 * HD) for g in range(nu)]
     arrived = [heads[0]] + [
         pp(heads[i], "ulysses", ring(nu, OFFSETS[i])) for i in range(1, nu)
     ]

time: 234 us -> 199 us (0.85)
  waiting for transfers between devices: 74.7 us -> 50.6 us
  between operations: 16.6 us -> 3.23 us
  starting transfers between devices: 38.7 us -> 51.6 us
  local copies, waits for them, and re-layouts: 18.8 us -> 10.5 us
    ppermute x1, waiting for transfers between devices: 0.01 us -> 17.2 us  [local(): b_m = pp(b_own, 'tensor', ring(nt, 1))]
    ppermute x1, waiting for transfers between devices: 14.8 us -> 0.01 us  [local(): b_p = pp(b_own, 'tensor', ring(nt, -1))]
    ppermute x6 -> x10, waiting for transfers between devices: 18.3 us -> 8.27 us  [the longest x4 6.68 us: near_y(): return [pp(kv, 'blk', y_ring(nb, s)) for s in (1, -1)]]
    all_gather x2 -> x0, waiting for transfers between devices: 8.11 us -> none  [the longest x1 8.11 us: local(): a_own = lax.all_gather(tokens[:half], 'tensor', axis=0, tiled=True)]
    ppermute x6 -> x10, starting transfers between devices: 7.09 us -> 13.8 us  [the longest x4 6.62 us: near_y(): return [pp(kv, 'blk', y_ring(nb, s)) for s in (1, -1)]]
    ppermute x3 -> x6, starting transfers between devices: 6.05 us -> 12.3 us  [direct(): return [value] + [pp(value, axis, ring(n, s)) for s in (1, -1, 2)]]
    unnamed x51 -> x42, local copies, waits for them, and re-layouts: 9.52 us -> 3.45 us
    ppermute x3 -> x6, waiting for transfers between devices: 14 us -> 8.21 us  [direct(): return [value] + [pp(value, axis, ring(n, s)) for s in (1, -1, 2)]]
  transfers between devices with their start and end apart: 27 -> 32, of which waited for: 12 -> 13; matrix products, arithmetic and copies ran while one was open for 6% -> 4% of each run, Pallas kernels for 27% -> 27%
where the time goes in v4:
time: 199 us
  Pallas kernels  75.2 us (38%)
  starting transfers between devices  51.6 us (26%)
  waiting for transfers between devices  50.6 us (25%)
  local copies, waits for them, and re-layouts  10.5 us (5%)
  other arithmetic  7.17 us (4%)
  between operations  3.23 us (2%)
    pallas_call x4, Pallas kernels, attention(): pl.pallas_call(functools.partial(attn_kernel, bk, first_block, begin, end...  35.8 us
    pallas_call x3, Pallas kernels, project_stage(): pl.pallas_call(functools.partial(stage_kernel, len(a_parts), b_slices, in...  24.8 us
    ppermute x1, waiting for transfers between devices, local(): b_m = pp(b_own, 'tensor', ring(nt, 1))  17.2 us
    pallas_call x3, Pallas kernels, out_project(): pl.pallas_call(out_kernel, grid_spec=pltpu.PrefetchScalarGridSpec(num_sca...  14.6 us
    ppermute x6, starting transfers between devices, direct(): return [value] + [pp(value, axis, ring(n, s)) for s in (1, -1, 2)]  12.3 us
    ppermute x6, waiting for transfers between devices, direct(): return [value] + [pp(value, axis, ring(n, s)) for s in (1, -1, 2)]  8.21 us
    ppermute x1, waiting for transfers between devices, local(): from_m = pp(to_p, 'tensor', ring(nt, 1))  7.69 us
    ppermute x3, waiting for transfers between devices, local(): pp(heads[i], 'ulysses', ring(nu, OFFSETS[i]))  7.18 us
  transfers between devices with their start and end apart: 32, of which 13 were waited for; matrix products, arithmetic and copies ran while one was open for 4% of the time, Pallas kernels for 27%

profile of v4, /device:TPU:0, one launch (start us, length us, event | category | flops | bytes accessed | tf_op | source)
XLA Modules:
  0.0 198.6 jit_solution(13614022290240323121)
XLA Ops:
  13.0 3.0 %collective-permute-start.2 = (bf16[128,1280]{1,0:T(8,128)(2,1)S(1)}, bf16[128,1280]{1,0:T(8,128)(2,1)S(1)}, u32[]{:S(2)}, u32[]{:S(2)}) collective-permute-start(bf16[128,1280]{1,0:T(8,128)(2,1)S(1)} %get-tuple-element.30), channel_id=1, source_target_pairs={{0,2},{1,3},{2,0},{3,1},{4,6},{5,7},{6,4},{7,5},{8,10},{9,11},{10,... | collective-permute-start | bytes 983048 | tf_op jit(solution)/shard_map/ppermute | solution.py:235
  16.0 3.4 %collective-permute-done.6 = bf16[128,1280]{1,0:T(8,128)(2,1)S(1)} collective-permute-done((bf16[128,1280]{1,0:T(8,128)(2,1)S(1)}, bf16[128,1280]{1,0:T(8,128)(2,1)S(1)}, u32[]{:S(2)}, u32[]{:S(2)}) %collective-permute-start.6) | collective-permute-done | bytes 327712 | tf_op jit(solution)/shard_map/ppermute | solution.py:235
  25.2 5.1 %collective-permute-start.3 = (bf16[128,5120]{1,0:T(8,128)(2,1)S(1)}, bf16[128,5120]{1,0:T(8,128)(2,1)}, u32[]{:S(2)}, u32[]{:S(2)}) collective-permute-start(bf16[128,5120]{1,0:T(8,128)(2,1)S(1)} %pad_maximum_fusion.refs_0_), channel_id=1, source_target_pairs={{0,32},{32,64},{64,96},{96,0},{1,33},{33,65},{65,97},{97,1},{2,34}... | collective-permute-start | bytes 3932168 | tf_op jit(solution)/shard_map/ppermute | solution.py:275
  30.8 5.2 %shard_map.73 = (f32[128,768]{1,0:T(8,128)S(1)}, f32[512,768]{1,0:T(8,128)S(1)}) custom-call(s32[9]{0:T(128)S(1)} %pad_add_fusion.where_ref, bf16[3,5120,256]{2,1,0:T(8,128)(2,1)} %bitcast.94, f32[1,768]{1,0:T(1,128)S(1)} %bitcast.91, bf16[128,5120]{1,0:T(8,128)(2,1)S(1)} %pad_maximum_fusion.refs_0_, bf16[512,1280]{1,0:T(8,128)(2,1)S(1)} %pad_maximum_fusion.1.refs_1_), custom_call_target="tpu_custom_call" | custom-call | flops 2013265920 | bytes 7864320 | tf_op jit(solution)/shard_map/pallas_call | solution.py:109
  36.0 17.2 %collective-permute-done.8.refs_2_ = bf16[512,1280]{1,0:T(8,128)(2,1)} collective-permute-done((bf16[512,1280]{1,0:T(8,128)(2,1)S(1)}, bf16[512,1280]{1,0:T(8,128)(2,1)}, u32[]{:S(2)}, u32[]{:S(2)}) %collective-permute-start.8) | collective-permute-done | bytes 1310752 | tf_op jit(solution)/shard_map/ppermute | solution.py:276
  55.6 3.3 %collective-permute-start.13 = (bf16[256,1280]{1,0:T(8,128)(2,1)S(1)}, bf16[256,1280]{1,0:T(8,128)(2,1)S(1)}, u32[]{:S(2)}, u32[]{:S(2)}) collective-permute-start(bf16[256,1280]{1,0:T(8,128)(2,1)S(1)} %slice.101), channel_id=1, source_target_pairs={{0,3},{1,0},{2,1},{3,2},{4,7},{5,4},{6,5},{7,6},{8,11},{9,8},{10,9... | collective-permute-start | bytes 1966088 | tf_op jit(solution)/shard_map/ppermute | solution.py:283
  60.0 2.8 %collective-permute-start.10 = (bf16[64,5120]{1,0:T(8,128)(2,1)S(1)}, bf16[64,5120]{1,0:T(8,128)(2,1)S(1)}, u32[]{:S(2)}, u32[]{:S(2)}) collective-permute-start(bf16[64,5120]{1,0:T(8,128)(2,1)S(1)} %slice.98), channel_id=1, source_target_pairs={{0,32},{32,64},{64,96},{96,0},{1,33},{33,65},{65,97},{97,1},{2,34}... | collective-permute-start | bytes 1966088 | tf_op jit(solution)/shard_map/ppermute | solution.py:280
  64.5 11.3 %shard_map.74 = (bf16[384,128]{1,0:T(8,128)(2,1)S(1)}, bf16[384,256]{1,0:T(8,128)(2,1)S(1)}, bf16[384,384]{1,0:T(8,128)(2,1)S(1)}, f32[512,768]{1,0:T(8,128)S(1)}) custom-call(s32[9]{0:T(128)S(1)} %pad_add_fusion.where_ref, bf16[3,5120,256]{2,1,0:T(8,128)(2,1)} %bitcast.95, f32[1,768]{1,0:T(1,128)S(1)} %bitcast.92, ...), custom_call_target="tpu_custom_call" | custom-call | flops 4026531840 | bytes 7864320 | tf_op jit(solution)/shard_map/pallas_call | solution.py:109
  80.2 8.3 %shard_map.75 = (bf16[640,128]{1,0:T(8,128)(2,1)}, bf16[640,256]{1,0:T(8,128)(2,1)}, bf16[640,384]{1,0:T(8,128)(2,1)}) custom-call(s32[9]{0:T(128)} %copy-done.3, bf16[3,5120,256]{2,1,0:T(8,128)(2,1)} %bitcast.96, f32[1,768]{1,0:T(1,128)} %bitcast.93, bf16[64,5120]{1,0:T(8,128)(2,1)} %copy-done.10, bf16[64,5120]{1,0:T(8,128)(2,1)} %copy-done.11, ...), custom_call_target="tpu_custom_call" | custom-call | flops 2013265920 | bytes 7864320 | tf_op jit(solution)/shard_map/pallas_call | solution.py:109
  96.0 5.5 %collective-permute-done.16.refs_1_ = bf16[768,256]{1,0:T(8,128)(2,1)S(1)} collective-permute-done((bf16[768,256]{1,0:T(8,128)(2,1)S(1)}, bf16[768,256]{1,0:T(8,128)(2,1)S(1)}, u32[]{:S(2)}, u32[]{:S(2)}) %collective-permute-start.16) | collective-permute-done | bytes 393248 | tf_op jit(solution)/shard_map/ppermute | solution.py:290
  101.9 3.0 %collective-permute-start.19 = (bf16[384,256]{1,0:T(8,128)(2,1)S(1)}, bf16[384,256]{1,0:T(8,128)(2,1)S(1)}, u32[]{:S(2)}, u32[]{:S(2)}) collective-permute-start(bf16[384,256]{1,0:T(8,128)(2,1)S(1)} %slice.106), channel_id=1, source_target_pairs={{0,24},{4,28},{8,0},{12,4},{16,8},{20,12},{24,16},{28,20},{1,25},{... | collective-permute-start | bytes 589832 | tf_op jit(solution)/shard_map/ppermute | solution.py:294
  105.1 3.2 %collective-permute-start.21 = (bf16[1280,256]{1,0:T(8,128)(2,1)S(1)}, bf16[1280,256]{1,0:T(8,128)(2,1)S(1)}, u32[]{:S(2)}, u32[]{:S(2)}) collective-permute-start(bf16[1280,256]{1,0:T(8,128)(2,1)S(1)} %pad_maximum_fusion.2.refs_1_), channel_id=1, source_target_pairs={{0,24},{4,28},{8,0},{12,4},{16,8},{20,12},{24,16},{28,20},{1,25},{... | collective-permute-start | bytes 1966088 | tf_op jit(solution)/shard_map/ppermute | solution.py:290
  108.5 6.5 %shard_map.76.refs_0_ = f32[2048,256]{1,0:T(8,128)S(1)} custom-call(bf16[2048,128]{1,0:T(8,128)(2,1)S(1)} %pad_maximum_fusion.5.q_ref, bf16[2048,128]{1,0:T(8,128)(2,1)S(1)} %bitcast.87, bf16[768,256]{1,0:T(8,128)(2,1)S(1)} %pad_maximum_fusion.6.refs_0_, bf16[768,256]{1,0:T(8,128)(2,1)S(1)} %collective-permute-done.16.refs_1_, ...), custom_call_target="tpu_custom_call" | custom-call | flops 4831838208 | bytes 1179648 | tf_op jit(solution)/shard_map/pallas_call | solution.py:208
  115.1 7.1 %shard_map.77.refs_0_ = f32[2048,256]{1,0:T(8,128)S(1)} custom-call(bf16[2048,128]{1,0:T(8,128)(2,1)S(1)} %pad_maximum_fusion.5.q_ref, bf16[2048,128]{1,0:T(8,128)(2,1)S(1)} %bitcast.88, f32[2048,256]{1,0:T(8,128)S(1)} %shard_map.76.refs_0_, bf16[384,256]{1,0:T(8,128)(2,1)S(1)} %collective-permute-done.18.refs_1_, ...), custom_call_target="tpu_custom_call" | custom-call | flops 1610612736 | bytes 393216 | tf_op jit(solution)/shard_map/pallas_call | solution.py:208
  123.4 3.5 %collective-permute-start.23 = (bf16[640,256]{1,0:T(8,128)(2,1)S(1)}, bf16[640,256]{1,0:T(8,128)(2,1)S(1)}, u32[]{:S(2)}, u32[]{:S(2)}) collective-permute-start(bf16[640,256]{1,0:T(8,128)(2,1)S(1)} %slice.217), channel_id=1, source_target_pairs={{0,24},{4,28},{8,0},{12,4},{16,8},{20,12},{24,16},{28,20},{1,25},{... | collective-permute-start | bytes 983048 | tf_op jit(solution)/shard_map/ppermute | solution.py:294
  126.9 13.7 %shard_map.78.refs_0_ = f32[2048,256]{1,0:T(8,128)S(1)} custom-call(bf16[2048,128]{1,0:T(8,128)(2,1)S(1)} %pad_maximum_fusion.5.q_ref, bf16[2048,128]{1,0:T(8,128)(2,1)S(1)} %bitcast.89, f32[2048,256]{1,0:T(8,128)S(1)} %shard_map.77.refs_0_, bf16[1280,256]{1,0:T(8,128)(2,1)S(1)} %pad_maximum_fusion.2.refs_1_, ...), custom_call_target="tpu_custom_call" | custom-call | flops 8053063680 | bytes 1966080 | tf_op jit(solution)/shard_map/pallas_call | solution.py:208
  140.7 8.5 %shard_map.79 = bf16[2048,128]{1,0:T(8,128)(2,1)S(1)} custom-call(bf16[2048,128]{1,0:T(8,128)(2,1)S(1)} %pad_maximum_fusion.5.q_ref, bf16[2048,128]{1,0:T(8,128)(2,1)S(1)} %bitcast.90, f32[2048,256]{1,0:T(8,128)S(1)} %shard_map.78.refs_0_, bf16[640,256]{1,0:T(8,128)(2,1)S(1)} %collective-permute-done.22.refs_1_, ...), custom_call_target="tpu_custom_call" | custom-call | flops 2684354560 | bytes 655360 | tf_op jit(solution)/shard_map/pallas_call | solution.py:208
  157.2 5.2 %collective-permute-done.26.refs_2_ = bf16[256,256]{1,0:T(8,128)(2,1)S(1)} collective-permute-done((bf16[256,256]{1,0:T(8,128)(2,1)S(1)}, bf16[256,256]{1,0:T(8,128)(2,1)S(1)}, u32[]{:S(2)}, u32[]{:S(2)}) %collective-permute-start.26) | collective-permute-done | bytes 131104 | tf_op jit(solution)/shard_map/ppermute | solution.py:322
  163.1 4.6 %shard_map.82 = f32[256,1280]{1,0:T(8,128)} custom-call(s32[9]{0:T(128)} %copy-done.3, bf16[256,256]{1,0:T(8,128)(2,1)} %bitcast.97, bf16[256,256]{1,0:T(8,128)(2,1)} %copy-done.5, bf16[256,256]{1,0:T(8,128)(2,1)} %copy-done.6, bf16[256,256]{1,0:T(8,128)(2,1)} %copy-done.7, bf16[4,256,5120]{2,1,0:T(8,128)(2,1)} %refs_4_.5), custom_call_target="tpu_custom_call" | custom-call | flops 671088640 | bytes 2621440 | tf_op jit(solution)/shard_map/pallas_call | solution.py:143
  169.3 3.2 %collective-permute-start.30 = (bf16[128,1280]{1,0:T(8,128)(2,1)S(1)}, bf16[128,1280]{1,0:T(8,128)(2,1)S(1)}, u32[]{:S(2)}, u32[]{:S(2)}) collective-permute-start(bf16[128,1280]{1,0:T(8,128)(2,1)S(1)} %get-tuple-element.28), channel_id=1, source_target_pairs={{0,3},{1,0},{2,1},{3,2},{4,7},{5,4},{6,5},{7,6},{8,11},{9,8},{10,9... | collective-permute-start | bytes 983048 | tf_op jit(solution)/shard_map/ppermute | solution.py:329
  172.5 5.3 %shard_map.81 = f32[512,1280]{1,0:T(8,128)} custom-call(s32[9]{0:T(128)} %copy-done.3, bf16[256,256]{1,0:T(8,128)(2,1)} %bitcast.98, bf16[256,256]{1,0:T(8,128)(2,1)} %copy-done.5, bf16[256,256]{1,0:T(8,128)(2,1)} %copy-done.6, bf16[256,256]{1,0:T(8,128)(2,1)} %copy-done.7, bf16[4,256,5120]{2,1,0:T(8,128)(2,1)} %refs_4_.5), custom_call_target="tpu_custom_call" | custom-call | flops 1342177280 | bytes 5242880 | tf_op jit(solution)/shard_map/pallas_call | solution.py:143
  180.7 3.3 %collective-permute-start.31 = (bf16[256,1280]{1,0:T(8,128)(2,1)S(1)}, bf16[256,1280]{1,0:T(8,128)(2,1)S(1)}, u32[]{:S(2)}, u32[]{:S(2)}) collective-permute-start(bf16[256,1280]{1,0:T(8,128)(2,1)S(1)} %pad_maximum_fusion.4), channel_id=1, source_target_pairs={{0,3},{1,0},{2,1},{3,2},{4,7},{5,4},{6,5},{7,6},{8,11},{9,8},{10,9... | collective-permute-start | bytes 1966088 | tf_op jit(solution)/shard_map/ppermute | solution.py:335
  183.9 4.6 %shard_map.80 = f32[256,1280]{1,0:T(8,128)} custom-call(s32[9]{0:T(128)} %copy-done.3, bf16[256,256]{1,0:T(8,128)(2,1)} %bitcast.99, bf16[256,256]{1,0:T(8,128)(2,1)} %copy-done.5, bf16[256,256]{1,0:T(8,128)(2,1)} %copy-done.6, bf16[256,256]{1,0:T(8,128)(2,1)} %copy-done.7, bf16[4,256,5120]{2,1,0:T(8,128)(2,1)} %refs_4_.5), custom_call_target="tpu_custom_call" | custom-call | flops 671088640 | bytes 2621440 | tf_op jit(solution)/shard_map/pallas_call | solution.py:143
  188.6 7.7 %collective-permute-done.29 = bf16[256,1280]{1,0:T(8,128)(2,1)S(1)} collective-permute-done((bf16[256,1280]{1,0:T(8,128)(2,1)S(1)}, bf16[256,1280]{1,0:T(8,128)(2,1)S(1)}, u32[]{:S(2)}, u32[]{:S(2)}) %collective-permute-start.29) | collective-permute-done | bytes 655392 | tf_op jit(solution)/shard_map/ppermute | solution.py:334
  (135 shorter events, 50.7 us)
Async XLA Ops:
  1.1 11.9 %collective-permute-start.5 = (bf16[128,1280]{1,0:T(8,128)(2,1)S(1)}, bf16[128,1280]{1,0:T(8,128)(2,1)S(1)}, u32[]{:S(2)}, u32[]{:S(2)}) collective-permute-start(bf16[128,1280]{1,0:T(8,128)(2,1)S(1)} %get-tuple-element.29), channel_id=1, source_target_pairs={{0,32},{32,64},{64,96},{96,0},{1,33},{33,65},{65,97},{97,1},{2,34}... | collective-permute-start | bytes 983048 | tf_op jit(solution)/shard_map/ppermute | solution.py:235
  3.2 16.2 %collective-permute-start.6 = (bf16[128,1280]{1,0:T(8,128)(2,1)S(1)}, bf16[128,1280]{1,0:T(8,128)(2,1)S(1)}, u32[]{:S(2)}, u32[]{:S(2)}) collective-permute-start(bf16[128,1280]{1,0:T(8,128)(2,1)S(1)} %get-tuple-element.29), channel_id=1, source_target_pairs={{0,96},{32,0},{64,32},{96,64},{1,97},{33,1},{65,33},{97,65},{2,98}... | collective-permute-start | bytes 983048 | tf_op jit(solution)/shard_map/ppermute | solution.py:235
  5.4 15.8 %collective-permute-start.7 = (bf16[128,1280]{1,0:T(8,128)(2,1)S(1)}, bf16[128,1280]{1,0:T(8,128)(2,1)S(1)}, u32[]{:S(2)}, u32[]{:S(2)}) collective-permute-start(bf16[128,1280]{1,0:T(8,128)(2,1)S(1)} %get-tuple-element.29), channel_id=1, source_target_pairs={{0,64},{32,96},{64,0},{96,32},{1,65},{33,97},{65,1},{97,33},{2,66}... | collective-permute-start | bytes 983048 | tf_op jit(solution)/shard_map/ppermute | solution.py:235
  7.2 17.5 %collective-permute-start = (bf16[128,1280]{1,0:T(8,128)(2,1)S(1)}, bf16[128,1280]{1,0:T(8,128)(2,1)S(1)}, u32[]{:S(2)}, u32[]{:S(2)}) collective-permute-start(bf16[128,1280]{1,0:T(8,128)(2,1)S(1)} %get-tuple-element.30), channel_id=1, source_target_pairs={{0,1},{1,2},{2,3},{3,0},{4,5},{5,6},{6,7},{7,4},{8,9},{9,10},{10,1... | collective-permute-start | bytes 983048 | tf_op jit(solution)/shard_map/ppermute | solution.py:235
  8.7 16.0 %collective-permute-start.1 = (bf16[128,1280]{1,0:T(8,128)(2,1)S(1)}, bf16[128,1280]{1,0:T(8,128)(2,1)S(1)}, u32[]{:S(2)}, u32[]{:S(2)}) collective-permute-start(bf16[128,1280]{1,0:T(8,128)(2,1)S(1)} %get-tuple-element.30), channel_id=1, source_target_pairs={{0,3},{1,0},{2,1},{3,2},{4,7},{5,4},{6,5},{7,6},{8,11},{9,8},{10,9... | collective-permute-start | bytes 983048 | tf_op jit(solution)/shard_map/ppermute | solution.py:235
  13.0 12.1 %collective-permute-start.2 = (bf16[128,1280]{1,0:T(8,128)(2,1)S(1)}, bf16[128,1280]{1,0:T(8,128)(2,1)S(1)}, u32[]{:S(2)}, u32[]{:S(2)}) collective-permute-start(bf16[128,1280]{1,0:T(8,128)(2,1)S(1)} %get-tuple-element.30), channel_id=1, source_target_pairs={{0,2},{1,3},{2,0},{3,1},{4,6},{5,7},{6,4},{7,5},{8,10},{9,11},{10,... | collective-permute-start | bytes 983048 | tf_op jit(solution)/shard_map/ppermute | solution.py:235
  21.4 31.8 %collective-permute-start.8 = (bf16[512,1280]{1,0:T(8,128)(2,1)S(1)}, bf16[512,1280]{1,0:T(8,128)(2,1)}, u32[]{:S(2)}, u32[]{:S(2)}) collective-permute-start(bf16[512,1280]{1,0:T(8,128)(2,1)S(1)} %pad_maximum_fusion.1.refs_1_), channel_id=1, source_target_pairs={{0,1},{1,2},{2,3},{3,0},{4,5},{5,6},{6,7},{7,4},{8,9},{9,10},{10,1... | collective-permute-start | bytes 3932168 | tf_op jit(solution)/shard_map/ppermute | solution.py:276
  22.9 31.5 %collective-permute-start.9 = (bf16[512,1280]{1,0:T(8,128)(2,1)S(1)}, bf16[512,1280]{1,0:T(8,128)(2,1)}, u32[]{:S(2)}, u32[]{:S(2)}) collective-permute-start(bf16[512,1280]{1,0:T(8,128)(2,1)S(1)} %pad_maximum_fusion.1.refs_1_), channel_id=1, source_target_pairs={{0,3},{1,0},{2,1},{3,2},{4,7},{5,4},{6,5},{7,6},{8,11},{9,8},{10,9... | collective-permute-start | bytes 3932168 | tf_op jit(solution)/shard_map/ppermute | solution.py:278
  25.2 33.6 %collective-permute-start.3 = (bf16[128,5120]{1,0:T(8,128)(2,1)S(1)}, bf16[128,5120]{1,0:T(8,128)(2,1)}, u32[]{:S(2)}, u32[]{:S(2)}) collective-permute-start(bf16[128,5120]{1,0:T(8,128)(2,1)S(1)} %pad_maximum_fusion.refs_0_), channel_id=1, source_target_pairs={{0,32},{32,64},{64,96},{96,0},{1,33},{33,65},{65,97},{97,1},{2,34}... | collective-permute-start | bytes 3932168 | tf_op jit(solution)/shard_map/ppermute | solution.py:275
  30.4 32.4 %collective-permute-start.4 = (bf16[128,5120]{1,0:T(8,128)(2,1)S(1)}, bf16[128,5120]{1,0:T(8,128)(2,1)}, u32[]{:S(2)}, u32[]{:S(2)}) collective-permute-start(bf16[128,5120]{1,0:T(8,128)(2,1)S(1)} %pad_maximum_fusion.refs_0_), channel_id=1, source_target_pairs={{0,96},{32,0},{64,32},{96,64},{1,97},{33,1},{65,33},{97,65},{2,98}... | collective-permute-start | bytes 3932168 | tf_op jit(solution)/shard_map/ppermute | solution.py:277
  54.3 24.3 %collective-permute-start.12 = (bf16[256,1280]{1,0:T(8,128)(2,1)S(1)}, bf16[256,1280]{1,0:T(8,128)(2,1)S(1)}, u32[]{:S(2)}, u32[]{:S(2)}) collective-permute-start(bf16[256,1280]{1,0:T(8,128)(2,1)S(1)} %slice.100), channel_id=1, source_target_pairs={{0,1},{1,2},{2,3},{3,0},{4,5},{5,6},{6,7},{7,4},{8,9},{9,10},{10,1... | collective-permute-start | bytes 1966088 | tf_op jit(solution)/shard_map/ppermute | solution.py:282
  55.6 23.1 %collective-permute-start.13 = (bf16[256,1280]{1,0:T(8,128)(2,1)S(1)}, bf16[256,1280]{1,0:T(8,128)(2,1)S(1)}, u32[]{:S(2)}, u32[]{:S(2)}) collective-permute-start(bf16[256,1280]{1,0:T(8,128)(2,1)S(1)} %slice.101), channel_id=1, source_target_pairs={{0,3},{1,0},{2,1},{3,2},{4,7},{5,4},{6,5},{7,6},{8,11},{9,8},{10,9... | collective-permute-start | bytes 1966088 | tf_op jit(solution)/shard_map/ppermute | solution.py:283
  60.0 18.7 %collective-permute-start.10 = (bf16[64,5120]{1,0:T(8,128)(2,1)S(1)}, bf16[64,5120]{1,0:T(8,128)(2,1)S(1)}, u32[]{:S(2)}, u32[]{:S(2)}) collective-permute-start(bf16[64,5120]{1,0:T(8,128)(2,1)S(1)} %slice.98), channel_id=1, source_target_pairs={{0,32},{32,64},{64,96},{96,0},{1,33},{33,65},{65,97},{97,1},{2,34}... | collective-permute-start | bytes 1966088 | tf_op jit(solution)/shard_map/ppermute | solution.py:280
  63.9 15.3 %collective-permute-start.11 = (bf16[64,5120]{1,0:T(8,128)(2,1)S(1)}, bf16[64,5120]{1,0:T(8,128)(2,1)S(1)}, u32[]{:S(2)}, u32[]{:S(2)}) collective-permute-start(bf16[64,5120]{1,0:T(8,128)(2,1)S(1)} %slice.99), channel_id=1, source_target_pairs={{0,96},{32,0},{64,32},{96,64},{1,97},{33,1},{65,33},{97,65},{2,98}... | collective-permute-start | bytes 1966088 | tf_op jit(solution)/shard_map/ppermute | solution.py:281
  88.5 16.4 %collective-permute-start.15 = (bf16[640,384]{1,0:T(8,128)(2,1)}, bf16[640,384]{1,0:T(8,128)(2,1)S(1)}, u32[]{:S(2)}, u32[]{:S(2)}) collective-permute-start(bf16[640,384]{1,0:T(8,128)(2,1)} %get-tuple-element.20), channel_id=1, source_target_pairs={{0,4},{4,0},{8,12},{12,8},{16,20},{20,16},{24,28},{28,24},{1,5},{5... | collective-permute-start | bytes 1474568 | tf_op jit(solution)/shard_map/ppermute | solution.py:286
  88.8 12.7 %collective-permute-start.16 = (bf16[768,256]{1,0:T(8,128)(2,1)S(1)}, bf16[768,256]{1,0:T(8,128)(2,1)S(1)}, u32[]{:S(2)}, u32[]{:S(2)}) collective-permute-start(bf16[768,256]{1,0:T(8,128)(2,1)S(1)} %pad_maximum_fusion.6.refs_0_), channel_id=1, source_target_pairs={{0,8},{4,12},{8,16},{12,20},{16,24},{20,28},{24,0},{28,4},{1,9},{5... | collective-permute-start | bytes 1179656 | tf_op jit(solution)/shard_map/ppermute | solution.py:290
  101.5 13.5 %collective-permute-start.18 = (bf16[384,256]{1,0:T(8,128)(2,1)S(1)}, bf16[384,256]{1,0:T(8,128)(2,1)S(1)}, u32[]{:S(2)}, u32[]{:S(2)}) collective-permute-start(bf16[384,256]{1,0:T(8,128)(2,1)S(1)} %slice.105), channel_id=1, source_target_pairs={{0,8},{4,12},{8,16},{12,20},{16,24},{20,28},{24,0},{28,4},{1,9},{5... | collective-permute-start | bytes 589832 | tf_op jit(solution)/shard_map/ppermute | solution.py:294
  101.9 13.1 %collective-permute-start.19 = (bf16[384,256]{1,0:T(8,128)(2,1)S(1)}, bf16[384,256]{1,0:T(8,128)(2,1)S(1)}, u32[]{:S(2)}, u32[]{:S(2)}) collective-permute-start(bf16[384,256]{1,0:T(8,128)(2,1)S(1)} %slice.106), channel_id=1, source_target_pairs={{0,24},{4,28},{8,0},{12,4},{16,8},{20,12},{24,16},{28,20},{1,25},{... | collective-permute-start | bytes 589832 | tf_op jit(solution)/shard_map/ppermute | solution.py:294
  105.0 18.3 %collective-permute-start.20 = (bf16[1280,256]{1,0:T(8,128)(2,1)S(1)}, bf16[1280,256]{1,0:T(8,128)(2,1)S(1)}, u32[]{:S(2)}, u32[]{:S(2)}) collective-permute-start(bf16[1280,256]{1,0:T(8,128)(2,1)S(1)} %pad_maximum_fusion.2.refs_1_), channel_id=1, source_target_pairs={{0,8},{4,12},{8,16},{12,20},{16,24},{20,28},{24,0},{28,4},{1,9},{5... | collective-permute-start | bytes 1966088 | tf_op jit(solution)/shard_map/ppermute | solution.py:290
  105.1 18.3 %collective-permute-start.21 = (bf16[1280,256]{1,0:T(8,128)(2,1)S(1)}, bf16[1280,256]{1,0:T(8,128)(2,1)S(1)}, u32[]{:S(2)}, u32[]{:S(2)}) collective-permute-start(bf16[1280,256]{1,0:T(8,128)(2,1)S(1)} %pad_maximum_fusion.2.refs_1_), channel_id=1, source_target_pairs={{0,24},{4,28},{8,0},{12,4},{16,8},{20,12},{24,16},{28,20},{1,25},{... | collective-permute-start | bytes 1966088 | tf_op jit(solution)/shard_map/ppermute | solution.py:290
  123.3 17.3 %collective-permute-start.22 = (bf16[640,256]{1,0:T(8,128)(2,1)S(1)}, bf16[640,256]{1,0:T(8,128)(2,1)S(1)}, u32[]{:S(2)}, u32[]{:S(2)}) collective-permute-start(bf16[640,256]{1,0:T(8,128)(2,1)S(1)} %slice.216), channel_id=1, source_target_pairs={{0,8},{4,12},{8,16},{12,20},{16,24},{20,28},{24,0},{28,4},{1,9},{5... | collective-permute-start | bytes 983048 | tf_op jit(solution)/shard_map/ppermute | solution.py:294
  123.4 17.2 %collective-permute-start.23 = (bf16[640,256]{1,0:T(8,128)(2,1)S(1)}, bf16[640,256]{1,0:T(8,128)(2,1)S(1)}, u32[]{:S(2)}, u32[]{:S(2)}) collective-permute-start(bf16[640,256]{1,0:T(8,128)(2,1)S(1)} %slice.217), channel_id=1, source_target_pairs={{0,24},{4,28},{8,0},{12,4},{16,8},{20,12},{24,16},{28,20},{1,25},{... | collective-permute-start | bytes 983048 | tf_op jit(solution)/shard_map/ppermute | solution.py:294
  180.5 15.7 %collective-permute-start.29 = (bf16[256,1280]{1,0:T(8,128)(2,1)S(1)}, bf16[256,1280]{1,0:T(8,128)(2,1)S(1)}, u32[]{:S(2)}, u32[]{:S(2)}) collective-permute-start(bf16[256,1280]{1,0:T(8,128)(2,1)S(1)} %pad_maximum_fusion.3), channel_id=1, source_target_pairs={{0,1},{1,2},{2,3},{3,0},{4,5},{5,6},{6,7},{7,4},{8,9},{9,10},{10,1... | collective-permute-start | bytes 1966088 | tf_op jit(solution)/shard_map/ppermute | solution.py:334
  180.7 15.6 %collective-permute-start.31 = (bf16[256,1280]{1,0:T(8,128)(2,1)S(1)}, bf16[256,1280]{1,0:T(8,128)(2,1)S(1)}, u32[]{:S(2)}, u32[]{:S(2)}) collective-permute-start(bf16[256,1280]{1,0:T(8,128)(2,1)S(1)} %pad_maximum_fusion.4), channel_id=1, source_target_pairs={{0,3},{1,0},{2,1},{3,2},{4,7},{5,4},{6,5},{7,6},{8,11},{9,8},{10,9... | collective-permute-start | bytes 1966088 | tf_op jit(solution)/shard_map/ppermute | solution.py:335
  (29 other events, 252.5 us)
